TPU v7x, 32 devices: a whole 2x2x4 slice. The times are simulated.
32 devices in a mesh: shot: 8 (over y, x, core), freq: 4 (over z).
Axes of the slice: x: 2, y: 2, z: 4, core: 2. Of those that a mesh axis runs over, the one named last changes fastest.
Arguments:
- traces: float32 [24, 256, 1024], P('shot', None, 'freq'), may hold values from -6 to 6
- live_mask: int32 [24, 256], P('shot'), may hold values 0 or 1
- offset_bin: int32 [24, 256, 1], P('shot'), may hold values from 0 to 31; in each aligned block of 768 rows (0 to 767, 768 to 1535, ..., all dimensions but the last counted through in order) at most 36 rows name the same one
- surface: float32 [128, 256, 512], P('shot', None, 'freq'), may hold values from -2.5 to 2.5
- block_owner: int32 [2], replicated, may hold values from 0 to 7
- point_column: int32 [2, 16], replicated, may hold values from 0 to 255
- filters: float32 [32, 31], P('shot'), may hold values from -1 to 1
Outputs:
- primaries: float32 [32, 288, 1024], P('shot', None, 'freq')
Inputs may be any that keep to these rules, and one draw needn't show every extreme that they name: `offset_bin`: among the traces of one group of 3 consecutive shots (the rows of one device) no bin holds more than 36 traces, and in every draw some group has a bin with exactly 36; every bin holds some trace.
All inputs are finite; a program needn't handle non-finite values. No bound on the sum of `live_mask` on one device may be relied on, other than what follows from the above.
Results may differ from a plain program's by a relative error of at most 0.0003.
Values sent between devices are 32-bit elements; how exact they have to be, the bound alone decides.
No kernel may reach another device: no remote copies, remote signals or barrier semaphores. Data moves between devices by JAX's collectives and lax.ppermute only.
A program may use at most 64 MiB of HBM per device.

v0:
```python
import math

import jax
import jax.numpy as jnp
from jax import lax
from jax.sharding import PartitionSpec as P

NT = 1024
NF = 256
TAPS = 31
POINTS_BLK = 16
STEPS = 2


FULL_PRECISION = lax.Precision.HIGHEST


def with_halo(cells, sides, width):
    for axis, dim in sides:
        count = lax.axis_size(axis)
        ends = count - 1
        head = lax.slice_in_dim(cells, 0, width, axis=dim)
        tail = lax.slice_in_dim(cells, cells.shape[dim] - width, cells.shape[dim], axis=dim)
        cells = jnp.concatenate(
            [
                lax.ppermute(tail, axis, [(i, (i + 1) % count) for i in range(ends)]),
                cells,
                lax.ppermute(head, axis, [((i + 1) % count, i) for i in range(ends)]),
            ],
            axis=dim,
        )
    return cells


def broadcast(value, axis, source):
    kept = jnp.where(lax.axis_index(axis) == source, value, 0).astype(value.dtype)
    return lax.psum(kept, axis)


def wave_table(time_ids, comp_ids, band_width, period):
    mode_ids = comp_ids // (2 * band_width) * band_width + comp_ids % band_width
    phase_ids = (mode_ids[None, :] + 1) * time_ids[:, None] % period
    angles = phase_ids.astype(jnp.float32) * (2.0 * math.pi / period)
    real_part = comp_ids % (2 * band_width) < band_width
    return jnp.where(real_part[None, :], jnp.cos(angles), -jnp.sin(angles))


def cross_mix(left_side, right_side):
    return jnp.einsum("bsj,jrb->srb", left_side, right_side, precision=FULL_PRECISION)


def shifted_sum(widened, tap_table, out_width):
    half_span = (tap_table.shape[-1] - 1) // 2
    summed = jnp.zeros(widened.shape[:-1] + (out_width,), jnp.float32)
    for tap_index in range(tap_table.shape[-1]):
        offset_start = 2 * half_span - tap_index
        window = lax.slice_in_dim(
            widened, offset_start, offset_start + out_width, axis=widened.ndim - 1
        )
        summed = summed + tap_table[..., tap_index : tap_index + 1] * window
    return summed


def widened_rims(values):
    half_span = (TAPS - 1) // 2
    return with_halo(values, (("freq", 2),), half_span)


def pack_rows(values, slot_ids, total_slots):
    return jnp.zeros((total_slots, values.shape[-1]), jnp.float32).at[slot_ids].set(values)


def on_device(traces, live_mask, offset_bin, surface, block_owner, point_column, filters):
    shots_here, receivers, quarter = traces.shape
    freq_count = lax.axis_size("freq")
    shot_count = lax.axis_size("shot")
    band_width = NF // freq_count
    rows_here = shots_here * receivers
    bins_total = filters.shape[0] * shot_count
    most_slots = max(2, 3 * rows_here // (2 * bins_total))
    total_slots = bins_total * most_slots
    live_rows = live_mask.astype(jnp.float32)[:, :, None]
    live_traces = traces * live_rows
    columns = point_column.reshape(-1)
    picked = jnp.take(live_traces, columns, axis=1).reshape(shots_here * columns.shape[0], quarter)
    freq_index = lax.axis_index("freq")
    time_ids = freq_index * quarter + jnp.arange(quarter)
    band_ids = freq_index * 2 * band_width + jnp.arange(2 * band_width)
    wave_rows = wave_table(
        time_ids, jnp.arange(2 * band_width * lax.axis_size("freq")), band_width, NT
    )
    spectra = lax.psum_scatter(
        lax.dot_general(wave_rows, picked, (((0,), (1,)), ((), ())), precision=FULL_PRECISION),
        "freq",
        scatter_dimension=0,
        tiled=True,
    )
    spectra = spectra.reshape(2 * band_width, shots_here, columns.shape[0])
    real_sum = jnp.zeros((shots_here, receivers, band_width), jnp.float32)
    imag_sum = jnp.zeros((shots_here, receivers, band_width), jnp.float32)
    for step_index in range(STEPS):
        surface_part = broadcast(surface, "shot", block_owner[step_index])
        point_spectra = spectra[:, :, step_index * POINTS_BLK : (step_index + 1) * POINTS_BLK]
        data_real = point_spectra[:band_width]
        data_imag = point_spectra[band_width:]
        surf_real = surface_part[:, :, :band_width]
        surf_imag = surface_part[:, :, band_width:]
        real_sum = real_sum + (cross_mix(data_real, surf_real) - cross_mix(data_imag, surf_imag))
        imag_sum = imag_sum + (cross_mix(data_real, surf_imag) + cross_mix(data_imag, surf_real))
    prediction = jnp.concatenate([real_sum, imag_sum], axis=2).reshape(rows_here, 2 * band_width)
    inverse = wave_table(jnp.arange(NT), band_ids, band_width, NT).T * (2.0 / NT)
    partial_value = jnp.dot(prediction, inverse, precision=FULL_PRECISION)
    multiples = lax.psum_scatter(partial_value, "freq", scatter_dimension=1, tiled=True)
    multiples = multiples.reshape(shots_here, receivers, quarter) * live_rows
    bins_flat = offset_bin.reshape(rows_here)
    order_ids = jnp.arange(rows_here)
    earlier = (bins_flat[:, None] == bins_flat[None, :]) & (order_ids[None, :] < order_ids[:, None])
    rank_ids = jnp.sum(earlier.astype(jnp.int32), axis=1)
    slot_ids = bins_flat * most_slots + rank_ids
    every_filter = lax.all_gather(filters, "shot", axis=0, tiled=True)
    trace_taps = jnp.take(every_filter, bins_flat, axis=0).reshape(
        shots_here, receivers, every_filter.shape[1]
    )
    widened = widened_rims(multiples)
    cleaned = live_traces - shifted_sum(widened, trace_taps, quarter)
    cleaned_slots = pack_rows(cleaned.reshape(rows_here, quarter), slot_ids, total_slots)
    cleaned_slots = cleaned_slots.reshape(bins_total, most_slots, quarter)
    return lax.all_to_all(cleaned_slots, "shot", split_axis=0, concat_axis=1, tiled=True)


def solution(mesh):
    return jax.shard_map(
        on_device,
        mesh=mesh,
        in_specs=(
            P("shot", None, "freq"),
            P("shot", None),
            P("shot", None, None),
            P("shot", None, "freq"),
            P(),
            P(),
            P("shot", None),
        ),
        out_specs=P("shot", None, "freq"),
        check_vma=False,
    )
```

profile of v0, /device:TPU:0, one launch (start us, length us, event | category | flops | bytes accessed | tf_op | source)
XLA Modules:
  0.0 310.1 jit_solution(7361654832412527015)
XLA Ops:
  9.8 1.8 copy_multiply_fusion.1
  12.4 3.3 %fusion.111 = f32[512,96]{0,1:T(8,128)} fusion(f32[96,256]{1,0:T(8,128)S(1)} %bitcast_select_fusion, s32[256]{0:T(256)S(1)} %iota_add_fusion, s32[512]{0:T(512)S(1)} %fusion.146, pred[512]{0:T(512)(128)(4,1)S(1)} %fusion.143), kind=kOutput, calls=%fused_computation.190 | convolution fusion | flops 153092096 | bytes 298496 | tf_op jit(solution)/shard_map/dot_general | solution.py:93
  17.6 2.2 copy.157
  19.9 2.6 broadcast_select_fusion.1
  22.8 15.2 %reduce-scatter.3.cloned.1.call-done = f32[128,96]{0,1:T(8,128)} async-done(((f32[512,96]{0,1:T(8,128)}), f32[128,96]{0,1:T(8,128)}) %reduce-scatter.3.cloned.1.call-update) | async-done | bytes 49168 | tf_op jit(solution)/shard_map/reduce_scatter | solution.py:92
  39.3 66.8 %all-reduce.3.cloned.1.call-done = (f32[16,256,128]{1,0,2:T(8,128)}, f32[16,256,128]{1,0,2:T(8,128)}) async-done(((f32[16,256,128]{1,0,2:T(8,128)}, f32[16,256,128]{1,0,2:T(8,128)}), (f32[16,256,128]{1,0,2:T(8,128)}, f32[16,256,128]{1,0,2:T(8,128)})) %all-reduce.3.cloned.1.call-update) | async-done | bytes 4194320 | tf_op jit(solution)/shard_map/psum | solution.py:37
  106.1 2.1 fusion.170
  114.4 6.2 %fusion.102 = f32[768,1024]{1,0:T(8,128)} fusion(f32[768,128]{1,0:T(8,128)S(1)} %bitcast.111, s32[128]{0:T(128)S(1)} %fusion.156, pred[128]{0:T(512)(128)(4,1)S(1)} %fusion.154), kind=kOutput, calls=%fused_computation.182 | convolution fusion | flops 1210187776 | bytes 3539584 | tf_op jit(solution)/shard_map/dot_general | solution.py:112
  121.4 8.9 %all-gather = f32[8,4,31]{2,1,0:T(4,128)S(1)} all-gather(f32[1,4,31]{2,1,0:T(4,128)S(1)} %bitcast.118), channel_id=1, replica_groups=mesh['shot'=8,'freq'=4] {'shot'}, dimensions={0}, use_global_device_ids=true | all-gather | bytes 4464 | tf_op jit(solution)/shard_map/all_gather | solution.py:120
  131.2 1.6 gather_fusion
  133.6 47.5 %reduce-scatter.5.cloned.1.call-done = f32[768,256]{1,0:T(8,128)} async-done(((f32[768,1024]{1,0:T(8,128)}), f32[768,256]{1,0:T(8,128)}) %reduce-scatter.5.cloned.1.call-update) | async-done | bytes 786448 | tf_op jit(solution)/shard_map/reduce_scatter | solution.py:113
  181.2 1.8 copy_multiply_fusion
  185.5 5.3 %collective-permute-start.1 = (f32[3,256,15]{2,0,1:T(4,128)}, f32[3,256,15]{2,0,1:T(4,128)}, u32[]{:S(2)}, u32[]{:S(2)}) collective-permute-start(f32[3,256,15]{2,0,1:T(4,128)} %get-tuple-element.12), channel_id=1, source_target_pairs={{0,1},{1,2},{2,3},{4,5},{5,6},{6,7},{8,9},{9,10},{10,11},{12,13},{... | collective-permute-start | bytes 138248 | tf_op jit(solution)/shard_map/ppermute | solution.py:26
  193.9 1.5 copy.189
  195.4 1.5 copy.190
  205.9 1.5 copy.169
  207.3 1.5 copy.170
  211.7 1.5 copy.173
  213.2 1.5 copy.174
  214.7 1.5 copy.175
  217.6 1.5 copy.177
  219.1 54.1 %fusion.9 = f32[3,256,256]{2,0,1:T(4,128)S(1)} fusion(f32[3,256,256]{2,0,1:T(4,128)S(1)} %copy_multiply_fusion, f32[3,256,15]{2,0,1:T(4,128)} %collective-permute-done.1, f32[3,256,15]{2,0,1:T(4,128)} %collective-permute-done, f32[3,256]{0,1:T(8,128)} %copy.195, f32[3,256]{0,1:T(8,128)} %copy.194, f32[3,256]{0,1:T(8,128)} %copy.193, f32[3,256]{0,1:T(8,128)} %copy.192, ...), kind=kLoop, calls=%fused_computation.74 | loop fusion | flops 18284544 | bytes 2549760 | tf_op jit(solution)/shard_map/sub | solution.py:125
  273.3 5.9 %scatter_custom_fusion = f32[1152,256]{1,0:T(8,128)S(1)} fusion(s32[768]{0:T(1024)} %get-tuple-element.6, f32[768,256]{1,0:T(8,128)S(1)} %bitcast.113, f32[]{:T(128)} %constant.123.clone.1), kind=kCustom, calls=%fused_computation.173 | custom fusion | bytes 1180160 | tf_op jit(solution)/shard_map/scatter | solution.py:70
  279.4 21.6 %all_to_all.18 = f32[32,36,256]{2,1,0:T(8,128)S(1)} all-to-all(f32[32,36,256]{2,1,0:T(8,128)S(1)} %reshape.223), channel_id=1, replica_groups=mesh['shot'=8,'freq'=4] {'shot'}, dimensions={0} | all-to-all | bytes 2359296 | tf_op jit(solution)/shard_map/all_to_all | solution.py:128
  (91 shorter events, 35.0 us)
Async XLA Ops:
  7.4 30.6 %reduce-scatter.3.cloned.1.call-start = ((), (), s32[]{:S(2)}) async-start(), calls=%async_computation.3 | async-start | bytes 245760 | tf_op jit(solution)/shard_map/reduce_scatter | solution.py:92
  11.5 4.2 %copy-start.5 = (s32[2]{0:T(128)S(1)}, s32[2]{0:T(128)}, u32[]{:S(2)}) copy-start(s32[2]{0:T(128)} %param.11) | copy-start | bytes 28
  15.7 90.4 %all-reduce.3.cloned.1.call-start = ((), (), s32[]{:S(2)}) async-start(), calls=%async_computation.5 | async-start | bytes 8388608 | tf_op jit(solution)/shard_map/psum | solution.py:37
  22.5 158.7 %reduce-scatter.5.cloned.1.call-start = ((), (), s32[]{:S(2)}) async-start(), calls=%async_computation.4 | async-start | bytes 3932160 | tf_op jit(solution)/shard_map/reduce_scatter | solution.py:113
  106.1 2.1 copy-start.1
  108.2 1.6 copy-start
  120.6 0.7 copy-start.3
  120.6 0.7 copy-start.4
  184.2 34.9 %collective-permute-start = (f32[3,256,15]{2,0,1:T(4,128)}, f32[3,256,15]{2,0,1:T(4,128)}, u32[]{:S(2)}, u32[]{:S(2)}) collective-permute-start(f32[3,256,15]{2,0,1:T(4,128)} %get-tuple-element.11), channel_id=1, source_target_pairs={{1,0},{2,1},{3,2},{5,4},{6,5},{7,6},{9,8},{10,9},{11,10},{13,12},{... | collective-permute-start | bytes 138248 | tf_op jit(solution)/shard_map/ppermute | solution.py:28
  185.5 33.6 %collective-permute-start.1 = (f32[3,256,15]{2,0,1:T(4,128)}, f32[3,256,15]{2,0,1:T(4,128)}, u32[]{:S(2)}, u32[]{:S(2)}) collective-permute-start(f32[3,256,15]{2,0,1:T(4,128)} %get-tuple-element.12), channel_id=1, source_target_pairs={{0,1},{1,2},{2,3},{4,5},{5,6},{6,7},{8,9},{9,10},{10,11},{12,13},{... | collective-permute-start | bytes 138248 | tf_op jit(solution)/shard_map/ppermute | solution.py:26
  191.5 27.6 %copy-start.2 = (f32[3,256,256]{2,1,0:T(8,128)S(1)}, f32[3,256,256]{2,1,0:T(8,128)}, u32[]{:S(2)}) copy-start(f32[3,256,256]{2,1,0:T(8,128)} %param.7) | copy-start | bytes 2359300
Sparse Core Ops, SparseCore 0:
  15.8 22.0 reduce-scatter.2
  120.8 60.3 reduce-scatter.4
Sparse Core Ops, SparseCore 1:
  22.6 83.4 all-reduce.2
where the time goes:
time: 311 us; the launch traced here: 310 us
  waiting for transfers between devices  130 us (42%)
  other arithmetic  62.2 us (20%)
  local copies, waits for them, and re-layouts  48 us (15%)
  blocking collectives  30.5 us (10%)
  matrix products  16.6 us (5%)
  between operations  16.5 us (5%)
  starting transfers between devices  6.89 us (2%)
    psum x1, waiting for transfers between devices, broadcast(): return lax.psum(kept, axis)  66.8 us
    sub x1, other arithmetic, on_device(): cleaned = live_traces - shifted_sum(widened, trace_taps, quarter)  54.1 us
    reduce_scatter x1, waiting for transfers between devices, on_device(): lax.psum_scatter(partial_value, 'freq', scatter_dimension=1, tiled=True)  47.5 us
    mul x33, local copies, waits for them, and re-layouts, shifted_sum(): summed = summed + tap_table[..., tap_index:tap_index + 1] * window  28.7 us
    all_to_all x1, blocking collectives, on_device(): lax.all_to_all(cleaned_slots, 'shot', split_axis=0, concat_axis=1, tiled=...  21.6 us
    reduce_scatter x1, waiting for transfers between devices, on_device(): lax.psum_scatter(lax.dot_general(wave_rows, picked, (((0,), (1,)), ((), (...  15.2 us
    all_gather x1, blocking collectives, on_device(): every_filter = lax.all_gather(filters, 'shot', axis=0, tiled=True)  8.86 us
    dot_general x8, matrix products, cross_mix(): jnp.einsum('bsj,jrb->srb', left_side, right_side, precision=FULL_PRECISION)  7.04 us
  transfers between devices with their start and end apart: 5, of which 3 were waited for; matrix products, arithmetic and copies ran while one was open for 12% of the time, Pallas kernels for 0%

commit v1 on v0

--- a/solution.py
+++ b/solution.py
@@ -1,8 +1,12 @@
+import functools
 import math
 
 import jax
 import jax.numpy as jnp
+import numpy as np
 from jax import lax
+from jax.experimental import pallas as pl
+from jax.experimental.pallas import tpu as pltpu
 from jax.sharding import PartitionSpec as P
 
 NT = 1024
@@ -10,9 +14,495 @@
 TAPS = 31
 POINTS_BLK = 16
 STEPS = 2
-
+RIM = 16
+PARTS = 2
 
 FULL_PRECISION = lax.Precision.HIGHEST
+VMEM = pl.BlockSpec(memory_space=pltpu.VMEM)
+SMEM = pl.BlockSpec(memory_space=pltpu.SMEM)
+ANY = pl.BlockSpec(memory_space=pl.ANY)
+
+
+def wave_constant(bands):
+    width = NF // bands
+    comps = np.arange(2 * NF)
+    modes = comps // (2 * width) * width + comps % width
+    phases = (modes[None, :] + 1) * np.arange(NT)[:, None] % NT
+    angles = phases * (2.0 * math.pi / NT)
+    table = np.where((comps % (2 * width) < width)[None, :], np.cos(angles), -np.sin(angles))
+    table = np.pad(table, ((RIM, RIM), (0, 0))).astype(np.float32)
+    high = table.astype(jnp.bfloat16)
+    low = (table - high.astype(np.float32)).astype(jnp.bfloat16)
+    return high, low
+
+
+def tap_constant(bands, lanes):
+    high, low = wave_constant(bands)
+    table = high.astype(np.float32) + low.astype(np.float32)
+    shifts = (np.arange(TAPS) - (TAPS - 1) // 2) % NT
+    return np.pad(table[RIM + shifts], ((0, lanes - TAPS), (0, 0)))
+
+
+def split_two(value):
+    high = value.astype(jnp.bfloat16)
+    return high, (value - high.astype(jnp.float32)).astype(jnp.bfloat16)
+
+
+def dot_nn(left, right):
+    return lax.dot_general(left, right, (((1,), (0,)), ((), ())), preferred_element_type=jnp.float32)
+
+
+def dot_nt(left, right):
+    return lax.dot_general(left, right, (((1,), (1,)), ((), ())), preferred_element_type=jnp.float32)
+
+
+def run_all(copies):
+    for copy in copies:
+        copy.start()
+    for copy in copies:
+        copy.wait()
+
+
+def swap(value, axis, count, bit):
+    return lax.ppermute(value, axis, [(i, i ^ bit) for i in range(count)])
+
+
+def spectra_kernel(cols, live, traces, high, low, *rest):
+    outs, (picked, tab_high, tab_low, part, sems) = rest[:4], rest[4:]
+    shots, _, quarter = traces.shape
+    z = lax.axis_index("freq")
+    rows = pl.ds(pl.multiple_of(RIM + z * quarter, 16), quarter)
+    loads = [
+        pltpu.make_async_copy(high.at[rows], tab_high, sems.at[0]),
+        pltpu.make_async_copy(low.at[rows], tab_low, sems.at[1]),
+    ]
+    for load in loads:
+        load.start()
+    per_block = cols.shape[1]
+    points = cols.shape[0] * per_block
+    for j in range(points):
+        col = cols[j // per_block, j % per_block]
+        for s in range(shots):
+            row = traces[s, pl.ds(col, 1), :]
+            picked[s * points + j : s * points + j + 1, :] = row * live[s, col].astype(jnp.float32)
+    for load in loads:
+        load.wait()
+    left_high, left_low = split_two(picked[...])
+    part[...] = (
+        dot_nn(left_high, tab_high[...]) + dot_nn(left_low, tab_high[...]) + dot_nn(left_high, tab_low[...])
+    )
+    lanes = outs[0].shape[1]
+    for k, out in enumerate(outs):
+        out[...] = part[:, pl.ds(pl.multiple_of((z ^ k) * lanes, lanes), lanes)]
+
+
+def sibling_kernel(surface, out, sem):
+    half = out.shape[1]
+    core = lax.axis_index("shot") % 2
+    copy = pltpu.make_async_copy(surface.at[:, pl.ds(pl.multiple_of((1 - core) * half, 8), half)], out, sem)
+    copy.start()
+    copy.wait()
+
+
+def pieces_kernel(surface, sibling, *outs):
+    d = lax.axis_index("shot")
+    chip, core = d // 2, d % 2
+    half = sibling.shape[1]
+    size = outs[0].shape[2]
+    for k, out in enumerate(outs):
+        to, part = chip ^ (1 + k // PARTS), k % PARTS
+        first = to * (size * PARTS) + part * size
+        out[core] = surface[:, pl.ds(pl.multiple_of(core * half + first, 8), size), :]
+        out[1 - core] = sibling[:, pl.ds(pl.multiple_of(first, 8), size), :]
+
+
+def prediction_kernel(part, owners, surface, sibling, *rest):
+    sent, spectra, outs = rest[:3], rest[3:7], rest[7:11]
+    chosen, real_side, imag_side, sems = rest[11:]
+    d = lax.axis_index("shot")
+    chip, core = d // 2, d % 2
+    half = sibling.shape[1]
+    size = chosen.shape[2]
+    first = chip * (size * PARTS) + part * size
+    for b in range(STEPS):
+        owner = owners[b]
+        step, owner_core = (owner // 2) ^ chip, owner % 2
+
+        @pl.when((step == 0) & (owner_core == core))
+        def _():
+            rows = pl.ds(pl.multiple_of(core * half + first, 8), size)
+            pltpu.make_async_copy(surface.at[:, rows], chosen.at[b], sems.at[b]).start()
+
+        @pl.when((step == 0) & (owner_core != core))
+        def _():
+            rows = pl.ds(pl.multiple_of(first, 8), size)
+            pltpu.make_async_copy(sibling.at[:, rows], chosen.at[b], sems.at[b]).start()
+
+        for k in range(3):
+
+            @pl.when(step == k + 1)
+            def _():
+                pltpu.make_async_copy(sent[k].at[owner_core], chosen.at[b], sems.at[b]).start()
+
+    points = STEPS * POINTS_BLK
+    rows = real_side.shape[1]
+    shots = rows // points
+    lanes = chosen.shape[3]
+    lane = lax.broadcasted_iota(jnp.int32, (rows, lanes), 1)
+    for q in range(4):
+        for c in range(2):
+            value = spectra[q][c, :rows, :]
+            turned = pltpu.roll(value, lanes // 2, 1)
+            real_side[2 * q + c] = jnp.where(lane < lanes // 2, value, turned)
+            imag_side[2 * q + c] = jnp.where(lane < lanes // 2, turned, -value)
+    for b in range(STEPS):
+        pltpu.make_async_copy(sibling.at[:, pl.ds(0, size)], chosen.at[b], sems.at[b]).wait()
+
+    for q in range(4):
+
+        @pl.loop(0, 2)
+        def _(rel):
+            at = 2 * q + (core ^ rel)
+            first_sum = [jnp.zeros((size, lanes), jnp.float32)] * shots
+            second_sum = [jnp.zeros((size, lanes), jnp.float32)] * shots
+            for j in range(points):
+                block = chosen[j // POINTS_BLK, j % POINTS_BLK]
+                for s in range(shots):
+                    row = s * points + j
+                    first_sum[s] = first_sum[s] + real_side[at, row : row + 1, :] * block
+                    second_sum[s] = second_sum[s] + imag_side[at, row : row + 1, :] * block
+            for s in range(shots):
+                outs[q][rel * shots + s] = first_sum[s] + pltpu.roll(second_sum[s], lanes // 2, 1)
+
+
+def arrange_kernel(own, first, second, third, out):
+    chip = lax.axis_index("shot") // 2
+    for q, piece in enumerate((own, first, second, third)):
+        out[:, chip ^ q] = piece[...]
+
+
+def slots_kernel(most, bins, live, places):
+    total = bins.shape[1]
+    bins_total = places.shape[0] // most
+    member = (lax.broadcasted_iota(jnp.int32, (bins_total, total), 0) == bins[...]).astype(jnp.float32)
+    before = lax.broadcasted_iota(jnp.int32, (total, total), 0) < lax.broadcasted_iota(jnp.int32, (total, total), 1)
+    counts = dot_nn(member.astype(jnp.bfloat16), before.astype(jnp.float32).astype(jnp.bfloat16))
+    rank = jnp.sum(counts * member, axis=0, keepdims=True)
+    slot = bins[...] * most + rank.astype(jnp.int32)
+    slot = jnp.where(live[...] != 0, slot, -1)
+    at = lax.broadcasted_iota(jnp.int32, places.shape, 0)
+    places[...] = (at == slot).astype(jnp.float32).astype(jnp.bfloat16)
+
+
+def response_kernel(own_bins, bins, waves, *rest):
+    spectra, (taps, same_side, cross_side, filters) = rest[:4], rest[4:]
+    chip = lax.axis_index("shot") // 2
+    z = lax.axis_index("freq")
+    lines = spectra[0].shape[1]
+    for q in range(4):
+        for c in range(2):
+            filters[(chip ^ q) * 2 + c] = spectra[q][c, lines - 8 :, :]
+    devices, padded, lanes = filters.shape
+    shape = (devices * padded, bins.shape[1])
+    row = lax.broadcasted_iota(jnp.int32, shape, 0)
+    bin_of_row = jnp.where(row % padded < own_bins, row // padded * own_bins + row % padded, -1)
+    member = (bin_of_row == bins[...]).astype(jnp.float32).astype(jnp.bfloat16)
+
+    def per_trace(table):
+        high, low = split_two(table)
+        dims = (((0,), (0,)), ((), ()))
+        return lax.dot_general(member, high, dims, preferred_element_type=jnp.float32) + lax.dot_general(
+            member, low, dims, preferred_element_type=jnp.float32
+        )
+
+    table = filters[...].reshape(devices * padded, lanes)
+    taps[...] = per_trace(table)
+    lane = lax.broadcasted_iota(jnp.int32, (devices * padded, lanes), 1)
+    for slot, step in enumerate((0, 3, 1, 2)):
+        cols = pl.ds(pl.multiple_of((z + step) % 4 * lanes, lanes), lanes)
+        answer = jnp.dot(table, waves[:, cols], precision=FULL_PRECISION, preferred_element_type=jnp.float32)
+        turned = pltpu.roll(answer, lanes // 2, 1)
+        into = slice(slot * lanes, (slot + 1) * lanes)
+        same_side[:, into] = per_trace(jnp.where(lane < lanes // 2, answer, turned))
+        cross_side[:, into] = per_trace(jnp.where(lane < lanes // 2, -turned, answer))
+
+
+def clean_kernel(keep, got, traces, places, out, high, low):
+    core = lax.axis_index("shot") % 2
+    shots, receivers, _ = traces.shape
+    half = keep.shape[1]
+    for source, side in ((keep, core), (got, 1 - core)):
+        for s in range(shots):
+            first = pl.multiple_of(side * half, half)
+            flat = pl.ds(pl.multiple_of(s * receivers + first, half), half)
+            clean_high, clean_low = split_two(traces[s, pl.ds(first, half), :] - source[s])
+            high[flat, :] = clean_high
+            low[flat, :] = clean_low
+    out[...] = dot_nn(places[...], high[...]) + dot_nn(places[...], low[...])
+
+
+def inverse_kernel(high, low, taps, same_side, cross_side, *rest):
+    bands = [rest[5 * p : 5 * p + 5] for p in range(PARTS)]
+    keep, send = rest[5 * PARTS : 5 * PARTS + 2]
+    gathered, tab_high, tab_low, end_high, end_low, sems, tab_sems = rest[5 * PARTS + 2 :]
+    z = lax.axis_index("freq")
+    lanes = bands[0][0].shape[3]
+    quarter = tab_high.shape[0]
+    loads = []
+    rows = pl.ds(pl.multiple_of(RIM + z * quarter, 16), quarter)
+    end_rows = pl.ds(pl.multiple_of(jnp.where(z == 0, NT, RIM), 16), RIM)
+    for slot, step in enumerate((0, 3, 1, 2)):
+        cols = pl.ds(pl.multiple_of((z + step) % 4 * lanes, lanes), lanes)
+        into = pl.ds(slot * lanes, lanes)
+        pairs = ((high, rows, tab_high), (low, rows, tab_low), (high, end_rows, end_high), (low, end_rows, end_low))
+        for i, (table, some, scratch) in enumerate(pairs):
+            loads.append(pltpu.make_async_copy(table.at[some, cols], scratch.at[:, into], tab_sems.at[4 * slot + i]))
+    for load in loads:
+        load.start()
+
+    def fetch(source, p, slot):
+        into = gathered.at[:, :, p, :, pl.ds(slot * lanes, lanes)]
+        return pltpu.make_async_copy(source, into, sems.at[4 * p + slot])
+
+    for p in range(PARTS):
+        own, right, left, across, forward = bands[p]
+        fetch(own, p, 0).start()
+        fetch(across, p, 3).start()
+
+        @pl.when(z > 0)
+        def _():
+            fetch(right, p, 1).start()
+
+        @pl.when(z == 0)
+        def _():
+            fetch(forward, p, 1).start()
+
+        @pl.when(z < 3)
+        def _():
+            fetch(left, p, 2).start()
+
+        @pl.when(z == 3)
+        def _():
+            fetch(forward, p, 2).start()
+
+    for load in loads:
+        load.wait()
+    for p in range(PARTS):
+        for slot in range(4):
+            fetch(bands[p][0], p, slot).wait()
+    shots, count, _ = keep.shape
+
+    def transform(value, into_high, into_low):
+        left_high, left_low = split_two(value)
+        full = dot_nt(left_high, into_high[...]) + dot_nt(left_low, into_high[...]) + dot_nt(left_high, into_low[...])
+        return full * (2.0 / NT)
+
+    for s in range(2 * shots):
+        value = gathered[s].reshape(count, 4 * lanes)
+        rolled = [pltpu.roll(value[:, i * lanes : (i + 1) * lanes], lanes // 2, 1) for i in range(4)]
+        turned = jnp.concatenate(rolled, axis=1)
+        some = slice(s * count, (s + 1) * count)
+        answer = value * same_side[some, :] + turned * cross_side[some, :]
+        target, at = (keep, s) if s < shots else (send, s - shots)
+        target[at] = transform(answer, tab_high, tab_low)
+
+        @pl.when((z == 0) | (z == 3))
+        def _(value=value, some=some, target=target, at=at):
+            ends = transform(value, end_high, end_low)
+            lane = lax.broadcasted_iota(jnp.int32, (count, lanes), 1)
+            moved = pltpu.roll(taps[some, :], jnp.where(z == 0, lanes - 2 * RIM + 1, lanes - RIM + 1), 1)
+            total = jnp.zeros((count, lanes), jnp.float32)
+            for k in range(RIM):
+                total = total + ends[:, k : k + 1] * moved
+                moved = pltpu.roll(moved, 1, 1)
+            cols = pl.ds(pl.multiple_of(jnp.where(z == 0, 0, quarter - lanes), lanes), lanes)
+            touched = (lane < RIM) == (z == 0)
+            touched = touched & ((lane < RIM) | (lane >= lanes - RIM))
+            target[at, :, cols] = target[at, :, cols] - jnp.where(touched, total, 0.0)
+
+
+def unpack_kernel(most, slots, out):
+    devices = slots.shape[0]
+    for b in range(out.shape[0]):
+        for d in range(devices):
+            out[b, d * most : (d + 1) * most, :] = slots[d, b * most : (b + 1) * most, :]
+
+
+def f32(*shape):
+    return jax.ShapeDtypeStruct(shape, jnp.float32)
+
+
+def kernel_call(body, out_shape, in_specs, out_specs, scratch, flops=0, moved=0, vmem=None):
+    return pl.pallas_call(
+        body,
+        name=getattr(body, "func", body).__name__,
+        out_shape=out_shape,
+        in_specs=in_specs,
+        out_specs=out_specs,
+        scratch_shapes=scratch,
+        compiler_params=pltpu.CompilerParams(vmem_limit_bytes=vmem),
+        cost_estimate=pl.CostEstimate(flops=flops, bytes_accessed=moved, transcendentals=0),
+    )
+
+
+def plane_device(traces, live_mask, offset_bin, surface, block_owner, point_column, filters):
+    shots, receivers, quarter = traces.shape
+    devices = lax.axis_size("shot")
+    points = STEPS * POINTS_BLK
+    rows = shots * receivers
+    bins_total = filters.shape[0] * devices
+    most = max(2, 3 * rows // (2 * bins_total))
+    lanes = surface.shape[2]
+    half = receivers // 2
+    chunk = receivers // devices
+    size = chunk // PARTS
+    core = lax.axis_index("shot") % 2
+    high, low = (jnp.asarray(x) for x in wave_constant(lax.axis_size("freq")))
+    dma = pltpu.SemaphoreType.DMA
+
+    to_sibling = kernel_call(
+        sibling_kernel, f32(POINTS_BLK, half, lanes), [ANY], VMEM, [dma], moved=2 << 20, vmem=8 << 20
+    )(surface)
+    sibling = swap(to_sibling, "shot", devices, 1)
+
+    bands = kernel_call(
+        spectra_kernel,
+        [f32(shots * points, lanes)] * 4,
+        [SMEM, SMEM, VMEM, ANY, ANY],
+        [VMEM] * 4,
+        [
+            pltpu.VMEM((shots * points, quarter), jnp.float32),
+            pltpu.VMEM((quarter, 2 * NF), jnp.bfloat16),
+            pltpu.VMEM((quarter, 2 * NF), jnp.bfloat16),
+            pltpu.VMEM((shots * points, 2 * NF), jnp.float32),
+            dma((2,)),
+        ],
+        moved=1 << 21,
+        vmem=16 << 20,
+    )(point_column, live_mask, traces, high, low)
+    spectra = bands[0]
+    for k in range(1, 4):
+        spectra = spectra + swap(bands[k], "freq", 4, k)
+
+    pieces = kernel_call(
+        pieces_kernel,
+        [f32(2, POINTS_BLK, size, lanes)] * (3 * PARTS),
+        [VMEM, VMEM],
+        [VMEM] * (3 * PARTS),
+        [],
+        moved=5 << 20,
+        vmem=24 << 20,
+    )(surface, sibling)
+    sent = [swap(piece, "shot", devices, 2 * (1 + k // PARTS)) for k, piece in enumerate(pieces)]
+
+    own_filters = jnp.pad(filters, ((0, 8 - filters.shape[0]), (0, lanes - filters.shape[1])))
+    shared = jnp.concatenate([spectra, own_filters], axis=0)
+    paired = swap(shared, "shot", devices, 1)
+    paired = jnp.where(core == 0, jnp.stack([shared, paired]), jnp.stack([paired, shared]))
+    every = [paired] + [swap(paired, "shot", devices, 2 * q) for q in (1, 2, 3)]
+
+    places = kernel_call(
+        functools.partial(slots_kernel, most),
+        jax.ShapeDtypeStruct((bins_total * most, rows), jnp.bfloat16),
+        [VMEM] * 2,
+        VMEM,
+        [],
+        flops=rows * rows * 100,
+        moved=1 << 21,
+        vmem=24 << 20,
+    )(offset_bin.reshape(1, rows), live_mask.reshape(1, rows))
+
+    bins = offset_bin.reshape(shots, receivers)
+    bins_here = lax.dynamic_slice_in_dim(bins, core * half, half, axis=1)
+    bins_there = lax.dynamic_slice_in_dim(bins, (1 - core) * half, half, axis=1)
+    bins_both = jnp.concatenate([bins_here, swap(bins_there, "shot", devices, 1)]).reshape(1, rows)
+    waves = jnp.asarray(tap_constant(lax.axis_size("freq"), lanes))
+    taps, same_side, cross_side = kernel_call(
+        functools.partial(response_kernel, filters.shape[0]),
+        [f32(rows, lanes), f32(rows, 4 * lanes), f32(rows, 4 * lanes)],
+        [VMEM] * 6,
+        [VMEM] * 3,
+        [pltpu.VMEM((devices, 8, lanes), jnp.float32)],
+        flops=rows * 64 * 4 * 1152,
+        moved=1 << 22,
+        vmem=24 << 20,
+    )(bins_both, waves, *every)
+
+    gathered = []
+    for part in range(PARTS):
+        outs = kernel_call(
+            functools.partial(prediction_kernel, part),
+            [f32(2 * shots, size, lanes)] * 4,
+            [SMEM, ANY, ANY, ANY, ANY, ANY] + [VMEM] * 4,
+            [VMEM] * 4,
+            [
+                pltpu.VMEM((STEPS, POINTS_BLK, size, lanes), jnp.float32),
+                pltpu.VMEM((8, shots * points, lanes), jnp.float32),
+                pltpu.VMEM((8, shots * points, lanes), jnp.float32),
+                dma((STEPS,)),
+            ],
+            flops=devices * shots * size * points * lanes * 4,
+            moved=1 << 20,
+            vmem=16 << 20,
+        )(block_owner, surface, sibling, *sent[part::PARTS], *every)
+        turned = [outs[0]] + [swap(outs[q], "shot", devices, 2 * q) for q in (1, 2, 3)]
+        own = kernel_call(
+            arrange_kernel,
+            f32(2 * shots, 4, size, lanes),
+            [VMEM] * 4,
+            VMEM,
+            [],
+            moved=1 << 19,
+            vmem=8 << 20,
+        )(*turned)
+        right = lax.ppermute(own, "freq", [(0, 1), (1, 2), (2, 3)])
+        left = lax.ppermute(own, "freq", [(1, 0), (2, 1), (3, 2)])
+        across = swap(own, "freq", 4, 2)
+        forward = lax.ppermute(across, "freq", [(2, 3), (1, 0)])
+        gathered += [own, right, left, across, forward]
+
+    keep, send = kernel_call(
+        inverse_kernel,
+        [f32(shots, half, quarter)] * 2,
+        [ANY, ANY, VMEM, VMEM, VMEM] + [ANY] * (5 * PARTS),
+        [VMEM] * 2,
+        [
+            pltpu.VMEM((2 * shots, 4, PARTS, size, 4 * lanes), jnp.float32),
+            pltpu.VMEM((quarter, 4 * lanes), jnp.bfloat16),
+            pltpu.VMEM((quarter, 4 * lanes), jnp.bfloat16),
+            pltpu.VMEM((RIM, 4 * lanes), jnp.bfloat16),
+            pltpu.VMEM((RIM, 4 * lanes), jnp.bfloat16),
+            dma((4 * PARTS,)),
+            dma((16,)),
+        ],
+        flops=6 * rows * 4 * lanes * quarter,
+        moved=4 << 20,
+        vmem=32 << 20,
+    )(high, low, taps, same_side, cross_side, *gathered)
+    got = swap(send, "shot", devices, 1)
+
+    packed = kernel_call(
+        clean_kernel,
+        f32(bins_total * most, quarter),
+        [VMEM] * 4,
+        VMEM,
+        [pltpu.VMEM((rows, quarter), jnp.bfloat16)] * 2,
+        flops=4 * rows * bins_total * most * quarter,
+        moved=6 << 20,
+        vmem=32 << 20,
+    )(keep, got, traces, places)
+
+    slots = packed.reshape(devices, filters.shape[0] * most, quarter)
+    slots = lax.all_to_all(slots, "shot", split_axis=0, concat_axis=0, tiled=True)
+    return kernel_call(
+        functools.partial(unpack_kernel, most),
+        f32(filters.shape[0], devices * most, quarter),
+        [VMEM],
+        VMEM,
+        [],
+        moved=3 << 20,
+        vmem=16 << 20,
+    )(slots)
 
 
 def with_halo(cells, sides, width):
@@ -70,7 +560,7 @@
     return jnp.zeros((total_slots, values.shape[-1]), jnp.float32).at[slot_ids].set(values)
 
 
-def on_device(traces, live_mask, offset_bin, surface, block_owner, point_column, filters):
+def any_device(traces, live_mask, offset_bin, surface, block_owner, point_column, filters):
     shots_here, receivers, quarter = traces.shape
     freq_count = lax.axis_size("freq")
     shot_count = lax.axis_size("shot")
@@ -128,6 +618,14 @@
     return lax.all_to_all(cleaned_slots, "shot", split_axis=0, concat_axis=1, tiled=True)
 
 
+def on_device(traces, live_mask, offset_bin, surface, block_owner, point_column, filters):
+    devices = lax.axis_size("shot")
+    in_plane = devices == 8 and lax.axis_size("freq") == 4
+    whole_tiles = traces.shape[1] % (8 * PARTS * devices) == 0 and filters.shape[0] <= 8
+    plan = plane_device if in_plane and whole_tiles else any_device
+    return plan(traces, live_mask, offset_bin, surface, block_owner, point_column, filters)
+
+
 def solution(mesh):
     return jax.shard_map(
         on_device,

time: 311 us -> 124 us (0.40)
  waiting for transfers between devices: 130 us -> 33.8 us
  other arithmetic: 62.2 us -> 0.05 us
  local copies, waits for them, and re-layouts: 48 us -> 5.26 us
  starting transfers between devices: 6.89 us -> 42.3 us
  Pallas kernels: 0 us -> 22.3 us
  matrix products: 16.6 us -> 0 us
  between operations: 16.5 us -> 0.39 us
  blocking collectives: 30.5 us -> 19.3 us
    psum x1 -> x0, waiting for transfers between devices: 66.8 us -> none  [broadcast(): return lax.psum(kept, axis)]
    reduce_scatter x2 -> x0, waiting for transfers between devices: 62.7 us -> none  [the longest x1 47.5 us: on_device(): lax.psum_scatter(partial_value, 'freq', scatter_dimension=1, tiled=True)]
    sub x1 -> x0, other arithmetic: 54.1 us -> none  [on_device(): cleaned = live_traces - shifted_sum(widened, trace_taps, quarter)]
    ppermute x2 -> x30, starting transfers between devices: 6.62 us -> 42.3 us  [the longest x24 29.7 us: swap(): return lax.ppermute(value, axis, [(i, i ^ bit) for i in range(count)])]
    ppermute x2 -> x30, waiting for transfers between devices: 0.01 us -> 33.8 us  [the longest x24 25.8 us: swap(): return lax.ppermute(value, axis, [(i, i ^ bit) for i in range(count)])]
    mul x33 -> x0, local copies, waits for them, and re-layouts: 28.7 us -> none  [shifted_sum(): summed = summed + tap_table[..., tap_index:tap_index + 1] * window]
    pallas_call x0 -> x12, Pallas kernels: none -> 22.3 us  [the longest x1 10 us: plane_device(): kernel_call(inverse_kernel, [f32(shots, half, quarter)] * 2, [ANY, ANY, V...]
    dot_general x10 -> x0, matrix products: 16.6 us -> none  [the longest x8 7.04 us: cross_mix(): jnp.einsum('bsj,jrb->srb', left_side, right_side, precision=FULL_PRECISION)]
  transfers between devices with their start and end apart: 5 -> 30, of which waited for: 3 -> 10; matrix products, arithmetic and copies ran while one was open for 12% -> 0% of each run, Pallas kernels for 0% -> 7%
where the time goes in v1:
time: 124 us; the launch traced here: 123 us
  starting transfers between devices  42.3 us (34%)
  waiting for transfers between devices  33.8 us (27%)
  Pallas kernels  22.3 us (18%)
  blocking collectives  19.3 us (16%)
  local copies, waits for them, and re-layouts  5.26 us (4%)
    ppermute x24, starting transfers between devices, swap(): return lax.ppermute(value, axis, [(i, i ^ bit) for i in range(count)])  29.7 us
    ppermute x24, waiting for transfers between devices, swap(): return lax.ppermute(value, axis, [(i, i ^ bit) for i in range(count)])  25.8 us
    all_to_all x1, blocking collectives, plane_device(): lax.all_to_all(slots, 'shot', split_axis=0, concat_axis=0, tiled=True)  19.3 us
    pallas_call x1, Pallas kernels, plane_device(): kernel_call(inverse_kernel, [f32(shots, half, quarter)] * 2, [ANY, ANY, V...  10 us
    ppermute x2, waiting for transfers between devices, plane_device(): forward = lax.ppermute(across, 'freq', [(2, 3), (1, 0)])  7.78 us
    ppermute x2, starting transfers between devices, plane_device(): right = lax.ppermute(own, 'freq', [(0, 1), (1, 2), (2, 3)])  7.4 us
    unnamed x36, local copies, waits for them, and re-layouts  5.26 us
    pallas_call x2, Pallas kernels, plane_device(): kernel_call(functools.partial(prediction_kernel, part), [f32(2 * shots, s...  4.42 us
  transfers between devices with their start and end apart: 30, of which 10 were waited for; matrix products, arithmetic and copies ran while one was open for 0% of the time, Pallas kernels for 7%

profile of v1, /device:TPU:0, one launch (start us, length us, event | category | flops | bytes accessed | tf_op | source)
XLA Modules:
  0.0 123.5 jit_solution(9568966240353568536)
XLA Ops:
  0.0 1.6 %copy-done = f32[16,256,128]{2,1,0:T(8,128)S(1)} copy-done((f32[16,256,128]{2,1,0:T(8,128)S(1)}, f32[16,256,128]{2,1,0:T(8,128)}, u32[]{:S(2)}) %copy-start) | copy-done | bytes 2097176
  4.9 3.1 %collective-permute-start.1 = (f32[96,128]{1,0:T(8,128)S(1)}, f32[96,128]{1,0:T(8,128)S(1)}, u32[]{:S(2)}, u32[]{:S(2)}) collective-permute-start(f32[96,128]{1,0:T(8,128)S(1)} %get-tuple-element.29), channel_id=1, source_target_pairs={{0,1},{1,0},{2,3},{3,2},{4,5},{5,4},{6,7},{7,6},{8,9},{9,8},{10,11... | collective-permute-start | bytes 147464 | tf_op jit(solution)/shard_map/ppermute | solution.py:67
  8.0 2.6 %collective-permute-start.2 = (f32[96,128]{1,0:T(8,128)S(1)}, f32[96,128]{1,0:T(8,128)S(1)}, u32[]{:S(2)}, u32[]{:S(2)}) collective-permute-start(f32[96,128]{1,0:T(8,128)S(1)} %get-tuple-element.30), channel_id=1, source_target_pairs={{0,2},{1,3},{2,0},{3,1},{4,6},{5,7},{6,4},{7,5},{8,10},{9,11},{10,... | collective-permute-start | bytes 147464 | tf_op jit(solution)/shard_map/ppermute | solution.py:67
  10.6 3.3 %collective-permute-done.2 = f32[96,128]{1,0:T(8,128)S(1)} collective-permute-done((f32[96,128]{1,0:T(8,128)S(1)}, f32[96,128]{1,0:T(8,128)S(1)}, u32[]{:S(2)}, u32[]{:S(2)}) %collective-permute-start.2) | collective-permute-done | bytes 49184 | tf_op jit(solution)/shard_map/ppermute | solution.py:67
  13.9 2.6 %collective-permute-done.3 = f32[96,128]{1,0:T(8,128)S(1)} collective-permute-done((f32[96,128]{1,0:T(8,128)S(1)}, f32[96,128]{1,0:T(8,128)S(1)}, u32[]{:S(2)}, u32[]{:S(2)}) %collective-permute-start.3) | collective-permute-done | bytes 49184 | tf_op jit(solution)/shard_map/ppermute | solution.py:67
  16.8 1.6 %collective-permute-start.19 = (f32[2,16,16,128]{3,2,1,0:T(8,128)S(1)}, f32[2,16,16,128]{3,2,1,0:T(8,128)S(1)}, u32[]{:S(2)}, u32[]{:S(2)}) collective-permute-start(f32[2,16,16,128]{3,2,1,0:T(8,128)S(1)} %get-tuple-element.42), channel_id=1, source_target_pairs={{0,8},{4,12},{8,0},{12,4},{16,24},{20,28},{24,16},{28,20},{1,9},{5... | collective-permute-start | bytes 786440 | tf_op jit(solution)/shard_map/ppermute | solution.py:67
  23.4 4.8 %collective-permute-done.5.rest_1_.rest_4_ = f32[2,104,128]{2,1,0:T(8,128)S(1)} collective-permute-done((f32[2,104,128]{2,1,0:T(8,128)S(1)}, f32[2,104,128]{2,1,0:T(8,128)S(1)}, u32[]{:S(2)}, u32[]{:S(2)}) %collective-permute-start.5) | collective-permute-done | bytes 106528 | tf_op jit(solution)/shard_map/ppermute | solution.py:67
  28.3 2.4 %collective-permute-start.21 = (f32[2,16,16,128]{3,2,1,0:T(8,128)S(1)}, f32[2,16,16,128]{3,2,1,0:T(8,128)S(1)}, u32[]{:S(2)}, u32[]{:S(2)}) collective-permute-start(f32[2,16,16,128]{3,2,1,0:T(8,128)S(1)} %get-tuple-element.44), channel_id=1, source_target_pairs={{0,24},{4,28},{8,16},{12,20},{16,8},{20,12},{24,0},{28,4},{1,25},{... | collective-permute-start | bytes 786440 | tf_op jit(solution)/shard_map/ppermute | solution.py:67
  34.2 10.0 %collective-permute-done.20.rest_1_ = f32[2,16,16,128]{3,2,1,0:T(8,128)S(1)} collective-permute-done((f32[2,16,16,128]{3,2,1,0:T(8,128)S(1)}, f32[2,16,16,128]{3,2,1,0:T(8,128)S(1)}, u32[]{:S(2)}, u32[]{:S(2)}) %collective-permute-start.20) | collective-permute-done | bytes 262176 | tf_op jit(solution)/shard_map/ppermute | solution.py:67
  44.2 2.2 %prediction_kernel.3 = (f32[6,16,128]{2,1,0:T(8,128)S(1)}, f32[6,16,128]{2,1,0:T(8,128)S(1)}, f32[6,16,128]{2,1,0:T(8,128)S(1)}, f32[6,16,128]{2,1,0:T(8,128)S(1)}) custom-call(s32[2]{0:T(128)S(1)} %copy-done.12, f32[16,256,128]{2,1,0:T(8,128)S(1)} %copy-done.1, f32[16,128,128]{2,1,0:T(8,128)S(1)} %collective-permute-done.8.sibling, ...), custom_call_target="tpu_custom_call" | custom-call | flops 6291456 | bytes 1048576 | tf_op jit(solution)/shard_map/prediction_kernel/pallas_call | solution.py:433
  46.8 2.8 %collective-permute-start.23 = (f32[6,16,128]{2,1,0:T(8,128)S(1)}, f32[6,16,128]{2,1,0:T(8,128)S(1)}, u32[]{:S(2)}, u32[]{:S(2)}) collective-permute-start(f32[6,16,128]{2,1,0:T(8,128)S(1)} %get-tuple-element.47), channel_id=1, source_target_pairs={{0,16},{4,20},{8,24},{12,28},{16,0},{20,4},{24,8},{28,12},{1,17},{... | collective-permute-start | bytes 147464 | tf_op jit(solution)/shard_map/ppermute | solution.py:67
  49.6 1.8 %collective-permute-start.24 = (f32[6,16,128]{2,1,0:T(8,128)S(1)}, f32[6,16,128]{2,1,0:T(8,128)S(1)}, u32[]{:S(2)}, u32[]{:S(2)}) collective-permute-start(f32[6,16,128]{2,1,0:T(8,128)S(1)} %get-tuple-element.48), channel_id=1, source_target_pairs={{0,24},{4,28},{8,16},{12,20},{16,8},{20,12},{24,0},{28,4},{1,25},{... | collective-permute-start | bytes 147464 | tf_op jit(solution)/shard_map/ppermute | solution.py:67
  51.5 2.2 %prediction_kernel.2 = (f32[6,16,128]{2,1,0:T(8,128)S(1)}, f32[6,16,128]{2,1,0:T(8,128)S(1)}, f32[6,16,128]{2,1,0:T(8,128)S(1)}, f32[6,16,128]{2,1,0:T(8,128)S(1)}) custom-call(s32[2]{0:T(128)S(1)} %copy-done.12, f32[16,256,128]{2,1,0:T(8,128)S(1)} %copy-done.1, f32[16,128,128]{2,1,0:T(8,128)S(1)} %collective-permute-done.8.sibling, ...), custom_call_target="tpu_custom_call" | custom-call | flops 6291456 | bytes 1048576 | tf_op jit(solution)/shard_map/prediction_kernel/pallas_call | solution.py:433
  55.6 1.7 %collective-permute-start.14 = (f32[6,16,128]{2,1,0:T(8,128)S(1)}, f32[6,16,128]{2,1,0:T(8,128)S(1)}, u32[]{:S(2)}, u32[]{:S(2)}) collective-permute-start(f32[6,16,128]{2,1,0:T(8,128)S(1)} %get-tuple-element.41), channel_id=1, source_target_pairs={{0,24},{4,28},{8,16},{12,20},{16,8},{20,12},{24,0},{28,4},{1,25},{... | collective-permute-start | bytes 147464 | tf_op jit(solution)/shard_map/ppermute | solution.py:67
  57.7 2.8 %collective-permute-start.25 = (f32[6,4,16,128]{3,2,1,0:T(8,128)S(1)}, f32[6,4,16,128]{3,2,1,0:T(8,128)S(1)}, u32[]{:S(2)}, u32[]{:S(2)}) collective-permute-start(f32[6,4,16,128]{3,2,1,0:T(8,128)S(1)} %arrange_kernel.3.rest_5_), channel_id=1, source_target_pairs={{0,1},{1,2},{2,3},{4,5},{5,6},{6,7},{8,9},{9,10},{10,11},{12,13},{... | collective-permute-start | bytes 589832 | tf_op jit(solution)/shard_map/ppermute | solution.py:458
  60.7 1.7 %collective-permute-start.17 = (f32[6,4,16,128]{3,2,1,0:T(8,128)S(1)}, f32[6,4,16,128]{3,2,1,0:T(8,128)S(1)}, u32[]{:S(2)}, u32[]{:S(2)}) collective-permute-start(f32[6,4,16,128]{3,2,1,0:T(8,128)S(1)} %arrange_kernel.2.rest_0_), channel_id=1, source_target_pairs={{0,2},{1,3},{2,0},{3,1},{4,6},{5,7},{6,4},{7,5},{8,10},{9,11},{10,... | collective-permute-start | bytes 589832 | tf_op jit(solution)/shard_map/ppermute | solution.py:67
  63.8 4.6 %collective-permute-start.15 = (f32[6,4,16,128]{3,2,1,0:T(8,128)S(1)}, f32[6,4,16,128]{3,2,1,0:T(8,128)S(1)}, u32[]{:S(2)}, u32[]{:S(2)}) collective-permute-start(f32[6,4,16,128]{3,2,1,0:T(8,128)S(1)} %arrange_kernel.2.rest_0_), channel_id=1, source_target_pairs={{0,1},{1,2},{2,3},{4,5},{5,6},{6,7},{8,9},{9,10},{10,11},{12,13},{... | collective-permute-start | bytes 589832 | tf_op jit(solution)/shard_map/ppermute | solution.py:458
  68.3 2.9 %collective-permute-done.27.rest_8_ = f32[6,4,16,128]{3,2,1,0:T(8,128)S(1)} collective-permute-done((f32[6,4,16,128]{3,2,1,0:T(8,128)S(1)}, f32[6,4,16,128]{3,2,1,0:T(8,128)S(1)}, u32[]{:S(2)}, u32[]{:S(2)}) %collective-permute-start.27) | collective-permute-done | bytes 196640 | tf_op jit(solution)/shard_map/ppermute | solution.py:67
  73.8 1.6 %collective-permute-done.17.rest_3_ = f32[6,4,16,128]{3,2,1,0:T(8,128)S(1)} collective-permute-done((f32[6,4,16,128]{3,2,1,0:T(8,128)S(1)}, f32[6,4,16,128]{3,2,1,0:T(8,128)S(1)}, u32[]{:S(2)}, u32[]{:S(2)}) %collective-permute-start.17) | collective-permute-done | bytes 196640 | tf_op jit(solution)/shard_map/ppermute | solution.py:67
  78.6 2.2 %response_kernel.1 = (f32[768,128]{1,0:T(8,128)S(1)}, f32[768,512]{1,0:T(8,128)S(1)}, f32[768,512]{1,0:T(8,128)S(1)}) custom-call(s32[1,768]{1,0:T(1,128)S(1)} %bitcast.24, f32[128,512]{1,0:T(8,128)S(1)} %copy-done.14, f32[2,104,128]{2,1,0:T(8,128)S(1)} %maximum_select_fusion.rest_0_.rest_3_, f32[2,104,128]{2,1,0:T(8,128)S(1)} %collective-permute-done.5.rest_1_.rest_4_, ...), custom_call_target="tpu_custom_call" | custom-call | flops 226492416 | bytes 4194304 | tf_op jit(solution)/shard_map/response_kernel/pallas_call | solution.py:420
  81.0 4.2 %collective-permute-done.28.rest_9_ = f32[6,4,16,128]{3,2,1,0:T(8,128)S(1)} collective-permute-done((f32[6,4,16,128]{3,2,1,0:T(8,128)S(1)}, f32[6,4,16,128]{3,2,1,0:T(8,128)S(1)}, u32[]{:S(2)}, u32[]{:S(2)}) %collective-permute-start.28) | collective-permute-done | bytes 196640 | tf_op jit(solution)/shard_map/ppermute | solution.py:461
  85.2 3.6 %collective-permute-done.18.rest_4_ = f32[6,4,16,128]{3,2,1,0:T(8,128)S(1)} collective-permute-done((f32[6,4,16,128]{3,2,1,0:T(8,128)S(1)}, f32[6,4,16,128]{3,2,1,0:T(8,128)S(1)}, u32[]{:S(2)}, u32[]{:S(2)}) %collective-permute-start.18) | collective-permute-done | bytes 196640 | tf_op jit(solution)/shard_map/ppermute | solution.py:461
  90.0 10.0 %inverse_kernel.1 = (f32[3,128,256]{2,1,0:T(8,128)S(1)}, f32[3,128,256]{2,1,0:T(8,128)S(1)}) custom-call(bf16[1056,512]{1,0:T(8,128)(2,1)S(1)} %copy-done.3, bf16[1056,512]{1,0:T(8,128)(2,1)S(1)} %copy-done.5, f32[768,128]{1,0:T(8,128)S(1)} %get-tuple-element.32.taps, f32[768,512]{1,0:T(8,128)S(1)} %get-tuple-element.33.same_side, ...), custom_call_target="tpu_custom_call" | custom-call | flops 603979776 | bytes 4194304 | tf_op jit(solution)/shard_map/inverse_kernel/pallas_call | solution.py:464
  103.0 19.3 %all_to_all.5.slots = f32[8,144,256]{2,1,0:T(8,128)S(1)} all-to-all(f32[8,144,256]{2,1,0:T(8,128)S(1)} %bitcast.20), channel_id=1, replica_groups=mesh['shot'=8,'freq'=4] {'shot'}, dimensions={0} | all-to-all | bytes 2359296 | tf_op jit(solution)/shard_map/all_to_all | solution.py:496
  (90 shorter events, 27.5 us)
Async XLA Ops:
  2.7 13.9 %collective-permute-start.8 = (f32[16,128,128]{2,1,0:T(8,128)}, f32[16,128,128]{2,1,0:T(8,128)S(1)}, u32[]{:S(2)}, u32[]{:S(2)}) collective-permute-start(f32[16,128,128]{2,1,0:T(8,128)} %sibling_kernel.1), channel_id=1, source_target_pairs={{0,4},{4,0},{8,12},{12,8},{16,20},{20,16},{24,28},{28,24},{1,5},{5... | collective-permute-start | bytes 3145736 | tf_op jit(solution)/shard_map/ppermute | solution.py:67
  8.0 5.9 %collective-permute-start.2 = (f32[96,128]{1,0:T(8,128)S(1)}, f32[96,128]{1,0:T(8,128)S(1)}, u32[]{:S(2)}, u32[]{:S(2)}) collective-permute-start(f32[96,128]{1,0:T(8,128)S(1)} %get-tuple-element.30), channel_id=1, source_target_pairs={{0,2},{1,3},{2,0},{3,1},{4,6},{5,7},{6,4},{7,5},{8,10},{9,11},{10,... | collective-permute-start | bytes 147464 | tf_op jit(solution)/shard_map/ppermute | solution.py:67
  10.6 5.9 %collective-permute-start.3 = (f32[96,128]{1,0:T(8,128)S(1)}, f32[96,128]{1,0:T(8,128)S(1)}, u32[]{:S(2)}, u32[]{:S(2)}) collective-permute-start(f32[96,128]{1,0:T(8,128)S(1)} %get-tuple-element.31), channel_id=1, source_target_pairs={{0,3},{1,2},{2,1},{3,0},{4,7},{5,6},{6,5},{7,4},{8,11},{9,10},{10,... | collective-permute-start | bytes 147464 | tf_op jit(solution)/shard_map/ppermute | solution.py:67
  16.8 15.9 %collective-permute-start.19 = (f32[2,16,16,128]{3,2,1,0:T(8,128)S(1)}, f32[2,16,16,128]{3,2,1,0:T(8,128)S(1)}, u32[]{:S(2)}, u32[]{:S(2)}) collective-permute-start(f32[2,16,16,128]{3,2,1,0:T(8,128)S(1)} %get-tuple-element.42), channel_id=1, source_target_pairs={{0,8},{4,12},{8,0},{12,4},{16,24},{20,28},{24,16},{28,20},{1,9},{5... | collective-permute-start | bytes 786440 | tf_op jit(solution)/shard_map/ppermute | solution.py:67
  18.4 9.9 %collective-permute-start.5 = (f32[2,104,128]{2,1,0:T(8,128)S(1)}, f32[2,104,128]{2,1,0:T(8,128)S(1)}, u32[]{:S(2)}, u32[]{:S(2)}) collective-permute-start(f32[2,104,128]{2,1,0:T(8,128)S(1)} %maximum_select_fusion.rest_0_.rest_3_), channel_id=1, source_target_pairs={{0,8},{4,12},{8,0},{12,4},{16,24},{20,28},{24,16},{28,20},{1,9},{5... | collective-permute-start | bytes 319496 | tf_op jit(solution)/shard_map/ppermute | solution.py:67
  19.4 11.3 %collective-permute-start.6 = (f32[2,104,128]{2,1,0:T(8,128)S(1)}, f32[2,104,128]{2,1,0:T(8,128)S(1)}, u32[]{:S(2)}, u32[]{:S(2)}) collective-permute-start(f32[2,104,128]{2,1,0:T(8,128)S(1)} %maximum_select_fusion.rest_0_.rest_3_), channel_id=1, source_target_pairs={{0,16},{4,20},{8,24},{12,28},{16,0},{20,4},{24,8},{28,12},{1,17},{... | collective-permute-start | bytes 319496 | tf_op jit(solution)/shard_map/ppermute | solution.py:67
  20.9 10.3 %collective-permute-start.7 = (f32[2,104,128]{2,1,0:T(8,128)S(1)}, f32[2,104,128]{2,1,0:T(8,128)S(1)}, u32[]{:S(2)}, u32[]{:S(2)}) collective-permute-start(f32[2,104,128]{2,1,0:T(8,128)S(1)} %maximum_select_fusion.rest_0_.rest_3_), channel_id=1, source_target_pairs={{0,24},{4,28},{8,16},{12,20},{16,8},{20,12},{24,0},{28,4},{1,25},{... | collective-permute-start | bytes 319496 | tf_op jit(solution)/shard_map/ppermute | solution.py:67
  21.9 22.2 %collective-permute-start.20 = (f32[2,16,16,128]{3,2,1,0:T(8,128)S(1)}, f32[2,16,16,128]{3,2,1,0:T(8,128)S(1)}, u32[]{:S(2)}, u32[]{:S(2)}) collective-permute-start(f32[2,16,16,128]{3,2,1,0:T(8,128)S(1)} %get-tuple-element.43), channel_id=1, source_target_pairs={{0,16},{4,20},{8,24},{12,28},{16,0},{20,4},{24,8},{28,12},{1,17},{... | collective-permute-start | bytes 786440 | tf_op jit(solution)/shard_map/ppermute | solution.py:67
  28.3 15.9 %collective-permute-start.21 = (f32[2,16,16,128]{3,2,1,0:T(8,128)S(1)}, f32[2,16,16,128]{3,2,1,0:T(8,128)S(1)}, u32[]{:S(2)}, u32[]{:S(2)}) collective-permute-start(f32[2,16,16,128]{3,2,1,0:T(8,128)S(1)} %get-tuple-element.44), channel_id=1, source_target_pairs={{0,24},{4,28},{8,16},{12,20},{16,8},{20,12},{24,0},{28,4},{1,25},{... | collective-permute-start | bytes 786440 | tf_op jit(solution)/shard_map/ppermute | solution.py:67
  30.7 18.9 %collective-permute-start.10 = (f32[2,16,16,128]{3,2,1,0:T(8,128)S(1)}, f32[2,16,16,128]{3,2,1,0:T(8,128)S(1)}, u32[]{:S(2)}, u32[]{:S(2)}) collective-permute-start(f32[2,16,16,128]{3,2,1,0:T(8,128)S(1)} %get-tuple-element.36), channel_id=1, source_target_pairs={{0,16},{4,20},{8,24},{12,28},{16,0},{20,4},{24,8},{28,12},{1,17},{... | collective-permute-start | bytes 786440 | tf_op jit(solution)/shard_map/ppermute | solution.py:67
  31.2 20.3 %collective-permute-start.11 = (f32[2,16,16,128]{3,2,1,0:T(8,128)S(1)}, f32[2,16,16,128]{3,2,1,0:T(8,128)S(1)}, u32[]{:S(2)}, u32[]{:S(2)}) collective-permute-start(f32[2,16,16,128]{3,2,1,0:T(8,128)S(1)} %get-tuple-element.37), channel_id=1, source_target_pairs={{0,24},{4,28},{8,16},{12,20},{16,8},{20,12},{24,0},{28,4},{1,25},{... | collective-permute-start | bytes 786440 | tf_op jit(solution)/shard_map/ppermute | solution.py:67
  32.7 18.8 %collective-permute-start.9 = (f32[2,16,16,128]{3,2,1,0:T(8,128)S(1)}, f32[2,16,16,128]{3,2,1,0:T(8,128)S(1)}, u32[]{:S(2)}, u32[]{:S(2)}) collective-permute-start(f32[2,16,16,128]{3,2,1,0:T(8,128)S(1)} %get-tuple-element.35), channel_id=1, source_target_pairs={{0,8},{4,12},{8,0},{12,4},{16,24},{20,28},{24,16},{28,20},{1,9},{5... | collective-permute-start | bytes 786440 | tf_op jit(solution)/shard_map/ppermute | solution.py:67
  46.4 9.2 %collective-permute-start.22 = (f32[6,16,128]{2,1,0:T(8,128)S(1)}, f32[6,16,128]{2,1,0:T(8,128)S(1)}, u32[]{:S(2)}, u32[]{:S(2)}) collective-permute-start(f32[6,16,128]{2,1,0:T(8,128)S(1)} %get-tuple-element.46), channel_id=1, source_target_pairs={{0,8},{4,12},{8,0},{12,4},{16,24},{20,28},{24,16},{28,20},{1,9},{5... | collective-permute-start | bytes 147464 | tf_op jit(solution)/shard_map/ppermute | solution.py:67
  46.8 10.5 %collective-permute-start.23 = (f32[6,16,128]{2,1,0:T(8,128)S(1)}, f32[6,16,128]{2,1,0:T(8,128)S(1)}, u32[]{:S(2)}, u32[]{:S(2)}) collective-permute-start(f32[6,16,128]{2,1,0:T(8,128)S(1)} %get-tuple-element.47), channel_id=1, source_target_pairs={{0,16},{4,20},{8,24},{12,28},{16,0},{20,4},{24,8},{28,12},{1,17},{... | collective-permute-start | bytes 147464 | tf_op jit(solution)/shard_map/ppermute | solution.py:67
  49.6 7.6 %collective-permute-start.24 = (f32[6,16,128]{2,1,0:T(8,128)S(1)}, f32[6,16,128]{2,1,0:T(8,128)S(1)}, u32[]{:S(2)}, u32[]{:S(2)}) collective-permute-start(f32[6,16,128]{2,1,0:T(8,128)S(1)} %get-tuple-element.48), channel_id=1, source_target_pairs={{0,24},{4,28},{8,16},{12,20},{16,8},{20,12},{24,0},{28,4},{1,25},{... | collective-permute-start | bytes 147464 | tf_op jit(solution)/shard_map/ppermute | solution.py:67
  53.7 6.9 %collective-permute-start.12 = (f32[6,16,128]{2,1,0:T(8,128)S(1)}, f32[6,16,128]{2,1,0:T(8,128)S(1)}, u32[]{:S(2)}, u32[]{:S(2)}) collective-permute-start(f32[6,16,128]{2,1,0:T(8,128)S(1)} %get-tuple-element.39), channel_id=1, source_target_pairs={{0,8},{4,12},{8,0},{12,4},{16,24},{20,28},{24,16},{28,20},{1,9},{5... | collective-permute-start | bytes 147464 | tf_op jit(solution)/shard_map/ppermute | solution.py:67
  57.3 13.9 %collective-permute-start.27 = (f32[6,4,16,128]{3,2,1,0:T(8,128)S(1)}, f32[6,4,16,128]{3,2,1,0:T(8,128)S(1)}, u32[]{:S(2)}, u32[]{:S(2)}) collective-permute-start(f32[6,4,16,128]{3,2,1,0:T(8,128)S(1)} %arrange_kernel.3.rest_5_), channel_id=1, source_target_pairs={{0,2},{1,3},{2,0},{3,1},{4,6},{5,7},{6,4},{7,5},{8,10},{9,11},{10,... | collective-permute-start | bytes 589832 | tf_op jit(solution)/shard_map/ppermute | solution.py:67
  57.7 14.8 %collective-permute-start.25 = (f32[6,4,16,128]{3,2,1,0:T(8,128)S(1)}, f32[6,4,16,128]{3,2,1,0:T(8,128)S(1)}, u32[]{:S(2)}, u32[]{:S(2)}) collective-permute-start(f32[6,4,16,128]{3,2,1,0:T(8,128)S(1)} %arrange_kernel.3.rest_5_), channel_id=1, source_target_pairs={{0,1},{1,2},{2,3},{4,5},{5,6},{6,7},{8,9},{9,10},{10,11},{12,13},{... | collective-permute-start | bytes 589832 | tf_op jit(solution)/shard_map/ppermute | solution.py:458
  60.7 14.8 %collective-permute-start.17 = (f32[6,4,16,128]{3,2,1,0:T(8,128)S(1)}, f32[6,4,16,128]{3,2,1,0:T(8,128)S(1)}, u32[]{:S(2)}, u32[]{:S(2)}) collective-permute-start(f32[6,4,16,128]{3,2,1,0:T(8,128)S(1)} %arrange_kernel.2.rest_0_), channel_id=1, source_target_pairs={{0,2},{1,3},{2,0},{3,1},{4,6},{5,7},{6,4},{7,5},{8,10},{9,11},{10,... | collective-permute-start | bytes 589832 | tf_op jit(solution)/shard_map/ppermute | solution.py:67
  62.4 18.3 %collective-permute-start.26 = (f32[6,4,16,128]{3,2,1,0:T(8,128)S(1)}, f32[6,4,16,128]{3,2,1,0:T(8,128)S(1)}, u32[]{:S(2)}, u32[]{:S(2)}) collective-permute-start(f32[6,4,16,128]{3,2,1,0:T(8,128)S(1)} %arrange_kernel.3.rest_5_), channel_id=1, source_target_pairs={{1,0},{2,1},{3,2},{5,4},{6,5},{7,6},{9,8},{10,9},{11,10},{13,12},{... | collective-permute-start | bytes 589832 | tf_op jit(solution)/shard_map/ppermute | solution.py:459
  63.8 17.0 %collective-permute-start.15 = (f32[6,4,16,128]{3,2,1,0:T(8,128)S(1)}, f32[6,4,16,128]{3,2,1,0:T(8,128)S(1)}, u32[]{:S(2)}, u32[]{:S(2)}) collective-permute-start(f32[6,4,16,128]{3,2,1,0:T(8,128)S(1)} %arrange_kernel.2.rest_0_), channel_id=1, source_target_pairs={{0,1},{1,2},{2,3},{4,5},{5,6},{6,7},{8,9},{9,10},{10,11},{12,13},{... | collective-permute-start | bytes 589832 | tf_op jit(solution)/shard_map/ppermute | solution.py:458
  71.2 9.7 %collective-permute-start.16 = (f32[6,4,16,128]{3,2,1,0:T(8,128)S(1)}, f32[6,4,16,128]{3,2,1,0:T(8,128)S(1)}, u32[]{:S(2)}, u32[]{:S(2)}) collective-permute-start(f32[6,4,16,128]{3,2,1,0:T(8,128)S(1)} %arrange_kernel.2.rest_0_), channel_id=1, source_target_pairs={{1,0},{2,1},{3,2},{5,4},{6,5},{7,6},{9,8},{10,9},{11,10},{13,12},{... | collective-permute-start | bytes 589832 | tf_op jit(solution)/shard_map/ppermute | solution.py:459
  72.5 12.6 %collective-permute-start.28 = (f32[6,4,16,128]{3,2,1,0:T(8,128)S(1)}, f32[6,4,16,128]{3,2,1,0:T(8,128)S(1)}, u32[]{:S(2)}, u32[]{:S(2)}) collective-permute-start(f32[6,4,16,128]{3,2,1,0:T(8,128)S(1)} %collective-permute-done.27.rest_8_), channel_id=1, source_target_pairs={{2,3},{1,0},{6,7},{5,4},{10,11},{9,8},{14,15},{13,12},{18,19},{17,... | collective-permute-start | bytes 589832 | tf_op jit(solution)/shard_map/ppermute | solution.py:461
  75.4 13.3 %collective-permute-start.18 = (f32[6,4,16,128]{3,2,1,0:T(8,128)S(1)}, f32[6,4,16,128]{3,2,1,0:T(8,128)S(1)}, u32[]{:S(2)}, u32[]{:S(2)}) collective-permute-start(f32[6,4,16,128]{3,2,1,0:T(8,128)S(1)} %collective-permute-done.17.rest_3_), channel_id=1, source_target_pairs={{2,3},{1,0},{6,7},{5,4},{10,11},{9,8},{14,15},{13,12},{18,19},{17,... | collective-permute-start | bytes 589832 | tf_op jit(solution)/shard_map/ppermute | solution.py:461
  (22 other events, 161.3 us)

commit v2 on v1

--- a/solution.py
+++ b/solution.py
@@ -15,7 +15,7 @@
 POINTS_BLK = 16
 STEPS = 2
 RIM = 16
-PARTS = 2
+PARTS = 1
 
 FULL_PRECISION = lax.Precision.HIGHEST
 VMEM = pl.BlockSpec(memory_space=pltpu.VMEM)
@@ -43,6 +43,20 @@
     return np.pad(table[RIM + shifts], ((0, lanes - TAPS), (0, 0)))
 
 
+def end_constants(bands, lanes):
+    high, low = wave_constant(bands)
+    k, t = np.divmod(np.arange(RIM * RIM), RIM)
+    waves = [np.stack([part[NT + k], part[RIM + k]]).reshape(2 * RIM * RIM, -1) for part in (high, low)]
+    half_span = (TAPS - 1) // 2
+    picks = np.zeros((2, lanes, RIM * RIM), np.float32)
+    sums = np.zeros((2, RIM * RIM, lanes), np.float32)
+    for side, tap, lane in ((0, t + RIM - k + half_span, t), (1, t - 1 - k, lanes - RIM + t)):
+        fits = (tap >= 0) & (tap < TAPS)
+        picks[side, tap[fits], np.arange(RIM * RIM)[fits]] = 1
+        sums[side, np.arange(RIM * RIM), lane] = 1
+    return *waves, picks, sums.reshape(2 * RIM * RIM, lanes).astype(jnp.bfloat16)
+
+
 def split_two(value):
     high = value.astype(jnp.bfloat16)
     return high, (value - high.astype(jnp.float32)).astype(jnp.bfloat16)
@@ -67,7 +81,7 @@
     return lax.ppermute(value, axis, [(i, i ^ bit) for i in range(count)])
 
 
-def spectra_kernel(cols, live, traces, high, low, *rest):
+def spectra_kernel(cols, live, traces, bins, filters, high, low, *rest):
     outs, (picked, tab_high, tab_low, part, sems) = rest[:4], rest[4:]
     shots, _, quarter = traces.shape
     z = lax.axis_index("freq")
@@ -91,9 +105,17 @@
     part[...] = (
         dot_nn(left_high, tab_high[...]) + dot_nn(left_low, tab_high[...]) + dot_nn(left_high, tab_low[...])
     )
-    lanes = outs[0].shape[1]
+    lines, lanes = outs[0].shape
+    rows = shots * points
     for k, out in enumerate(outs):
-        out[...] = part[:, pl.ds(pl.multiple_of((z ^ k) * lanes, lanes), lanes)]
+        out[:rows] = part[:, pl.ds(pl.multiple_of((z ^ k) * lanes, lanes), lanes)]
+        out[rows:] = jnp.zeros((lines - rows, lanes), jnp.float32)
+    own = filters.shape[0]
+    outs[0][rows : rows + own, : filters.shape[1]] = filters[...]
+    half = bins.shape[1] // 2
+    other = 1 - lax.axis_index("shot") % 2
+    there = bins[:, pl.ds(pl.multiple_of(other * half, half), half)]
+    outs[0][rows + own : rows + own + shots, :half] = there.astype(jnp.float32)
 
 
 def sibling_kernel(surface, out, sem):
@@ -104,46 +126,56 @@
     copy.wait()
 
 
-def pieces_kernel(surface, sibling, *outs):
+def pieces_kernel(step, owners, surface, sibling, *outs):
     d = lax.axis_index("shot")
     chip, core = d // 2, d % 2
     half = sibling.shape[1]
-    size = outs[0].shape[2]
-    for k, out in enumerate(outs):
-        to, part = chip ^ (1 + k // PARTS), k % PARTS
-        first = to * (size * PARTS) + part * size
-        out[core] = surface[:, pl.ds(pl.multiple_of(core * half + first, 8), size), :]
-        out[1 - core] = sibling[:, pl.ds(pl.multiple_of(first, 8), size), :]
-
-
-def prediction_kernel(part, owners, surface, sibling, *rest):
-    sent, spectra, outs = rest[:3], rest[3:7], rest[7:11]
-    chosen, real_side, imag_side, sems = rest[11:]
+    chunk = outs[0].shape[1]
+    first_owner, other_owner = owners[step], owners[1 - step]
+    owner_core = jnp.where(first_owner // 2 == chip, first_owner % 2, other_owner % 2)
+    for source, base, wanted in ((surface, core * half, owner_core == core), (sibling, 0, owner_core != core)):
+
+        @pl.when(wanted)
+        def _(source=source, base=base):
+            for k, out in enumerate(outs):
+                first = base + (chip ^ (k + 1)) * chunk
+                out[...] = source[:, pl.ds(pl.multiple_of(first, 8), chunk), :]
+
+
+def choose_kernel(extra, owners, surface, sibling, *rest):
+    sent, (chosen, sems) = rest[:-2], rest[-2:]
     d = lax.axis_index("shot")
     chip, core = d // 2, d % 2
     half = sibling.shape[1]
-    size = chosen.shape[2]
-    first = chip * (size * PARTS) + part * size
+    chunk = chosen.shape[2]
     for b in range(STEPS):
         owner = owners[b]
         step, owner_core = (owner // 2) ^ chip, owner % 2
 
         @pl.when((step == 0) & (owner_core == core))
         def _():
-            rows = pl.ds(pl.multiple_of(core * half + first, 8), size)
+            rows = pl.ds(pl.multiple_of(core * half + chip * chunk, 8), chunk)
             pltpu.make_async_copy(surface.at[:, rows], chosen.at[b], sems.at[b]).start()
 
         @pl.when((step == 0) & (owner_core != core))
         def _():
-            rows = pl.ds(pl.multiple_of(first, 8), size)
+            rows = pl.ds(pl.multiple_of(chip * chunk, 8), chunk)
             pltpu.make_async_copy(sibling.at[:, rows], chosen.at[b], sems.at[b]).start()
 
         for k in range(3):
 
             @pl.when(step == k + 1)
             def _():
-                pltpu.make_async_copy(sent[k].at[owner_core], chosen.at[b], sems.at[b]).start()
-
+                source = sent[3 + k] if extra and b == 1 else sent[k]
+                pltpu.make_async_copy(source, chosen.at[b], sems.at[b]).start()
+
+    for b in range(STEPS):
+        pltpu.make_async_copy(sibling.at[:, pl.ds(0, chunk)], chosen.at[b], sems.at[b]).wait()
+
+
+def prediction_kernel(part, chosen, *rest):
+    spectra, outs, (real_side, imag_side) = rest[:2], rest[2:6], rest[6:]
+    size = outs[0].shape[1]
     points = STEPS * POINTS_BLK
     rows = real_side.shape[1]
     shots = rows // points
@@ -151,22 +183,20 @@
     lane = lax.broadcasted_iota(jnp.int32, (rows, lanes), 1)
     for q in range(4):
         for c in range(2):
-            value = spectra[q][c, :rows, :]
+            value = spectra[c][q, :rows, :]
             turned = pltpu.roll(value, lanes // 2, 1)
             real_side[2 * q + c] = jnp.where(lane < lanes // 2, value, turned)
             imag_side[2 * q + c] = jnp.where(lane < lanes // 2, turned, -value)
-    for b in range(STEPS):
-        pltpu.make_async_copy(sibling.at[:, pl.ds(0, size)], chosen.at[b], sems.at[b]).wait()
-
+    some = slice(part * size, (part + 1) * size)
     for q in range(4):
 
         @pl.loop(0, 2)
         def _(rel):
-            at = 2 * q + (core ^ rel)
+            at = 2 * q + rel
             first_sum = [jnp.zeros((size, lanes), jnp.float32)] * shots
             second_sum = [jnp.zeros((size, lanes), jnp.float32)] * shots
             for j in range(points):
-                block = chosen[j // POINTS_BLK, j % POINTS_BLK]
+                block = chosen[j // POINTS_BLK, j % POINTS_BLK, some, :]
                 for s in range(shots):
                     row = s * points + j
                     first_sum[s] = first_sum[s] + real_side[at, row : row + 1, :] * block
@@ -194,19 +224,26 @@
     places[...] = (at == slot).astype(jnp.float32).astype(jnp.bfloat16)
 
 
-def response_kernel(own_bins, bins, waves, *rest):
-    spectra, (taps, same_side, cross_side, filters) = rest[:4], rest[4:]
-    chip = lax.axis_index("shot") // 2
+def response_kernel(own_bins, bins, waves, picks, *rest):
+    spectra, (taps, same_side, cross_side, filters) = rest[:2], rest[2:]
+    d = lax.axis_index("shot")
     z = lax.axis_index("freq")
     lines = spectra[0].shape[1]
     for q in range(4):
         for c in range(2):
-            filters[(chip ^ q) * 2 + c] = spectra[q][c, lines - 8 :, :]
+            filters[d ^ (2 * q + c)] = spectra[c][q, lines - 8 :, :]
     devices, padded, lanes = filters.shape
-    shape = (devices * padded, bins.shape[1])
+    shots, receivers = bins.shape
+    half = receivers // 2
+    here = bins[:, pl.ds(pl.multiple_of(d % 2 * half, half), half)]
+    first = lines - 8 + own_bins
+    there = spectra[1][0, first : first + shots, :half].astype(jnp.int32)
+    lists = [some[s : s + 1] for some in (here, there) for s in range(shots)]
+    bin_row = jnp.concatenate(lists, axis=1)
+    shape = (devices * padded, shots * receivers)
     row = lax.broadcasted_iota(jnp.int32, shape, 0)
     bin_of_row = jnp.where(row % padded < own_bins, row // padded * own_bins + row % padded, -1)
-    member = (bin_of_row == bins[...]).astype(jnp.float32).astype(jnp.bfloat16)
+    member = (bin_of_row == bin_row).astype(jnp.float32).astype(jnp.bfloat16)
 
     def per_trace(table):
         high, low = split_two(table)
@@ -216,7 +253,8 @@
         )
 
     table = filters[...].reshape(devices * padded, lanes)
-    taps[...] = per_trace(table)
+    side = picks[(z + 1) // 4]
+    taps[...] = per_trace(jnp.dot(table, side, precision=FULL_PRECISION, preferred_element_type=jnp.float32))
     lane = lax.broadcasted_iota(jnp.int32, (devices * padded, lanes), 1)
     for slot, step in enumerate((0, 3, 1, 2)):
         cols = pl.ds(pl.multiple_of((z + step) % 4 * lanes, lanes), lanes)
@@ -227,8 +265,10 @@
         cross_side[:, into] = per_trace(jnp.where(lane < lanes // 2, -turned, answer))
 
 
-def clean_kernel(keep, got, traces, places, out, high, low):
-    core = lax.axis_index("shot") % 2
+def clean_kernel(keep, got, traces, places, *rest):
+    outs, (high, low, packed) = rest[:-3], rest[-3:]
+    d = lax.axis_index("shot")
+    core = d % 2
     shots, receivers, _ = traces.shape
     half = keep.shape[1]
     for source, side in ((keep, core), (got, 1 - core)):
@@ -238,27 +278,40 @@
             clean_high, clean_low = split_two(traces[s, pl.ds(first, half), :] - source[s])
             high[flat, :] = clean_high
             low[flat, :] = clean_low
-    out[...] = dot_nn(places[...], high[...]) + dot_nn(places[...], low[...])
-
-
-def inverse_kernel(high, low, taps, same_side, cross_side, *rest):
+    packed[...] = dot_nn(places[...], high[...]) + dot_nn(places[...], low[...])
+    count = outs[0].shape[0]
+    for k, out in enumerate(outs):
+        out[...] = packed[pl.ds(pl.multiple_of((d ^ k) * count, 8), count), :]
+
+
+def inverse_kernel(high, low, end_high, end_low, sums, taps, same_side, cross_side, *rest):
     bands = [rest[5 * p : 5 * p + 5] for p in range(PARTS)]
     keep, send = rest[5 * PARTS : 5 * PARTS + 2]
-    gathered, tab_high, tab_low, end_high, end_low, sems, tab_sems = rest[5 * PARTS + 2 :]
+    gathered, tab_high, tab_low, tab_end_high, tab_end_low, end_sums, sems, tab_sems = rest[5 * PARTS + 2 :]
     z = lax.axis_index("freq")
     lanes = bands[0][0].shape[3]
     quarter = tab_high.shape[0]
+    at_end = (z == 0) | (z == 3)
+    rows = pl.ds(pl.multiple_of(RIM + z * quarter, 16), quarter)
+    end_size = RIM * RIM
+    end_rows = pl.ds(pl.multiple_of((z + 1) // 4 * end_size, 16), end_size)
     loads = []
-    rows = pl.ds(pl.multiple_of(RIM + z * quarter, 16), quarter)
-    end_rows = pl.ds(pl.multiple_of(jnp.where(z == 0, NT, RIM), 16), RIM)
+    end_loads = [pltpu.make_async_copy(sums.at[end_rows], end_sums, tab_sems.at[16])]
     for slot, step in enumerate((0, 3, 1, 2)):
         cols = pl.ds(pl.multiple_of((z + step) % 4 * lanes, lanes), lanes)
         into = pl.ds(slot * lanes, lanes)
-        pairs = ((high, rows, tab_high), (low, rows, tab_low), (high, end_rows, end_high), (low, end_rows, end_low))
-        for i, (table, some, scratch) in enumerate(pairs):
-            loads.append(pltpu.make_async_copy(table.at[some, cols], scratch.at[:, into], tab_sems.at[4 * slot + i]))
+        for i, (table, scratch) in enumerate(((high, tab_high), (low, tab_low))):
+            loads.append(pltpu.make_async_copy(table.at[rows, cols], scratch.at[:, into], tab_sems.at[4 * slot + i]))
+        for i, (table, scratch) in enumerate(((end_high, tab_end_high), (end_low, tab_end_low))):
+            copy = pltpu.make_async_copy(table.at[end_rows, cols], scratch.at[:, into], tab_sems.at[4 * slot + 2 + i])
+            end_loads.append(copy)
     for load in loads:
         load.start()
+
+    @pl.when(at_end)
+    def _():
+        for load in end_loads:
+            load.start()
 
     def fetch(source, p, slot):
         into = gathered.at[:, :, p, :, pl.ds(slot * lanes, lanes)]
@@ -291,41 +344,44 @@
         for slot in range(4):
             fetch(bands[p][0], p, slot).wait()
     shots, count, _ = keep.shape
+    total = 2 * shots * count
+    value = gathered[...].reshape(total, 4 * lanes)
+    rolled = [pltpu.roll(value[:, i * lanes : (i + 1) * lanes], lanes // 2, 1) for i in range(4)]
+    answer = value * same_side[...] + jnp.concatenate(rolled, axis=1) * cross_side[...]
 
     def transform(value, into_high, into_low):
         left_high, left_low = split_two(value)
         full = dot_nt(left_high, into_high[...]) + dot_nt(left_low, into_high[...]) + dot_nt(left_high, into_low[...])
         return full * (2.0 / NT)
 
-    for s in range(2 * shots):
-        value = gathered[s].reshape(count, 4 * lanes)
-        rolled = [pltpu.roll(value[:, i * lanes : (i + 1) * lanes], lanes // 2, 1) for i in range(4)]
-        turned = jnp.concatenate(rolled, axis=1)
-        some = slice(s * count, (s + 1) * count)
-        answer = value * same_side[some, :] + turned * cross_side[some, :]
-        target, at = (keep, s) if s < shots else (send, s - shots)
-        target[at] = transform(answer, tab_high, tab_low)
-
-        @pl.when((z == 0) | (z == 3))
-        def _(value=value, some=some, target=target, at=at):
-            ends = transform(value, end_high, end_low)
-            lane = lax.broadcasted_iota(jnp.int32, (count, lanes), 1)
-            moved = pltpu.roll(taps[some, :], jnp.where(z == 0, lanes - 2 * RIM + 1, lanes - RIM + 1), 1)
-            total = jnp.zeros((count, lanes), jnp.float32)
-            for k in range(RIM):
-                total = total + ends[:, k : k + 1] * moved
-                moved = pltpu.roll(moved, 1, 1)
-            cols = pl.ds(pl.multiple_of(jnp.where(z == 0, 0, quarter - lanes), lanes), lanes)
-            touched = (lane < RIM) == (z == 0)
-            touched = touched & ((lane < RIM) | (lane >= lanes - RIM))
-            target[at, :, cols] = target[at, :, cols] - jnp.where(touched, total, 0.0)
-
-
-def unpack_kernel(most, slots, out):
-    devices = slots.shape[0]
-    for b in range(out.shape[0]):
-        for d in range(devices):
-            out[b, d * most : (d + 1) * most, :] = slots[d, b * most : (b + 1) * most, :]
+    result = transform(answer, tab_high, tab_low).reshape(2 * shots, count, quarter)
+    keep[...] = result[:shots]
+    send[...] = result[shots:]
+
+    @pl.when(at_end)
+    def _():
+        for load in end_loads:
+            load.wait()
+        beyond = transform(gathered[...].reshape(total, 4 * lanes), tab_end_high, tab_end_low) * taps[...]
+        beyond_high, beyond_low = split_two(beyond)
+        wrapped = dot_nn(beyond_high, end_sums[...]) + dot_nn(beyond_low, end_sums[...])
+        wrapped = wrapped.reshape(2 * shots, count, lanes)
+        cols = pl.ds(pl.multiple_of(jnp.where(z == 0, 0, quarter - lanes), lanes), lanes)
+        keep[:, :, cols] = keep[:, :, cols] - wrapped[:shots]
+        send[:, :, cols] = send[:, :, cols] - wrapped[shots:]
+
+
+def unpack_kernel(most, *rest):
+    slots, out = rest[:-1], rest[-1]
+    d = lax.axis_index("shot")
+    chip, core = d // 2, d % 2
+    for q in range(len(slots) // 2):
+        own, other = slots[2 * q][...], slots[2 * q + 1][...]
+        first, second = jnp.where(core == 0, own, other), jnp.where(core == 0, other, own)
+        rows = pl.ds(pl.multiple_of((chip ^ q) * (2 * most), 8), 2 * most)
+        for b in range(out.shape[0]):
+            some = slice(b * most, (b + 1) * most)
+            out[b, rows, :] = jnp.concatenate([first[some], second[some]], axis=0)
 
 
 def f32(*shape):
@@ -356,7 +412,7 @@
     half = receivers // 2
     chunk = receivers // devices
     size = chunk // PARTS
-    core = lax.axis_index("shot") % 2
+    core = lax.axis_index("shot") & 1
     high, low = (jnp.asarray(x) for x in wave_constant(lax.axis_size("freq")))
     dma = pltpu.SemaphoreType.DMA
 
@@ -365,10 +421,11 @@
     )(surface)
     sibling = swap(to_sibling, "shot", devices, 1)
 
+    bins = offset_bin.reshape(shots, receivers)
     bands = kernel_call(
         spectra_kernel,
-        [f32(shots * points, lanes)] * 4,
-        [SMEM, SMEM, VMEM, ANY, ANY],
+        [f32(shots * points + 8, lanes)] * 4,
+        [SMEM, SMEM, VMEM, VMEM, VMEM, ANY, ANY],
         [VMEM] * 4,
         [
             pltpu.VMEM((shots * points, quarter), jnp.float32),
@@ -379,27 +436,37 @@
         ],
         moved=1 << 21,
         vmem=16 << 20,
-    )(point_column, live_mask, traces, high, low)
+    )(point_column, live_mask, traces, bins, filters, high, low)
+    def scatter(step):
+        pieces = kernel_call(
+            functools.partial(pieces_kernel, step),
+            [f32(POINTS_BLK, chunk, lanes)] * 3,
+            [SMEM, VMEM, VMEM],
+            [VMEM] * 3,
+            [],
+            moved=4 << 20,
+            vmem=24 << 20,
+        )(block_owner, surface, sibling)
+        return [swap(piece, "shot", devices, 2 * (k + 1)) for k, piece in enumerate(pieces)]
+
+    def choose(*sent):
+        return kernel_call(
+            functools.partial(choose_kernel, len(sent) > 3),
+            f32(STEPS, POINTS_BLK, chunk, lanes),
+            [SMEM] + [ANY] * (2 + len(sent)),
+            VMEM,
+            [dma((STEPS,))],
+            moved=1 << 20,
+            vmem=8 << 20,
+        )(block_owner, surface, sibling, *sent)
+
+    sent = scatter(0)
+
     spectra = bands[0]
     for k in range(1, 4):
         spectra = spectra + swap(bands[k], "freq", 4, k)
-
-    pieces = kernel_call(
-        pieces_kernel,
-        [f32(2, POINTS_BLK, size, lanes)] * (3 * PARTS),
-        [VMEM, VMEM],
-        [VMEM] * (3 * PARTS),
-        [],
-        moved=5 << 20,
-        vmem=24 << 20,
-    )(surface, sibling)
-    sent = [swap(piece, "shot", devices, 2 * (1 + k // PARTS)) for k, piece in enumerate(pieces)]
-
-    own_filters = jnp.pad(filters, ((0, 8 - filters.shape[0]), (0, lanes - filters.shape[1])))
-    shared = jnp.concatenate([spectra, own_filters], axis=0)
-    paired = swap(shared, "shot", devices, 1)
-    paired = jnp.where(core == 0, jnp.stack([shared, paired]), jnp.stack([paired, shared]))
-    every = [paired] + [swap(paired, "shot", devices, 2 * q) for q in (1, 2, 3)]
+    every = jnp.stack([spectra] + [swap(spectra, "shot", devices, 2 * q) for q in (1, 2, 3)])
+    every = [every, swap(every, "shot", devices, 1)]
 
     places = kernel_call(
         functools.partial(slots_kernel, most),
@@ -412,39 +479,37 @@
         vmem=24 << 20,
     )(offset_bin.reshape(1, rows), live_mask.reshape(1, rows))
 
-    bins = offset_bin.reshape(shots, receivers)
-    bins_here = lax.dynamic_slice_in_dim(bins, core * half, half, axis=1)
-    bins_there = lax.dynamic_slice_in_dim(bins, (1 - core) * half, half, axis=1)
-    bins_both = jnp.concatenate([bins_here, swap(bins_there, "shot", devices, 1)]).reshape(1, rows)
     waves = jnp.asarray(tap_constant(lax.axis_size("freq"), lanes))
+    end_high, end_low, picks, sums = (jnp.asarray(x) for x in end_constants(lax.axis_size("freq"), lanes))
     taps, same_side, cross_side = kernel_call(
         functools.partial(response_kernel, filters.shape[0]),
-        [f32(rows, lanes), f32(rows, 4 * lanes), f32(rows, 4 * lanes)],
-        [VMEM] * 6,
+        [f32(rows, RIM * RIM), f32(rows, 4 * lanes), f32(rows, 4 * lanes)],
+        [VMEM] * 5,
         [VMEM] * 3,
         [pltpu.VMEM((devices, 8, lanes), jnp.float32)],
         flops=rows * 64 * 4 * 1152,
         moved=1 << 22,
         vmem=24 << 20,
-    )(bins_both, waves, *every)
+    )(bins, waves, picks, *every)
+
+    both = (block_owner[0] ^ block_owner[1]) == 1
+    sent, every = lax.optimization_barrier((sent, every))
+    chosen = lax.cond(both, lambda *sent: choose(*sent, *scatter(1)), choose, *sent)
 
     gathered = []
     for part in range(PARTS):
         outs = kernel_call(
             functools.partial(prediction_kernel, part),
             [f32(2 * shots, size, lanes)] * 4,
-            [SMEM, ANY, ANY, ANY, ANY, ANY] + [VMEM] * 4,
+            [VMEM] * 3,
             [VMEM] * 4,
-            [
-                pltpu.VMEM((STEPS, POINTS_BLK, size, lanes), jnp.float32),
-                pltpu.VMEM((8, shots * points, lanes), jnp.float32),
-                pltpu.VMEM((8, shots * points, lanes), jnp.float32),
-                dma((STEPS,)),
-            ],
+            [pltpu.VMEM((8, shots * points, lanes), jnp.float32)] * 2,
             flops=devices * shots * size * points * lanes * 4,
             moved=1 << 20,
             vmem=16 << 20,
-        )(block_owner, surface, sibling, *sent[part::PARTS], *every)
+        )(chosen, *every)
+        if gathered:
+            outs, gathered[0] = lax.optimization_barrier((outs, gathered[0]))
         turned = [outs[0]] + [swap(outs[q], "shot", devices, 2 * q) for q in (1, 2, 3)]
         own = kernel_call(
             arrange_kernel,
@@ -464,45 +529,45 @@
     keep, send = kernel_call(
         inverse_kernel,
         [f32(shots, half, quarter)] * 2,
-        [ANY, ANY, VMEM, VMEM, VMEM] + [ANY] * (5 * PARTS),
+        [ANY] * 5 + [VMEM] * 3 + [ANY] * (5 * PARTS),
         [VMEM] * 2,
         [
             pltpu.VMEM((2 * shots, 4, PARTS, size, 4 * lanes), jnp.float32),
             pltpu.VMEM((quarter, 4 * lanes), jnp.bfloat16),
             pltpu.VMEM((quarter, 4 * lanes), jnp.bfloat16),
-            pltpu.VMEM((RIM, 4 * lanes), jnp.bfloat16),
-            pltpu.VMEM((RIM, 4 * lanes), jnp.bfloat16),
+            pltpu.VMEM((RIM * RIM, 4 * lanes), jnp.bfloat16),
+            pltpu.VMEM((RIM * RIM, 4 * lanes), jnp.bfloat16),
+            pltpu.VMEM((RIM * RIM, lanes), jnp.bfloat16),
             dma((4 * PARTS,)),
-            dma((16,)),
+            dma((17,)),
         ],
         flops=6 * rows * 4 * lanes * quarter,
         moved=4 << 20,
         vmem=32 << 20,
-    )(high, low, taps, same_side, cross_side, *gathered)
+    )(high, low, end_high, end_low, sums, taps, same_side, cross_side, *gathered)
     got = swap(send, "shot", devices, 1)
 
-    packed = kernel_call(
+    bin_slots = filters.shape[0] * most
+    slots = kernel_call(
         clean_kernel,
-        f32(bins_total * most, quarter),
+        [f32(bin_slots, quarter)] * devices,
         [VMEM] * 4,
-        VMEM,
-        [pltpu.VMEM((rows, quarter), jnp.bfloat16)] * 2,
+        [VMEM] * devices,
+        [pltpu.VMEM((rows, quarter), jnp.bfloat16)] * 2 + [pltpu.VMEM((devices * bin_slots, quarter), jnp.float32)],
         flops=4 * rows * bins_total * most * quarter,
         moved=6 << 20,
         vmem=32 << 20,
     )(keep, got, traces, places)
-
-    slots = packed.reshape(devices, filters.shape[0] * most, quarter)
-    slots = lax.all_to_all(slots, "shot", split_axis=0, concat_axis=0, tiled=True)
+    slots = [slots[0]] + [swap(slots[k], "shot", devices, k) for k in range(1, devices)]
     return kernel_call(
         functools.partial(unpack_kernel, most),
         f32(filters.shape[0], devices * most, quarter),
-        [VMEM],
+        [VMEM] * devices,
         VMEM,
         [],
         moved=3 << 20,
         vmem=16 << 20,
-    )(slots)
+    )(*slots)
 
 
 def with_halo(cells, sides, width):

time: 124 us -> 97.5 us (0.79)
  blocking collectives: 19.3 us -> 0 us
  waiting for transfers between devices: 33.8 us -> 47 us
  starting transfers between devices: 42.3 us -> 30.5 us
  Pallas kernels: 22.3 us -> 17.4 us
  local copies, waits for them, and re-layouts: 5.26 us -> 0.79 us
    all_to_all x1 -> x0, blocking collectives: 19.3 us -> none  [plane_device(): lax.all_to_all(slots, 'shot', split_axis=0, concat_axis=0, tiled=True)]
    ppermute x24 -> x23, waiting for transfers between devices: 25.8 us -> 40.2 us  [swap(): return lax.ppermute(value, axis, [(i, i ^ bit) for i in range(count)])]
    unnamed x36 -> x30, local copies, waits for them, and re-layouts: 5.26 us -> 0.2 us
    ppermute x24 -> x23, starting transfers between devices: 29.7 us -> 24.7 us  [swap(): return lax.ppermute(value, axis, [(i, i ^ bit) for i in range(count)])]
    pallas_call x4 -> x5, Pallas kernels: 12.5 us -> 7.86 us  [the longest x1 3.33 us: plane_device(): kernel_call(inverse_kernel, [f32(shots, half, quarter)] * 2, [ANY] * 5 +...]
    ppermute x2 -> x1, starting transfers between devices: 7.4 us -> 3.17 us  [plane_device(): right = lax.ppermute(own, 'freq', [(0, 1), (1, 2), (2, 3)])]
    ppermute x2 -> x1, starting transfers between devices: 2.57 us -> 1.28 us  [plane_device(): forward = lax.ppermute(across, 'freq', [(2, 3), (1, 0)])]
    ppermute x2 -> x1, starting transfers between devices: 2.57 us -> 1.29 us  [plane_device(): left = lax.ppermute(own, 'freq', [(1, 0), (2, 1), (3, 2)])]
  transfers between devices with their start and end apart: 30 -> 26, of which waited for: 10 -> 14; matrix products, arithmetic and copies ran while one was open for 0% -> 1% of each run, Pallas kernels for 7% -> 5%
where the time goes in v2:
time: 97.5 us; the launch traced here: 97.3 us
  waiting for transfers between devices  47 us (48%)
  starting transfers between devices  30.5 us (31%)
  Pallas kernels  17.4 us (18%)
  between operations  1.61 us (2%)
    ppermute x23, waiting for transfers between devices, swap(): return lax.ppermute(value, axis, [(i, i ^ bit) for i in range(count)])  40.2 us
    ppermute x23, starting transfers between devices, swap(): return lax.ppermute(value, axis, [(i, i ^ bit) for i in range(count)])  24.7 us
    ppermute x1, waiting for transfers between devices, plane_device(): forward = lax.ppermute(across, 'freq', [(2, 3), (1, 0)])  6.78 us
    pallas_call x1, Pallas kernels, plane_device(): kernel_call(functools.partial(prediction_kernel, part), [f32(2 * shots, s...  3.67 us
    pallas_call x1, Pallas kernels, plane_device(): kernel_call(inverse_kernel, [f32(shots, half, quarter)] * 2, [ANY] * 5 +...  3.33 us
    ppermute x1, starting transfers between devices, plane_device(): right = lax.ppermute(own, 'freq', [(0, 1), (1, 2), (2, 3)])  3.17 us
    pallas_call x1, Pallas kernels, plane_device(): kernel_call(functools.partial(response_kernel, filters.shape[0]), [f32(ro...  2.25 us
  transfers between devices with their start and end apart: 26, of which 14 were waited for; matrix products, arithmetic and copies ran while one was open for 1% of the time, Pallas kernels for 5%

profile of v2, /device:TPU:0, one launch (start us, length us, event | category | flops | bytes accessed | tf_op | source)
XLA Modules:
  0.0 97.3 jit_solution(15679923502589734063)
XLA Ops:
  3.3 3.1 %collective-permute-start.3 = (f32[104,128]{1,0:T(8,128)S(1)}, f32[104,128]{1,0:T(8,128)S(1)}, u32[]{:S(2)}, u32[]{:S(2)}) collective-permute-start(f32[104,128]{1,0:T(8,128)S(1)} %get-tuple-element.77), channel_id=1, source_target_pairs={{0,1},{1,0},{2,3},{3,2},{4,5},{5,4},{6,7},{7,6},{8,9},{9,8},{10,11... | collective-permute-start | bytes 159752 | tf_op jit(solution)/shard_map/ppermute | solution.py:81
  6.4 2.6 %collective-permute-start.4 = (f32[104,128]{1,0:T(8,128)S(1)}, f32[104,128]{1,0:T(8,128)S(1)}, u32[]{:S(2)}, u32[]{:S(2)}) collective-permute-start(f32[104,128]{1,0:T(8,128)S(1)} %get-tuple-element.78), channel_id=1, source_target_pairs={{0,2},{1,3},{2,0},{3,1},{4,6},{5,7},{6,4},{7,5},{8,10},{9,11},{10,... | collective-permute-start | bytes 159752 | tf_op jit(solution)/shard_map/ppermute | solution.py:81
  9.0 3.6 %collective-permute-done.4 = f32[104,128]{1,0:T(8,128)S(1)} collective-permute-done((f32[104,128]{1,0:T(8,128)S(1)}, f32[104,128]{1,0:T(8,128)S(1)}, u32[]{:S(2)}, u32[]{:S(2)}) %collective-permute-start.4) | collective-permute-done | bytes 53280 | tf_op jit(solution)/shard_map/ppermute | solution.py:81
  12.6 2.4 %collective-permute-done.5 = f32[104,128]{1,0:T(8,128)S(1)} collective-permute-done((f32[104,128]{1,0:T(8,128)S(1)}, f32[104,128]{1,0:T(8,128)S(1)}, u32[]{:S(2)}, u32[]{:S(2)}) %collective-permute-start.5) | collective-permute-done | bytes 53280 | tf_op jit(solution)/shard_map/ppermute | solution.py:81
  15.0 1.6 %collective-permute-start.6 = (f32[104,128]{1,0:T(8,128)S(1)}, f32[104,128]{1,0:T(8,128)S(1)}, u32[]{:S(2)}, u32[]{:S(2)}) collective-permute-start(f32[104,128]{1,0:T(8,128)S(1)} %add_add_fusion), channel_id=1, source_target_pairs={{0,8},{4,12},{8,0},{12,4},{16,24},{20,28},{24,16},{28,20},{1,9},{5... | collective-permute-start | bytes 159752 | tf_op jit(solution)/shard_map/ppermute | solution.py:81
  16.5 1.5 %collective-permute-start.7 = (f32[104,128]{1,0:T(8,128)S(1)}, f32[104,128]{1,0:T(8,128)S(1)}, u32[]{:S(2)}, u32[]{:S(2)}) collective-permute-start(f32[104,128]{1,0:T(8,128)S(1)} %add_add_fusion), channel_id=1, source_target_pairs={{0,16},{4,20},{8,24},{12,28},{16,0},{20,4},{24,8},{28,12},{1,17},{... | collective-permute-start | bytes 159752 | tf_op jit(solution)/shard_map/ppermute | solution.py:81
  19.1 1.6 %collective-permute-start.11 = (f32[16,32,128]{2,1,0:T(8,128)S(1)}, f32[16,32,128]{2,1,0:T(8,128)S(1)}, u32[]{:S(2)}, u32[]{:S(2)}) collective-permute-start(f32[16,32,128]{2,1,0:T(8,128)S(1)} %get-tuple-element.83), channel_id=1, source_target_pairs={{0,8},{4,12},{8,0},{12,4},{16,24},{20,28},{24,16},{28,20},{1,9},{5... | collective-permute-start | bytes 786440 | tf_op jit(solution)/shard_map/ppermute | solution.py:81
  20.7 1.5 %collective-permute-start.12 = (f32[16,32,128]{2,1,0:T(8,128)S(1)}, f32[16,32,128]{2,1,0:T(8,128)S(1)}, u32[]{:S(2)}, u32[]{:S(2)}) collective-permute-start(f32[16,32,128]{2,1,0:T(8,128)S(1)} %get-tuple-element.84), channel_id=1, source_target_pairs={{0,16},{4,20},{8,24},{12,28},{16,0},{20,4},{24,8},{28,12},{1,17},{... | collective-permute-start | bytes 786440 | tf_op jit(solution)/shard_map/ppermute | solution.py:81
  25.7 2.7 %collective-permute-done.11 = f32[16,32,128]{2,1,0:T(8,128)S(1)} collective-permute-done((f32[16,32,128]{2,1,0:T(8,128)S(1)}, f32[16,32,128]{2,1,0:T(8,128)S(1)}, u32[]{:S(2)}, u32[]{:S(2)}) %collective-permute-start.11) | collective-permute-done | bytes 262176 | tf_op jit(solution)/shard_map/ppermute | solution.py:81
  28.5 4.1 %collective-permute-done.12 = f32[16,32,128]{2,1,0:T(8,128)S(1)} collective-permute-done((f32[16,32,128]{2,1,0:T(8,128)S(1)}, f32[16,32,128]{2,1,0:T(8,128)S(1)}, u32[]{:S(2)}, u32[]{:S(2)}) %collective-permute-start.12) | collective-permute-done | bytes 262176 | tf_op jit(solution)/shard_map/ppermute | solution.py:81
  32.5 1.5 %conditional.1 = (f32[2,16,32,128]{3,2,1,0:T(8,128)}) conditional(s32[]{:T(128)} %bitcast.4, (s32[2]{0:T(128)S(1)}, f32[16,256,128]{2,1,0:T(8,128)S(1)}, f32[16,128,128]{2,1,0:T(8,128)S(1)}, f32[16,32,128]{2,1,0:T(8,128)S(1)}, f32[16,32,128]{2,1,0:T(8,128)S(1)}, /*index=5*/f32[16,32,128]{2,1,0:T(8,128)S(1)}) %tuple.19, (s32[2]{0:T(128)S(1)}, ...), branch_computations={%region_0.0_spmd, %region_1.0_spmd} | conditional | bytes 14680360 | solution.py:497
  32.5 1.5 %choose_kernel.2 = f32[2,16,32,128]{3,2,1,0:T(8,128)} custom-call(s32[2]{0:T(128)S(1)} %get-tuple-element.32.owners, f32[16,256,128]{2,1,0:T(8,128)S(1)} %get-tuple-element.33.surface, f32[16,128,128]{2,1,0:T(8,128)S(1)} %get-tuple-element.34.sibling, f32[16,32,128]{2,1,0:T(8,128)S(1)} %get-tuple-element.35.rest_0_, ...), custom_call_target="tpu_custom_call" | custom-call | bytes 1048576 | tf_op jit(solution)/shard_map/cond/branch_0_fun/choose_kernel/pallas_call | solution.py:453
  34.1 3.7 %prediction_kernel.1 = (f32[6,32,128]{2,1,0:T(8,128)S(1)}, f32[6,32,128]{2,1,0:T(8,128)S(1)}, f32[6,32,128]{2,1,0:T(8,128)S(1)}, f32[6,32,128]{2,1,0:T(8,128)S(1)}) custom-call(f32[2,16,32,128]{3,2,1,0:T(8,128)} %get-tuple-element.107.chosen, f32[4,104,128]{2,1,0:T(8,128)S(1)} %pad_maximum_fusion.rest_0_, f32[4,104,128]{2,1,0:T(8,128)S(1)} %collective-permute-done.9.rest_1_), custom_call_target="tpu_custom_call" | custom-call | flops 12582912 | bytes 1048576 | tf_op jit(solution)/shard_map/prediction_kernel/pallas_call | solution.py:501
  39.8 1.5 %collective-permute-start.16 = (f32[6,32,128]{2,1,0:T(8,128)S(1)}, f32[6,32,128]{2,1,0:T(8,128)S(1)}, u32[]{:S(2)}, u32[]{:S(2)}) collective-permute-start(f32[6,32,128]{2,1,0:T(8,128)S(1)} %get-tuple-element.94), channel_id=1, source_target_pairs={{0,24},{4,28},{8,16},{12,20},{16,8},{20,12},{24,0},{28,4},{1,25},{... | collective-permute-start | bytes 294920 | tf_op jit(solution)/shard_map/ppermute | solution.py:81
  43.5 1.8 %collective-permute-done.16.third = f32[6,32,128]{2,1,0:T(8,128)S(1)} collective-permute-done((f32[6,32,128]{2,1,0:T(8,128)S(1)}, f32[6,32,128]{2,1,0:T(8,128)S(1)}, u32[]{:S(2)}, u32[]{:S(2)}) %collective-permute-start.16) | collective-permute-done | bytes 98336 | tf_op jit(solution)/shard_map/ppermute | solution.py:81
  45.9 3.2 %collective-permute-start.17 = (f32[6,4,32,128]{3,2,1,0:T(8,128)S(1)}, f32[6,4,32,128]{3,2,1,0:T(8,128)S(1)}, u32[]{:S(2)}, u32[]{:S(2)}) collective-permute-start(f32[6,4,32,128]{3,2,1,0:T(8,128)S(1)} %arrange_kernel.1.rest_0_), channel_id=1, source_target_pairs={{0,1},{1,2},{2,3},{4,5},{5,6},{6,7},{8,9},{9,10},{10,11},{12,13},{... | collective-permute-start | bytes 1179656 | tf_op jit(solution)/shard_map/ppermute | solution.py:523
  50.3 11.9 %collective-permute-done.19.rest_3_ = f32[6,4,32,128]{3,2,1,0:T(8,128)S(1)} collective-permute-done((f32[6,4,32,128]{3,2,1,0:T(8,128)S(1)}, f32[6,4,32,128]{3,2,1,0:T(8,128)S(1)}, u32[]{:S(2)}, u32[]{:S(2)}) %collective-permute-start.19) | collective-permute-done | bytes 393248 | tf_op jit(solution)/shard_map/ppermute | solution.py:81
  63.5 2.3 %response_kernel.1 = (f32[768,256]{1,0:T(8,128)S(1)}, f32[768,512]{1,0:T(8,128)S(1)}, f32[768,512]{1,0:T(8,128)S(1)}) custom-call(s32[3,256]{1,0:T(4,128)S(1)} %bitcast.13, f32[128,512]{1,0:T(8,128)S(1)} %copy-done.5, f32[2,128,256]{2,1,0:T(8,128)S(1)} %copy-done.6, f32[4,104,128]{2,1,0:T(8,128)S(1)} %pad_maximum_fusion.rest_0_, ...), custom_call_target="tpu_custom_call" | custom-call | flops 226492416 | bytes 4194304 | tf_op jit(solution)/shard_map/response_kernel/pallas_call | solution.py:484
  65.8 6.8 %collective-permute-done.20.rest_4_ = f32[6,4,32,128]{3,2,1,0:T(8,128)S(1)} collective-permute-done((f32[6,4,32,128]{3,2,1,0:T(8,128)S(1)}, f32[6,4,32,128]{3,2,1,0:T(8,128)S(1)}, u32[]{:S(2)}, u32[]{:S(2)}) %collective-permute-start.20) | collective-permute-done | bytes 393248 | tf_op jit(solution)/shard_map/ppermute | solution.py:526
  72.6 3.3 %inverse_kernel.1 = (f32[3,128,256]{2,1,0:T(8,128)S(1)}, f32[3,128,256]{2,1,0:T(8,128)S(1)}) custom-call(bf16[1056,512]{1,0:T(8,128)(2,1)S(1)} %copy-done, bf16[1056,512]{1,0:T(8,128)(2,1)S(1)} %copy-done.1, bf16[512,512]{1,0:T(8,128)(2,1)S(1)} %copy-done.3, bf16[512,512]{1,0:T(8,128)(2,1)S(1)} %copy-done.4, bf16[512,128]{1,0:T(8,128)(2,1)S(1)} %copy-done.7, ...), custom_call_target="tpu_custom_call" | custom-call | flops 603979776 | bytes 4194304 | tf_op jit(solution)/shard_map/inverse_kernel/pallas_call | solution.py:529
  79.2 1.5 %collective-permute-start.23 = (f32[144,256]{1,0:T(8,128)S(1)}, f32[144,256]{1,0:T(8,128)S(1)}, u32[]{:S(2)}, u32[]{:S(2)}) collective-permute-start(f32[144,256]{1,0:T(8,128)S(1)} %get-tuple-element.99), channel_id=1, source_target_pairs={{0,8},{4,12},{8,0},{12,4},{16,24},{20,28},{24,16},{28,20},{1,9},{5... | collective-permute-start | bytes 442376 | tf_op jit(solution)/shard_map/ppermute | solution.py:81
  80.9 1.6 %collective-permute-start.25 = (f32[144,256]{1,0:T(8,128)S(1)}, f32[144,256]{1,0:T(8,128)S(1)}, u32[]{:S(2)}, u32[]{:S(2)}) collective-permute-start(f32[144,256]{1,0:T(8,128)S(1)} %get-tuple-element.101), channel_id=1, source_target_pairs={{0,16},{4,20},{8,24},{12,28},{16,0},{20,4},{24,8},{28,12},{1,17},{... | collective-permute-start | bytes 442376 | tf_op jit(solution)/shard_map/ppermute | solution.py:81
  82.7 2.4 %collective-permute-start.27 = (f32[144,256]{1,0:T(8,128)S(1)}, f32[144,256]{1,0:T(8,128)S(1)}, u32[]{:S(2)}, u32[]{:S(2)}) collective-permute-start(f32[144,256]{1,0:T(8,128)S(1)} %get-tuple-element.103), channel_id=1, source_target_pairs={{0,24},{4,28},{8,16},{12,20},{16,8},{20,12},{24,0},{28,4},{1,25},{... | collective-permute-start | bytes 442376 | tf_op jit(solution)/shard_map/ppermute | solution.py:81
  88.1 8.1 %collective-permute-done.26.rest_5_ = f32[144,256]{1,0:T(8,128)S(1)} collective-permute-done((f32[144,256]{1,0:T(8,128)S(1)}, f32[144,256]{1,0:T(8,128)S(1)}, u32[]{:S(2)}, u32[]{:S(2)}) %collective-permute-start.26) | collective-permute-done | bytes 147488 | tf_op jit(solution)/shard_map/ppermute | solution.py:81
  (73 shorter events, 21.6 us)
Async XLA Ops:
  1.4 17.1 %collective-permute-start.10 = (f32[16,128,128]{2,1,0:T(8,128)S(1)}, f32[16,128,128]{2,1,0:T(8,128)S(1)}, u32[]{:S(2)}, u32[]{:S(2)}) collective-permute-start(f32[16,128,128]{2,1,0:T(8,128)S(1)} %sibling_kernel.1), channel_id=1, source_target_pairs={{0,4},{4,0},{8,12},{12,8},{16,20},{20,16},{24,28},{28,24},{1,5},{5... | collective-permute-start | bytes 3145736 | tf_op jit(solution)/shard_map/ppermute | solution.py:81
  3.3 5.7 %collective-permute-start.3 = (f32[104,128]{1,0:T(8,128)S(1)}, f32[104,128]{1,0:T(8,128)S(1)}, u32[]{:S(2)}, u32[]{:S(2)}) collective-permute-start(f32[104,128]{1,0:T(8,128)S(1)} %get-tuple-element.77), channel_id=1, source_target_pairs={{0,1},{1,0},{2,3},{3,2},{4,5},{5,4},{6,7},{7,6},{8,9},{9,8},{10,11... | collective-permute-start | bytes 159752 | tf_op jit(solution)/shard_map/ppermute | solution.py:81
  6.4 6.2 %collective-permute-start.4 = (f32[104,128]{1,0:T(8,128)S(1)}, f32[104,128]{1,0:T(8,128)S(1)}, u32[]{:S(2)}, u32[]{:S(2)}) collective-permute-start(f32[104,128]{1,0:T(8,128)S(1)} %get-tuple-element.78), channel_id=1, source_target_pairs={{0,2},{1,3},{2,0},{3,1},{4,6},{5,7},{6,4},{7,5},{8,10},{9,11},{10,... | collective-permute-start | bytes 159752 | tf_op jit(solution)/shard_map/ppermute | solution.py:81
  9.0 5.9 %collective-permute-start.5 = (f32[104,128]{1,0:T(8,128)S(1)}, f32[104,128]{1,0:T(8,128)S(1)}, u32[]{:S(2)}, u32[]{:S(2)}) collective-permute-start(f32[104,128]{1,0:T(8,128)S(1)} %get-tuple-element.79), channel_id=1, source_target_pairs={{0,3},{1,2},{2,1},{3,0},{4,7},{5,6},{6,5},{7,4},{8,11},{9,10},{10,... | collective-permute-start | bytes 159752 | tf_op jit(solution)/shard_map/ppermute | solution.py:81
  15.0 7.3 %collective-permute-start.6 = (f32[104,128]{1,0:T(8,128)S(1)}, f32[104,128]{1,0:T(8,128)S(1)}, u32[]{:S(2)}, u32[]{:S(2)}) collective-permute-start(f32[104,128]{1,0:T(8,128)S(1)} %add_add_fusion), channel_id=1, source_target_pairs={{0,8},{4,12},{8,0},{12,4},{16,24},{20,28},{24,16},{28,20},{1,9},{5... | collective-permute-start | bytes 159752 | tf_op jit(solution)/shard_map/ppermute | solution.py:81
  16.5 6.2 %collective-permute-start.7 = (f32[104,128]{1,0:T(8,128)S(1)}, f32[104,128]{1,0:T(8,128)S(1)}, u32[]{:S(2)}, u32[]{:S(2)}) collective-permute-start(f32[104,128]{1,0:T(8,128)S(1)} %add_add_fusion), channel_id=1, source_target_pairs={{0,16},{4,20},{8,24},{12,28},{16,0},{20,4},{24,8},{28,12},{1,17},{... | collective-permute-start | bytes 159752 | tf_op jit(solution)/shard_map/ppermute | solution.py:81
  18.0 5.7 %collective-permute-start.8 = (f32[104,128]{1,0:T(8,128)S(1)}, f32[104,128]{1,0:T(8,128)S(1)}, u32[]{:S(2)}, u32[]{:S(2)}) collective-permute-start(f32[104,128]{1,0:T(8,128)S(1)} %add_add_fusion), channel_id=1, source_target_pairs={{0,24},{4,28},{8,16},{12,20},{16,8},{20,12},{24,0},{28,4},{1,25},{... | collective-permute-start | bytes 159752 | tf_op jit(solution)/shard_map/ppermute | solution.py:81
  19.1 9.3 %collective-permute-start.11 = (f32[16,32,128]{2,1,0:T(8,128)S(1)}, f32[16,32,128]{2,1,0:T(8,128)S(1)}, u32[]{:S(2)}, u32[]{:S(2)}) collective-permute-start(f32[16,32,128]{2,1,0:T(8,128)S(1)} %get-tuple-element.83), channel_id=1, source_target_pairs={{0,8},{4,12},{8,0},{12,4},{16,24},{20,28},{24,16},{28,20},{1,9},{5... | collective-permute-start | bytes 786440 | tf_op jit(solution)/shard_map/ppermute | solution.py:81
  20.7 11.8 %collective-permute-start.12 = (f32[16,32,128]{2,1,0:T(8,128)S(1)}, f32[16,32,128]{2,1,0:T(8,128)S(1)}, u32[]{:S(2)}, u32[]{:S(2)}) collective-permute-start(f32[16,32,128]{2,1,0:T(8,128)S(1)} %get-tuple-element.84), channel_id=1, source_target_pairs={{0,16},{4,20},{8,24},{12,28},{16,0},{20,4},{24,8},{28,12},{1,17},{... | collective-permute-start | bytes 786440 | tf_op jit(solution)/shard_map/ppermute | solution.py:81
  22.2 10.3 %collective-permute-start.13 = (f32[16,32,128]{2,1,0:T(8,128)S(1)}, f32[16,32,128]{2,1,0:T(8,128)S(1)}, u32[]{:S(2)}, u32[]{:S(2)}) collective-permute-start(f32[16,32,128]{2,1,0:T(8,128)S(1)} %get-tuple-element.85), channel_id=1, source_target_pairs={{0,24},{4,28},{8,16},{12,20},{16,8},{20,12},{24,0},{28,4},{1,25},{... | collective-permute-start | bytes 786440 | tf_op jit(solution)/shard_map/ppermute | solution.py:81
  37.8 4.7 %collective-permute-start.14 = (f32[6,32,128]{2,1,0:T(8,128)S(1)}, f32[6,32,128]{2,1,0:T(8,128)S(1)}, u32[]{:S(2)}, u32[]{:S(2)}) collective-permute-start(f32[6,32,128]{2,1,0:T(8,128)S(1)} %get-tuple-element.92), channel_id=1, source_target_pairs={{0,8},{4,12},{8,0},{12,4},{16,24},{20,28},{24,16},{28,20},{1,9},{5... | collective-permute-start | bytes 294920 | tf_op jit(solution)/shard_map/ppermute | solution.py:81
  38.9 4.6 %collective-permute-start.15 = (f32[6,32,128]{2,1,0:T(8,128)S(1)}, f32[6,32,128]{2,1,0:T(8,128)S(1)}, u32[]{:S(2)}, u32[]{:S(2)}) collective-permute-start(f32[6,32,128]{2,1,0:T(8,128)S(1)} %get-tuple-element.93), channel_id=1, source_target_pairs={{0,16},{4,20},{8,24},{12,28},{16,0},{20,4},{24,8},{28,12},{1,17},{... | collective-permute-start | bytes 294920 | tf_op jit(solution)/shard_map/ppermute | solution.py:81
  39.8 5.5 %collective-permute-start.16 = (f32[6,32,128]{2,1,0:T(8,128)S(1)}, f32[6,32,128]{2,1,0:T(8,128)S(1)}, u32[]{:S(2)}, u32[]{:S(2)}) collective-permute-start(f32[6,32,128]{2,1,0:T(8,128)S(1)} %get-tuple-element.94), channel_id=1, source_target_pairs={{0,24},{4,28},{8,16},{12,20},{16,8},{20,12},{24,0},{28,4},{1,25},{... | collective-permute-start | bytes 294920 | tf_op jit(solution)/shard_map/ppermute | solution.py:81
  45.4 16.8 %collective-permute-start.19 = (f32[6,4,32,128]{3,2,1,0:T(8,128)S(1)}, f32[6,4,32,128]{3,2,1,0:T(8,128)S(1)}, u32[]{:S(2)}, u32[]{:S(2)}) collective-permute-start(f32[6,4,32,128]{3,2,1,0:T(8,128)S(1)} %arrange_kernel.1.rest_0_), channel_id=1, source_target_pairs={{0,2},{1,3},{2,0},{3,1},{4,6},{5,7},{6,4},{7,5},{8,10},{9,11},{10,... | collective-permute-start | bytes 1179656 | tf_op jit(solution)/shard_map/ppermute | solution.py:81
  45.9 19.9 %collective-permute-start.17 = (f32[6,4,32,128]{3,2,1,0:T(8,128)S(1)}, f32[6,4,32,128]{3,2,1,0:T(8,128)S(1)}, u32[]{:S(2)}, u32[]{:S(2)}) collective-permute-start(f32[6,4,32,128]{3,2,1,0:T(8,128)S(1)} %arrange_kernel.1.rest_0_), channel_id=1, source_target_pairs={{0,1},{1,2},{2,3},{4,5},{5,6},{6,7},{8,9},{9,10},{10,11},{12,13},{... | collective-permute-start | bytes 1179656 | tf_op jit(solution)/shard_map/ppermute | solution.py:523
  49.0 16.7 %collective-permute-start.18 = (f32[6,4,32,128]{3,2,1,0:T(8,128)S(1)}, f32[6,4,32,128]{3,2,1,0:T(8,128)S(1)}, u32[]{:S(2)}, u32[]{:S(2)}) collective-permute-start(f32[6,4,32,128]{3,2,1,0:T(8,128)S(1)} %arrange_kernel.1.rest_0_), channel_id=1, source_target_pairs={{1,0},{2,1},{3,2},{5,4},{6,5},{7,6},{9,8},{10,9},{11,10},{13,12},{... | collective-permute-start | bytes 1179656 | tf_op jit(solution)/shard_map/ppermute | solution.py:524
  62.2 10.4 %collective-permute-start.20 = (f32[6,4,32,128]{3,2,1,0:T(8,128)S(1)}, f32[6,4,32,128]{3,2,1,0:T(8,128)S(1)}, u32[]{:S(2)}, u32[]{:S(2)}) collective-permute-start(f32[6,4,32,128]{3,2,1,0:T(8,128)S(1)} %collective-permute-done.19.rest_3_), channel_id=1, source_target_pairs={{2,3},{1,0},{6,7},{5,4},{10,11},{9,8},{14,15},{13,12},{18,19},{17,... | collective-permute-start | bytes 1179656 | tf_op jit(solution)/shard_map/ppermute | solution.py:526
  79.0 3.7 %collective-permute-start.22 = (f32[144,256]{1,0:T(8,128)S(1)}, f32[144,256]{1,0:T(8,128)S(1)}, u32[]{:S(2)}, u32[]{:S(2)}) collective-permute-start(f32[144,256]{1,0:T(8,128)S(1)} %get-tuple-element.98), channel_id=1, source_target_pairs={{0,4},{4,0},{8,12},{12,8},{16,20},{20,16},{24,28},{28,24},{1,5},{5... | collective-permute-start | bytes 442376 | tf_op jit(solution)/shard_map/ppermute | solution.py:81
  79.2 6.7 %collective-permute-start.23 = (f32[144,256]{1,0:T(8,128)S(1)}, f32[144,256]{1,0:T(8,128)S(1)}, u32[]{:S(2)}, u32[]{:S(2)}) collective-permute-start(f32[144,256]{1,0:T(8,128)S(1)} %get-tuple-element.99), channel_id=1, source_target_pairs={{0,8},{4,12},{8,0},{12,4},{16,24},{20,28},{24,16},{28,20},{1,9},{5... | collective-permute-start | bytes 442376 | tf_op jit(solution)/shard_map/ppermute | solution.py:81
  80.7 7.3 %collective-permute-start.24 = (f32[144,256]{1,0:T(8,128)S(1)}, f32[144,256]{1,0:T(8,128)S(1)}, u32[]{:S(2)}, u32[]{:S(2)}) collective-permute-start(f32[144,256]{1,0:T(8,128)S(1)} %get-tuple-element.100), channel_id=1, source_target_pairs={{0,12},{4,8},{8,4},{12,0},{16,28},{20,24},{24,20},{28,16},{1,13},{... | collective-permute-start | bytes 442376 | tf_op jit(solution)/shard_map/ppermute | solution.py:81
  80.9 7.1 %collective-permute-start.25 = (f32[144,256]{1,0:T(8,128)S(1)}, f32[144,256]{1,0:T(8,128)S(1)}, u32[]{:S(2)}, u32[]{:S(2)}) collective-permute-start(f32[144,256]{1,0:T(8,128)S(1)} %get-tuple-element.101), channel_id=1, source_target_pairs={{0,16},{4,20},{8,24},{12,28},{16,0},{20,4},{24,8},{28,12},{1,17},{... | collective-permute-start | bytes 442376 | tf_op jit(solution)/shard_map/ppermute | solution.py:81
  82.5 13.6 %collective-permute-start.26 = (f32[144,256]{1,0:T(8,128)S(1)}, f32[144,256]{1,0:T(8,128)S(1)}, u32[]{:S(2)}, u32[]{:S(2)}) collective-permute-start(f32[144,256]{1,0:T(8,128)S(1)} %get-tuple-element.102), channel_id=1, source_target_pairs={{0,20},{4,16},{8,28},{12,24},{16,4},{20,0},{24,12},{28,8},{1,21},{... | collective-permute-start | bytes 442376 | tf_op jit(solution)/shard_map/ppermute | solution.py:81
  82.7 13.4 %collective-permute-start.27 = (f32[144,256]{1,0:T(8,128)S(1)}, f32[144,256]{1,0:T(8,128)S(1)}, u32[]{:S(2)}, u32[]{:S(2)}) collective-permute-start(f32[144,256]{1,0:T(8,128)S(1)} %get-tuple-element.103), channel_id=1, source_target_pairs={{0,24},{4,28},{8,16},{12,20},{16,8},{20,12},{24,0},{28,4},{1,25},{... | collective-permute-start | bytes 442376 | tf_op jit(solution)/shard_map/ppermute | solution.py:81
  85.9 10.2 %collective-permute-start.28 = (f32[144,256]{1,0:T(8,128)S(1)}, f32[144,256]{1,0:T(8,128)S(1)}, u32[]{:S(2)}, u32[]{:S(2)}) collective-permute-start(f32[144,256]{1,0:T(8,128)S(1)} %get-tuple-element.104), channel_id=1, source_target_pairs={{0,28},{4,24},{8,20},{12,16},{16,12},{20,8},{24,4},{28,0},{1,29},{... | collective-permute-start | bytes 442376 | tf_op jit(solution)/shard_map/ppermute | solution.py:81
  (16 other events, 225.4 us)

commit v3 on v2

--- a/solution.py
+++ b/solution.py
@@ -15,7 +15,6 @@
 POINTS_BLK = 16
 STEPS = 2
 RIM = 16
-PARTS = 1
 
 FULL_PRECISION = lax.Precision.HIGHEST
 VMEM = pl.BlockSpec(memory_space=pltpu.VMEM)
@@ -142,8 +141,38 @@
                 out[...] = source[:, pl.ds(pl.multiple_of(first, 8), chunk), :]
 
 
-def choose_kernel(extra, owners, surface, sibling, *rest):
-    sent, (chosen, sems) = rest[:-2], rest[-2:]
+def predict(chosen, spectra, real_side, imag_side, outs):
+    points = STEPS * POINTS_BLK
+    rows = real_side.shape[1]
+    shots = rows // points
+    size, lanes = chosen.shape[2:]
+    lane = lax.broadcasted_iota(jnp.int32, (rows, lanes), 1)
+    for q in outs:
+        for c in range(2):
+            value = spectra[c][q, :rows, :]
+            turned = pltpu.roll(value, lanes // 2, 1)
+            real_side[2 * q + c] = jnp.where(lane < lanes // 2, value, turned)
+            imag_side[2 * q + c] = jnp.where(lane < lanes // 2, turned, -value)
+    yield
+    for q, out in outs.items():
+
+        @pl.loop(0, 2)
+        def _(rel, q=q, out=out):
+            at = 2 * q + rel
+            first_sum = [jnp.zeros((size, lanes), jnp.float32)] * shots
+            second_sum = [jnp.zeros((size, lanes), jnp.float32)] * shots
+            for j in range(points):
+                block = chosen[j // POINTS_BLK, j % POINTS_BLK]
+                for s in range(shots):
+                    row = s * points + j
+                    first_sum[s] = first_sum[s] + real_side[at, row : row + 1, :] * block
+                    second_sum[s] = second_sum[s] + imag_side[at, row : row + 1, :] * block
+            for s in range(shots):
+                out[rel * shots + s] = first_sum[s] + pltpu.roll(second_sum[s], lanes // 2, 1)
+
+
+def others_kernel(extra, owners, surface, sibling, *rest):
+    sent, spectra, outs, (chosen, real_side, imag_side, sems) = rest[:-9], rest[-9:-7], rest[-7:-4], rest[-4:]
     d = lax.axis_index("shot")
     chip, core = d // 2, d % 2
     half = sibling.shape[1]
@@ -169,40 +198,17 @@
                 source = sent[3 + k] if extra and b == 1 else sent[k]
                 pltpu.make_async_copy(source, chosen.at[b], sems.at[b]).start()
 
+    steps = predict(chosen, spectra, real_side, imag_side, dict(zip((1, 2, 3), outs)))
+    next(steps)
     for b in range(STEPS):
         pltpu.make_async_copy(sibling.at[:, pl.ds(0, chunk)], chosen.at[b], sems.at[b]).wait()
-
-
-def prediction_kernel(part, chosen, *rest):
-    spectra, outs, (real_side, imag_side) = rest[:2], rest[2:6], rest[6:]
-    size = outs[0].shape[1]
-    points = STEPS * POINTS_BLK
-    rows = real_side.shape[1]
-    shots = rows // points
-    lanes = chosen.shape[3]
-    lane = lax.broadcasted_iota(jnp.int32, (rows, lanes), 1)
-    for q in range(4):
-        for c in range(2):
-            value = spectra[c][q, :rows, :]
-            turned = pltpu.roll(value, lanes // 2, 1)
-            real_side[2 * q + c] = jnp.where(lane < lanes // 2, value, turned)
-            imag_side[2 * q + c] = jnp.where(lane < lanes // 2, turned, -value)
-    some = slice(part * size, (part + 1) * size)
-    for q in range(4):
-
-        @pl.loop(0, 2)
-        def _(rel):
-            at = 2 * q + rel
-            first_sum = [jnp.zeros((size, lanes), jnp.float32)] * shots
-            second_sum = [jnp.zeros((size, lanes), jnp.float32)] * shots
-            for j in range(points):
-                block = chosen[j // POINTS_BLK, j % POINTS_BLK, some, :]
-                for s in range(shots):
-                    row = s * points + j
-                    first_sum[s] = first_sum[s] + real_side[at, row : row + 1, :] * block
-                    second_sum[s] = second_sum[s] + imag_side[at, row : row + 1, :] * block
-            for s in range(shots):
-                outs[q][rel * shots + s] = first_sum[s] + pltpu.roll(second_sum[s], lanes // 2, 1)
+    for _ in steps:
+        pass
+
+
+def own_kernel(chosen, own, other, out, real_side, imag_side):
+    for _ in predict(chosen, (own, other), real_side, imag_side, {0: out}):
+        pass
 
 
 def arrange_kernel(own, first, second, third, out):
@@ -284,12 +290,28 @@
         out[...] = packed[pl.ds(pl.multiple_of((d ^ k) * count, 8), count), :]
 
 
+def transform(value, into_high, into_low):
+    left_high, left_low = split_two(value)
+    full = dot_nt(left_high, into_high[...]) + dot_nt(left_low, into_high[...]) + dot_nt(left_high, into_low[...])
+    return full * (2.0 / NT)
+
+
+def respond(value, same_side, cross_side):
+    lanes = 2 * NF // 4
+    bands = [value[:, i : i + lanes] for i in range(0, value.shape[1], lanes)]
+    turned = jnp.concatenate([pltpu.roll(band, lanes // 2, 1) for band in bands], axis=1)
+    return value * same_side + turned * cross_side
+
+
+def wrapped_ends(value, end_high, end_low, end_sums, taps):
+    beyond_high, beyond_low = split_two(transform(value, end_high, end_low) * taps[...])
+    return dot_nn(beyond_high, end_sums[...]) + dot_nn(beyond_low, end_sums[...])
+
+
 def inverse_kernel(high, low, end_high, end_low, sums, taps, same_side, cross_side, *rest):
-    bands = [rest[5 * p : 5 * p + 5] for p in range(PARTS)]
-    keep, send = rest[5 * PARTS : 5 * PARTS + 2]
-    gathered, tab_high, tab_low, tab_end_high, tab_end_low, end_sums, sems, tab_sems = rest[5 * PARTS + 2 :]
+    own, right, left, across, out, gathered, tab_high, tab_low, tab_end_high, tab_end_low, end_sums, sems, tab_sems = rest
     z = lax.axis_index("freq")
-    lanes = bands[0][0].shape[3]
+    lanes = own.shape[3]
     quarter = tab_high.shape[0]
     at_end = (z == 0) | (z == 3)
     rows = pl.ds(pl.multiple_of(RIM + z * quarter, 16), quarter)
@@ -313,62 +335,75 @@
         for load in end_loads:
             load.start()
 
-    def fetch(source, p, slot):
-        into = gathered.at[:, :, p, :, pl.ds(slot * lanes, lanes)]
-        return pltpu.make_async_copy(source, into, sems.at[4 * p + slot])
-
-    for p in range(PARTS):
-        own, right, left, across, forward = bands[p]
-        fetch(own, p, 0).start()
-        fetch(across, p, 3).start()
-
-        @pl.when(z > 0)
-        def _():
-            fetch(right, p, 1).start()
-
-        @pl.when(z == 0)
-        def _():
-            fetch(forward, p, 1).start()
-
-        @pl.when(z < 3)
-        def _():
-            fetch(left, p, 2).start()
-
-        @pl.when(z == 3)
-        def _():
-            fetch(forward, p, 2).start()
+    def fetch(source, slot):
+        return pltpu.make_async_copy(source, gathered.at[:, :, :, pl.ds(slot * lanes, lanes)], sems.at[slot])
+
+    fetch(own, 0).start()
+    fetch(across, 3).start()
+    for slot, source, there in ((1, right, z > 0), (2, left, z < 3)):
+
+        @pl.when(there)
+        def _(slot=slot, source=source):
+            fetch(source, slot).start()
+            fetch(source, slot).wait()
+
+        @pl.when(jnp.logical_not(there))
+        def _(slot=slot):
+            gathered[:, :, :, slot * lanes : (slot + 1) * lanes] = jnp.zeros(own.shape, jnp.float32)
 
     for load in loads:
         load.wait()
-    for p in range(PARTS):
-        for slot in range(4):
-            fetch(bands[p][0], p, slot).wait()
-    shots, count, _ = keep.shape
-    total = 2 * shots * count
+    fetch(own, 0).wait()
+    fetch(across, 3).wait()
+    total = math.prod(own.shape[:3])
     value = gathered[...].reshape(total, 4 * lanes)
-    rolled = [pltpu.roll(value[:, i * lanes : (i + 1) * lanes], lanes // 2, 1) for i in range(4)]
-    answer = value * same_side[...] + jnp.concatenate(rolled, axis=1) * cross_side[...]
-
-    def transform(value, into_high, into_low):
-        left_high, left_low = split_two(value)
-        full = dot_nt(left_high, into_high[...]) + dot_nt(left_low, into_high[...]) + dot_nt(left_high, into_low[...])
-        return full * (2.0 / NT)
-
-    result = transform(answer, tab_high, tab_low).reshape(2 * shots, count, quarter)
-    keep[...] = result[:shots]
-    send[...] = result[shots:]
+    out[...] = transform(respond(value, same_side[...], cross_side[...]), tab_high, tab_low)
 
     @pl.when(at_end)
     def _():
         for load in end_loads:
             load.wait()
-        beyond = transform(gathered[...].reshape(total, 4 * lanes), tab_end_high, tab_end_low) * taps[...]
-        beyond_high, beyond_low = split_two(beyond)
-        wrapped = dot_nn(beyond_high, end_sums[...]) + dot_nn(beyond_low, end_sums[...])
-        wrapped = wrapped.reshape(2 * shots, count, lanes)
+        wrapped = wrapped_ends(gathered[...].reshape(total, 4 * lanes), tab_end_high, tab_end_low, end_sums, taps)
         cols = pl.ds(pl.multiple_of(jnp.where(z == 0, 0, quarter - lanes), lanes), lanes)
-        keep[:, :, cols] = keep[:, :, cols] - wrapped[:shots]
-        send[:, :, cols] = send[:, :, cols] - wrapped[shots:]
+        out[:, cols] = out[:, cols] - wrapped
+
+
+def forward_kernel(high, low, end_high, end_low, sums, taps, same_side, cross_side, partial, forward, *rest):
+    keep, send, tab_high, tab_low, tab_end_high, tab_end_low, end_sums, result, sems = rest
+    z = lax.axis_index("freq")
+    lanes = forward.shape[3]
+    total, quarter = partial.shape
+    at_end = (z == 0) | (z == 3)
+
+    @pl.when(at_end)
+    def _():
+        rows = pl.ds(pl.multiple_of(RIM + z * quarter, 16), quarter)
+        end_size = RIM * RIM
+        end_rows = pl.ds(pl.multiple_of((z + 1) // 4 * end_size, 16), end_size)
+        cols = pl.ds(pl.multiple_of((3 - z) * lanes, lanes), lanes)
+        loads = [
+            pltpu.make_async_copy(high.at[rows, cols], tab_high, sems.at[0]),
+            pltpu.make_async_copy(low.at[rows, cols], tab_low, sems.at[1]),
+            pltpu.make_async_copy(end_high.at[end_rows, cols], tab_end_high, sems.at[2]),
+            pltpu.make_async_copy(end_low.at[end_rows, cols], tab_end_low, sems.at[3]),
+            pltpu.make_async_copy(sums.at[end_rows], end_sums, sems.at[4]),
+        ]
+        run_all(loads)
+        slot = jnp.where(z == 0, 1, 2)
+        some = pl.ds(pl.multiple_of(slot * lanes, lanes), lanes)
+        value = forward[...].reshape(total, lanes)
+        answer = respond(value, same_side[:, some], cross_side[:, some])
+        result[...] = partial[...] + transform(answer, tab_high, tab_low)
+        wrapped = wrapped_ends(value, tab_end_high, tab_end_low, end_sums, taps)
+        at = pl.ds(pl.multiple_of(jnp.where(z == 0, 0, quarter - lanes), lanes), lanes)
+        result[:, at] = result[:, at] - wrapped
+        keep[...] = result[: total // 2].reshape(keep.shape)
+        send[...] = result[total // 2 :].reshape(send.shape)
+
+    @pl.when(jnp.logical_not(at_end))
+    def _():
+        keep[...] = partial[: total // 2].reshape(keep.shape)
+        send[...] = partial[total // 2 :].reshape(send.shape)
 
 
 def unpack_kernel(most, *rest):
@@ -411,7 +446,6 @@
     lanes = surface.shape[2]
     half = receivers // 2
     chunk = receivers // devices
-    size = chunk // PARTS
     core = lax.axis_index("shot") & 1
     high, low = (jnp.asarray(x) for x in wave_constant(lax.axis_size("freq")))
     dma = pltpu.SemaphoreType.DMA
@@ -449,23 +483,29 @@
         )(block_owner, surface, sibling)
         return [swap(piece, "shot", devices, 2 * (k + 1)) for k, piece in enumerate(pieces)]
 
-    def choose(*sent):
+    sides = [pltpu.VMEM((8, shots * points, lanes), jnp.float32)] * 2
+    cost = shots * chunk * points * lanes * 8
+
+    def others(*sent):
         return kernel_call(
-            functools.partial(choose_kernel, len(sent) > 3),
-            f32(STEPS, POINTS_BLK, chunk, lanes),
-            [SMEM] + [ANY] * (2 + len(sent)),
-            VMEM,
-            [dma((STEPS,))],
+            functools.partial(others_kernel, len(sent) > 3),
+            [f32(2 * shots, chunk, lanes)] * 3 + [f32(STEPS, POINTS_BLK, chunk, lanes)],
+            [SMEM] + [ANY] * (2 + len(sent)) + [VMEM] * 2,
+            [VMEM] * 4,
+            sides + [dma((STEPS,))],
+            flops=3 * cost,
             moved=1 << 20,
-            vmem=8 << 20,
-        )(block_owner, surface, sibling, *sent)
+            vmem=16 << 20,
+        )(block_owner, surface, sibling, *sent, *every)
 
     sent = scatter(0)
 
     spectra = bands[0]
-    for k in range(1, 4):
+    for k in (3, 2, 1):
         spectra = spectra + swap(bands[k], "freq", 4, k)
-    every = jnp.stack([spectra] + [swap(spectra, "shot", devices, 2 * q) for q in (1, 2, 3)])
+    far, second, first = [swap(spectra, "shot", devices, 2 * q) for q in (3, 2, 1)]
+    every = jnp.stack([spectra, first, second, far])
+    sent[2:], every = lax.optimization_barrier((sent[2:], every))
     every = [every, swap(every, "shot", devices, 1)]
 
     places = kernel_call(
@@ -494,57 +534,71 @@
 
     both = (block_owner[0] ^ block_owner[1]) == 1
     sent, every = lax.optimization_barrier((sent, every))
-    chosen = lax.cond(both, lambda *sent: choose(*sent, *scatter(1)), choose, *sent)
-
-    gathered = []
-    for part in range(PARTS):
-        outs = kernel_call(
-            functools.partial(prediction_kernel, part),
-            [f32(2 * shots, size, lanes)] * 4,
-            [VMEM] * 3,
-            [VMEM] * 4,
-            [pltpu.VMEM((8, shots * points, lanes), jnp.float32)] * 2,
-            flops=devices * shots * size * points * lanes * 4,
-            moved=1 << 20,
-            vmem=16 << 20,
-        )(chosen, *every)
-        if gathered:
-            outs, gathered[0] = lax.optimization_barrier((outs, gathered[0]))
-        turned = [outs[0]] + [swap(outs[q], "shot", devices, 2 * q) for q in (1, 2, 3)]
-        own = kernel_call(
-            arrange_kernel,
-            f32(2 * shots, 4, size, lanes),
-            [VMEM] * 4,
-            VMEM,
-            [],
-            moved=1 << 19,
-            vmem=8 << 20,
-        )(*turned)
-        right = lax.ppermute(own, "freq", [(0, 1), (1, 2), (2, 3)])
-        left = lax.ppermute(own, "freq", [(1, 0), (2, 1), (3, 2)])
-        across = swap(own, "freq", 4, 2)
-        forward = lax.ppermute(across, "freq", [(2, 3), (1, 0)])
-        gathered += [own, right, left, across, forward]
-
-    keep, send = kernel_call(
+    *outs, chosen = lax.cond(both, lambda *sent: others(*sent, *scatter(1)), others, *sent)
+    turned = {q: swap(outs[q - 1], "shot", devices, 2 * q) for q in (3, 2, 1)}
+    own = kernel_call(
+        own_kernel,
+        f32(2 * shots, chunk, lanes),
+        [VMEM] * 3,
+        VMEM,
+        sides,
+        flops=cost,
+        moved=1 << 20,
+        vmem=16 << 20,
+    )(chosen, *every)
+    own = kernel_call(
+        arrange_kernel,
+        f32(2 * shots, 4, chunk, lanes),
+        [VMEM] * 4,
+        VMEM,
+        [],
+        moved=1 << 19,
+        vmem=8 << 20,
+    )(own, turned[1], turned[2], turned[3])
+    across = swap(own, "freq", 4, 2)
+    right = lax.ppermute(own, "freq", [(0, 1), (1, 2), (2, 3)])
+    left = lax.ppermute(own, "freq", [(1, 0), (2, 1), (3, 2)])
+    forward = lax.ppermute(across, "freq", [(2, 3), (1, 0)])
+
+    tables = (high, low, end_high, end_low, sums, taps, same_side, cross_side)
+    bf16 = functools.partial(pltpu.VMEM, dtype=jnp.bfloat16)
+    partial = kernel_call(
         inverse_kernel,
-        [f32(shots, half, quarter)] * 2,
-        [ANY] * 5 + [VMEM] * 3 + [ANY] * (5 * PARTS),
-        [VMEM] * 2,
+        f32(rows, quarter),
+        [ANY] * 5 + [VMEM] * 3 + [ANY] * 4,
+        VMEM,
         [
-            pltpu.VMEM((2 * shots, 4, PARTS, size, 4 * lanes), jnp.float32),
-            pltpu.VMEM((quarter, 4 * lanes), jnp.bfloat16),
-            pltpu.VMEM((quarter, 4 * lanes), jnp.bfloat16),
-            pltpu.VMEM((RIM * RIM, 4 * lanes), jnp.bfloat16),
-            pltpu.VMEM((RIM * RIM, 4 * lanes), jnp.bfloat16),
-            pltpu.VMEM((RIM * RIM, lanes), jnp.bfloat16),
-            dma((4 * PARTS,)),
+            pltpu.VMEM((2 * shots, 4, chunk, 4 * lanes), jnp.float32),
+            bf16((quarter, 4 * lanes)),
+            bf16((quarter, 4 * lanes)),
+            bf16((RIM * RIM, 4 * lanes)),
+            bf16((RIM * RIM, 4 * lanes)),
+            bf16((RIM * RIM, lanes)),
+            dma((4,)),
             dma((17,)),
         ],
         flops=6 * rows * 4 * lanes * quarter,
         moved=4 << 20,
         vmem=32 << 20,
-    )(high, low, end_high, end_low, sums, taps, same_side, cross_side, *gathered)
+    )(*tables, own, right, left, across)
+    keep, send = kernel_call(
+        forward_kernel,
+        [f32(shots, half, quarter)] * 2,
+        [ANY] * 5 + [VMEM] * 5,
+        [VMEM] * 2,
+        [
+            bf16((quarter, lanes)),
+            bf16((quarter, lanes)),
+            bf16((RIM * RIM, lanes)),
+            bf16((RIM * RIM, lanes)),
+            bf16((RIM * RIM, lanes)),
+            pltpu.VMEM((rows, quarter), jnp.float32),
+            dma((5,)),
+        ],
+        flops=6 * rows * lanes * quarter,
+        moved=2 << 20,
+        vmem=32 << 20,
+    )(*tables, partial, forward)
     got = swap(send, "shot", devices, 1)
 
     bin_slots = filters.shape[0] * most
@@ -686,7 +740,7 @@
 def on_device(traces, live_mask, offset_bin, surface, block_owner, point_column, filters):
     devices = lax.axis_size("shot")
     in_plane = devices == 8 and lax.axis_size("freq") == 4
-    whole_tiles = traces.shape[1] % (8 * PARTS * devices) == 0 and filters.shape[0] <= 8
+    whole_tiles = traces.shape[1] % (8 * devices) == 0 and filters.shape[0] <= 8
     plan = plane_device if in_plane and whole_tiles else any_device
     return plan(traces, live_mask, offset_bin, surface, block_owner, point_column, filters)
 

time: 97.5 us -> 94.4 us (0.968)
  waiting for transfers between devices: 47 us -> 39.2 us
  Pallas kernels: 17.4 us -> 20.8 us
    ppermute x23, waiting for transfers between devices: 40.2 us -> 34.9 us  [swap(): return lax.ppermute(value, axis, [(i, i ^ bit) for i in range(count)])]
    ppermute x1, waiting for transfers between devices: 6.78 us -> 3.06 us  [plane_device(): forward = lax.ppermute(across, 'freq', [(2, 3), (1, 0)])]
    pallas_call x4 -> x5, Pallas kernels: 8.51 us -> 10.9 us  [the longest x1 3.75 us: others(): kernel_call(functools.partial(others_kernel, len(sent) > 3), [f32(2 * sho...]
    ppermute x1, waiting for transfers between devices: 0.01 us -> 1.18 us  [plane_device(): left = lax.ppermute(own, 'freq', [(1, 0), (2, 1), (3, 2)])]
    pallas_call x1, Pallas kernels: 2.25 us -> 3.27 us  [plane_device(): kernel_call(functools.partial(response_kernel, filters.shape[0]), [f32(ro...]
  transfers between devices with their start and end apart: 26 -> 26, of which waited for: 14 -> 14; matrix products, arithmetic and copies ran while one was open for 1% -> 1% of each run, Pallas kernels for 5% -> 12%
where the time goes in v3:
time: 94.4 us; the launch traced here: 94.1 us
  waiting for transfers between devices  39.2 us (42%)
  starting transfers between devices  31.1 us (33%)
  Pallas kernels  20.8 us (22%)
  between operations  1.57 us (2%)
    ppermute x23, waiting for transfers between devices, swap(): return lax.ppermute(value, axis, [(i, i ^ bit) for i in range(count)])  34.9 us
    ppermute x23, starting transfers between devices, swap(): return lax.ppermute(value, axis, [(i, i ^ bit) for i in range(count)])  24.6 us
    ppermute x1, starting transfers between devices, plane_device(): right = lax.ppermute(own, 'freq', [(0, 1), (1, 2), (2, 3)])  3.93 us
    pallas_call x1, Pallas kernels, others(): kernel_call(functools.partial(others_kernel, len(sent) > 3), [f32(2 * sho...  3.75 us
    pallas_call x1, Pallas kernels, plane_device(): kernel_call(inverse_kernel, f32(rows, quarter), [ANY] * 5 + [VMEM] * 3 +...  3.36 us
    pallas_call x1, Pallas kernels, plane_device(): kernel_call(functools.partial(response_kernel, filters.shape[0]), [f32(ro...  3.27 us
    ppermute x1, waiting for transfers between devices, plane_device(): forward = lax.ppermute(across, 'freq', [(2, 3), (1, 0)])  3.06 us
  transfers between devices with their start and end apart: 26, of which 14 were waited for; matrix products, arithmetic and copies ran while one was open for 1% of the time, Pallas kernels for 12%

profile of v3, /device:TPU:0, one launch (start us, length us, event | category | flops | bytes accessed | tf_op | source)
XLA Modules:
  0.0 94.1 jit_solution(1437519442077057670)
XLA Ops:
  0.0 1.4 %sibling_kernel.1 = f32[16,128,128]{2,1,0:T(8,128)S(1)} custom-call(f32[16,256,128]{2,1,0:T(8,128)} %surface.3), custom_call_target="tpu_custom_call" | custom-call | bytes 2097152 | tf_op jit(solution)/shard_map/sibling_kernel/pallas_call | solution.py:453
  3.3 5.1 %collective-permute-start.5 = (f32[104,128]{1,0:T(8,128)S(1)}, f32[104,128]{1,0:T(8,128)S(1)}, u32[]{:S(2)}, u32[]{:S(2)}) collective-permute-start(f32[104,128]{1,0:T(8,128)S(1)} %get-tuple-element.89), channel_id=1, source_target_pairs={{0,3},{1,2},{2,1},{3,0},{4,7},{5,6},{6,5},{7,4},{8,11},{9,10},{10,... | collective-permute-start | bytes 159752 | tf_op jit(solution)/shard_map/ppermute | solution.py:80
  9.7 2.6 %collective-permute-start.4 = (f32[16,32,128]{2,1,0:T(8,128)S(1)}, f32[16,32,128]{2,1,0:T(8,128)S(1)}, u32[]{:S(2)}, u32[]{:S(2)}) collective-permute-start(f32[16,32,128]{2,1,0:T(8,128)S(1)} %get-tuple-element.87), channel_id=1, source_target_pairs={{0,24},{4,28},{8,16},{12,20},{16,8},{20,12},{24,0},{28,4},{1,25},{... | collective-permute-start | bytes 786440 | tf_op jit(solution)/shard_map/ppermute | solution.py:80
  13.5 1.6 %collective-permute-start.8 = (f32[104,128]{1,0:T(8,128)S(1)}, f32[104,128]{1,0:T(8,128)S(1)}, u32[]{:S(2)}, u32[]{:S(2)}) collective-permute-start(f32[104,128]{1,0:T(8,128)S(1)} %add_add_fusion), channel_id=1, source_target_pairs={{0,8},{4,12},{8,0},{12,4},{16,24},{20,28},{24,16},{28,20},{1,9},{5... | collective-permute-start | bytes 159752 | tf_op jit(solution)/shard_map/ppermute | solution.py:80
  15.0 1.5 %collective-permute-start.9 = (f32[104,128]{1,0:T(8,128)S(1)}, f32[104,128]{1,0:T(8,128)S(1)}, u32[]{:S(2)}, u32[]{:S(2)}) collective-permute-start(f32[104,128]{1,0:T(8,128)S(1)} %add_add_fusion), channel_id=1, source_target_pairs={{0,16},{4,20},{8,24},{12,28},{16,0},{20,4},{24,8},{28,12},{1,17},{... | collective-permute-start | bytes 159752 | tf_op jit(solution)/shard_map/ppermute | solution.py:80
  17.0 1.5 %collective-permute-start.12 = (f32[16,32,128]{2,1,0:T(8,128)S(1)}, f32[16,32,128]{2,1,0:T(8,128)S(1)}, u32[]{:S(2)}, u32[]{:S(2)}) collective-permute-start(f32[16,32,128]{2,1,0:T(8,128)S(1)} %get-tuple-element.96), channel_id=1, source_target_pairs={{0,8},{4,12},{8,0},{12,4},{16,24},{20,28},{24,16},{28,20},{1,9},{5... | collective-permute-start | bytes 786440 | tf_op jit(solution)/shard_map/ppermute | solution.py:80
  18.5 2.7 %collective-permute-done.8 = f32[104,128]{1,0:T(8,128)S(1)} collective-permute-done((f32[104,128]{1,0:T(8,128)S(1)}, f32[104,128]{1,0:T(8,128)S(1)}, u32[]{:S(2)}, u32[]{:S(2)}) %collective-permute-start.8) | collective-permute-done | bytes 53280 | tf_op jit(solution)/shard_map/ppermute | solution.py:80
  24.8 1.5 %collective-permute-done.12 = f32[16,32,128]{2,1,0:T(8,128)S(1)} collective-permute-done((f32[16,32,128]{2,1,0:T(8,128)S(1)}, f32[16,32,128]{2,1,0:T(8,128)S(1)}, u32[]{:S(2)}, u32[]{:S(2)}) %collective-permute-start.12) | collective-permute-done | bytes 262176 | tf_op jit(solution)/shard_map/ppermute | solution.py:80
  27.6 3.8 %conditional.1 = ((f32[6,32,128]{2,1,0:T(8,128)S(1)}, f32[6,32,128]{2,1,0:T(8,128)S(1)}, f32[6,32,128]{2,1,0:T(8,128)}, f32[2,16,32,128]{3,2,1,0:T(8,128)})) conditional(s32[]{:T(128)} %bitcast.4, (s32[2]{0:T(128)S(1)}, f32[16,256,128]{2,1,0:T(8,128)S(1)}, f32[16,128,128]{2,1,0:T(8,128)S(1)}, f32[16,32,128]{2,1,0:T(8,128)S(1)}, ...), branch_computations={%region_0.0_spmd, %region_1.0_spmd} | conditional | flops 9437184 | bytes 12583152 | solution.py:537
  27.6 3.8 %others_kernel.2 = (f32[6,32,128]{2,1,0:T(8,128)S(1)}, f32[6,32,128]{2,1,0:T(8,128)S(1)}, f32[6,32,128]{2,1,0:T(8,128)}, f32[2,16,32,128]{3,2,1,0:T(8,128)}) custom-call(s32[2]{0:T(128)S(1)} %get-tuple-element.37.owners, f32[16,256,128]{2,1,0:T(8,128)S(1)} %get-tuple-element.38.surface, f32[16,128,128]{2,1,0:T(8,128)S(1)} %get-tuple-element.39.sibling, ...), custom_call_target="tpu_custom_call" | custom-call | flops 9437184 | bytes 1048576 | tf_op jit(solution)/shard_map/cond/branch_0_fun/others_kernel/pallas_call | solution.py:490
  31.4 1.6 %collective-permute-start.14 = (f32[6,32,128]{2,1,0:T(8,128)S(1)}, f32[6,32,128]{2,1,0:T(8,128)S(1)}, u32[]{:S(2)}, u32[]{:S(2)}) collective-permute-start(f32[6,32,128]{2,1,0:T(8,128)S(1)} %get-tuple-element.105), channel_id=1, source_target_pairs={{0,8},{4,12},{8,0},{12,4},{16,24},{20,28},{24,16},{28,20},{1,9},{5... | collective-permute-start | bytes 294920 | tf_op jit(solution)/shard_map/ppermute | solution.py:80
  33.4 1.6 %collective-permute-start.16 = (f32[6,32,128]{2,1,0:T(8,128)}, f32[6,32,128]{2,1,0:T(8,128)S(1)}, u32[]{:S(2)}, u32[]{:S(2)}) collective-permute-start(f32[6,32,128]{2,1,0:T(8,128)} %get-tuple-element.107), channel_id=1, source_target_pairs={{0,24},{4,28},{8,16},{12,20},{16,8},{20,12},{24,0},{28,4},{1,25},{... | collective-permute-start | bytes 294920 | tf_op jit(solution)/shard_map/ppermute | solution.py:80
  35.0 1.9 %own_kernel.1.own = f32[6,32,128]{2,1,0:T(8,128)S(1)} custom-call(f32[2,16,32,128]{3,2,1,0:T(8,128)} %get-tuple-element.104.chosen, f32[4,104,128]{2,1,0:T(8,128)} %pad_maximum_fusion.rest_0_.own, f32[4,104,128]{2,1,0:T(8,128)} %collective-permute-done.11.rest_1_.other), custom_call_target="tpu_custom_call" | custom-call | flops 3145728 | bytes 1048576 | tf_op jit(solution)/shard_map/own_kernel/pallas_call | solution.py:539
  37.8 1.3 %collective-permute-done.16.third = f32[6,32,128]{2,1,0:T(8,128)S(1)} collective-permute-done((f32[6,32,128]{2,1,0:T(8,128)}, f32[6,32,128]{2,1,0:T(8,128)S(1)}, u32[]{:S(2)}, u32[]{:S(2)}) %collective-permute-start.16) | collective-permute-done | bytes 98336 | tf_op jit(solution)/shard_map/ppermute | solution.py:80
  39.2 2.4 %collective-permute-start.19 = (f32[6,4,32,128]{3,2,1,0:T(8,128)S(1)}, f32[6,4,32,128]{3,2,1,0:T(8,128)S(1)}, u32[]{:S(2)}, u32[]{:S(2)}) collective-permute-start(f32[6,4,32,128]{3,2,1,0:T(8,128)S(1)} %arrange_kernel.1.rest_0_), channel_id=1, source_target_pairs={{0,2},{1,3},{2,0},{3,1},{4,6},{5,7},{6,4},{7,5},{8,10},{9,11},{10,... | collective-permute-start | bytes 1179656 | tf_op jit(solution)/shard_map/ppermute | solution.py:80
  41.5 3.9 %collective-permute-start.17 = (f32[6,4,32,128]{3,2,1,0:T(8,128)S(1)}, f32[6,4,32,128]{3,2,1,0:T(8,128)S(1)}, u32[]{:S(2)}, u32[]{:S(2)}) collective-permute-start(f32[6,4,32,128]{3,2,1,0:T(8,128)S(1)} %arrange_kernel.1.rest_0_), channel_id=1, source_target_pairs={{0,1},{1,2},{2,3},{4,5},{5,6},{6,7},{8,9},{9,10},{10,11},{12,13},{... | collective-permute-start | bytes 1179656 | tf_op jit(solution)/shard_map/ppermute | solution.py:559
  46.8 11.9 %collective-permute-done.19.rest_3_ = f32[6,4,32,128]{3,2,1,0:T(8,128)S(1)} collective-permute-done((f32[6,4,32,128]{3,2,1,0:T(8,128)S(1)}, f32[6,4,32,128]{3,2,1,0:T(8,128)S(1)}, u32[]{:S(2)}, u32[]{:S(2)}) %collective-permute-start.19) | collective-permute-done | bytes 393248 | tf_op jit(solution)/shard_map/ppermute | solution.py:80
  60.0 3.3 %response_kernel.1 = (f32[768,256]{1,0:T(8,128)S(1)}, f32[768,512]{1,0:T(8,128)S(1)}, f32[768,512]{1,0:T(8,128)S(1)}) custom-call(s32[3,256]{1,0:T(4,128)S(1)} %bitcast.13, f32[128,512]{1,0:T(8,128)S(1)} %copy-done.7, f32[2,128,256]{2,1,0:T(8,128)S(1)} %copy-done.8, f32[4,104,128]{2,1,0:T(8,128)} %pad_maximum_fusion.rest_0_.own, ...), custom_call_target="tpu_custom_call" | custom-call | flops 226492416 | bytes 4194304 | tf_op jit(solution)/shard_map/response_kernel/pallas_call | solution.py:524
  64.5 3.4 %inverse_kernel.1.partial = f32[768,256]{1,0:T(8,128)S(1)} custom-call(bf16[1056,512]{1,0:T(8,128)(2,1)S(1)} %copy-done, bf16[1056,512]{1,0:T(8,128)(2,1)S(1)} %copy-done.1, bf16[512,512]{1,0:T(8,128)(2,1)S(1)} %copy-done.2, bf16[512,512]{1,0:T(8,128)(2,1)S(1)} %copy-done.3, bf16[512,128]{1,0:T(8,128)(2,1)S(1)} %copy-done.6, ...), custom_call_target="tpu_custom_call" | custom-call | flops 603979776 | bytes 4194304 | tf_op jit(solution)/shard_map/inverse_kernel/pallas_call | solution.py:565
  67.8 3.1 %collective-permute-done.20.forward = f32[6,4,32,128]{3,2,1,0:T(8,128)S(1)} collective-permute-done((f32[6,4,32,128]{3,2,1,0:T(8,128)S(1)}, f32[6,4,32,128]{3,2,1,0:T(8,128)S(1)}, u32[]{:S(2)}, u32[]{:S(2)}) %collective-permute-start.20) | collective-permute-done | bytes 393248 | tf_op jit(solution)/shard_map/ppermute | solution.py:561
  70.9 1.9 %forward_kernel.1 = (f32[3,128,256]{2,1,0:T(8,128)S(1)}, f32[3,128,256]{2,1,0:T(8,128)S(1)}) custom-call(bf16[1056,512]{1,0:T(8,128)(2,1)S(1)} %copy-done, bf16[1056,512]{1,0:T(8,128)(2,1)S(1)} %copy-done.1, bf16[512,512]{1,0:T(8,128)(2,1)S(1)} %copy-done.2, bf16[512,512]{1,0:T(8,128)(2,1)S(1)} %copy-done.3, bf16[512,128]{1,0:T(8,128)(2,1)S(1)} %copy-done.6, ...), custom_call_target="tpu_custom_call" | custom-call | flops 150994944 | bytes 2097152 | tf_op jit(solution)/shard_map/forward_kernel/pallas_call | solution.py:584
  80.5 2.3 %collective-permute-done.23.rest_2_ = f32[144,256]{1,0:T(8,128)S(1)} collective-permute-done((f32[144,256]{1,0:T(8,128)S(1)}, f32[144,256]{1,0:T(8,128)S(1)}, u32[]{:S(2)}, u32[]{:S(2)}) %collective-permute-start.23) | collective-permute-done | bytes 147488 | tf_op jit(solution)/shard_map/ppermute | solution.py:80
  82.8 2.0 %collective-permute-done.24.rest_3_ = f32[144,256]{1,0:T(8,128)S(1)} collective-permute-done((f32[144,256]{1,0:T(8,128)S(1)}, f32[144,256]{1,0:T(8,128)S(1)}, u32[]{:S(2)}, u32[]{:S(2)}) %collective-permute-start.24) | collective-permute-done | bytes 147488 | tf_op jit(solution)/shard_map/ppermute | solution.py:80
  84.8 8.2 %collective-permute-done.26.rest_5_ = f32[144,256]{1,0:T(8,128)S(1)} collective-permute-done((f32[144,256]{1,0:T(8,128)S(1)}, f32[144,256]{1,0:T(8,128)S(1)}, u32[]{:S(2)}, u32[]{:S(2)}) %collective-permute-start.26) | collective-permute-done | bytes 147488 | tf_op jit(solution)/shard_map/ppermute | solution.py:80
  (76 shorter events, 22.2 us)
Async XLA Ops:
  1.5 7.6 %collective-permute-start.3 = (f32[16,128,128]{2,1,0:T(8,128)S(1)}, f32[16,128,128]{2,1,0:T(8,128)S(1)}, u32[]{:S(2)}, u32[]{:S(2)}) collective-permute-start(f32[16,128,128]{2,1,0:T(8,128)S(1)} %sibling_kernel.1), channel_id=1, source_target_pairs={{0,4},{4,0},{8,12},{12,8},{16,20},{20,16},{24,28},{28,24},{1,5},{5... | collective-permute-start | bytes 3145736 | tf_op jit(solution)/shard_map/ppermute | solution.py:80
  3.3 9.1 %collective-permute-start.5 = (f32[104,128]{1,0:T(8,128)S(1)}, f32[104,128]{1,0:T(8,128)S(1)}, u32[]{:S(2)}, u32[]{:S(2)}) collective-permute-start(f32[104,128]{1,0:T(8,128)S(1)} %get-tuple-element.89), channel_id=1, source_target_pairs={{0,3},{1,2},{2,1},{3,0},{4,7},{5,6},{6,5},{7,4},{8,11},{9,10},{10,... | collective-permute-start | bytes 159752 | tf_op jit(solution)/shard_map/ppermute | solution.py:80
  8.4 5.0 %collective-permute-start.6 = (f32[104,128]{1,0:T(8,128)S(1)}, f32[104,128]{1,0:T(8,128)S(1)}, u32[]{:S(2)}, u32[]{:S(2)}) collective-permute-start(f32[104,128]{1,0:T(8,128)S(1)} %get-tuple-element.90), channel_id=1, source_target_pairs={{0,2},{1,3},{2,0},{3,1},{4,6},{5,7},{6,4},{7,5},{8,10},{9,11},{10,... | collective-permute-start | bytes 159752 | tf_op jit(solution)/shard_map/ppermute | solution.py:80
  8.4 5.0 %collective-permute-start.7 = (f32[104,128]{1,0:T(8,128)S(1)}, f32[104,128]{1,0:T(8,128)S(1)}, u32[]{:S(2)}, u32[]{:S(2)}) collective-permute-start(f32[104,128]{1,0:T(8,128)S(1)} %get-tuple-element.91), channel_id=1, source_target_pairs={{0,1},{1,0},{2,3},{3,2},{4,5},{5,4},{6,7},{7,6},{8,9},{9,8},{10,11... | collective-permute-start | bytes 159752 | tf_op jit(solution)/shard_map/ppermute | solution.py:80
  9.7 13.2 %collective-permute-start.4 = (f32[16,32,128]{2,1,0:T(8,128)S(1)}, f32[16,32,128]{2,1,0:T(8,128)S(1)}, u32[]{:S(2)}, u32[]{:S(2)}) collective-permute-start(f32[16,32,128]{2,1,0:T(8,128)S(1)} %get-tuple-element.87), channel_id=1, source_target_pairs={{0,24},{4,28},{8,16},{12,20},{16,8},{20,12},{24,0},{28,4},{1,25},{... | collective-permute-start | bytes 786440 | tf_op jit(solution)/shard_map/ppermute | solution.py:80
  13.5 7.8 %collective-permute-start.8 = (f32[104,128]{1,0:T(8,128)S(1)}, f32[104,128]{1,0:T(8,128)S(1)}, u32[]{:S(2)}, u32[]{:S(2)}) collective-permute-start(f32[104,128]{1,0:T(8,128)S(1)} %add_add_fusion), channel_id=1, source_target_pairs={{0,8},{4,12},{8,0},{12,4},{16,24},{20,28},{24,16},{28,20},{1,9},{5... | collective-permute-start | bytes 159752 | tf_op jit(solution)/shard_map/ppermute | solution.py:80
  15.0 6.2 %collective-permute-start.9 = (f32[104,128]{1,0:T(8,128)S(1)}, f32[104,128]{1,0:T(8,128)S(1)}, u32[]{:S(2)}, u32[]{:S(2)}) collective-permute-start(f32[104,128]{1,0:T(8,128)S(1)} %add_add_fusion), channel_id=1, source_target_pairs={{0,16},{4,20},{8,24},{12,28},{16,0},{20,4},{24,8},{28,12},{1,17},{... | collective-permute-start | bytes 159752 | tf_op jit(solution)/shard_map/ppermute | solution.py:80
  16.5 5.7 %collective-permute-start.10 = (f32[104,128]{1,0:T(8,128)S(1)}, f32[104,128]{1,0:T(8,128)S(1)}, u32[]{:S(2)}, u32[]{:S(2)}) collective-permute-start(f32[104,128]{1,0:T(8,128)S(1)} %add_add_fusion), channel_id=1, source_target_pairs={{0,24},{4,28},{8,16},{12,20},{16,8},{20,12},{24,0},{28,4},{1,25},{... | collective-permute-start | bytes 159752 | tf_op jit(solution)/shard_map/ppermute | solution.py:80
  17.0 9.2 %collective-permute-start.12 = (f32[16,32,128]{2,1,0:T(8,128)S(1)}, f32[16,32,128]{2,1,0:T(8,128)S(1)}, u32[]{:S(2)}, u32[]{:S(2)}) collective-permute-start(f32[16,32,128]{2,1,0:T(8,128)S(1)} %get-tuple-element.96), channel_id=1, source_target_pairs={{0,8},{4,12},{8,0},{12,4},{16,24},{20,28},{24,16},{28,20},{1,9},{5... | collective-permute-start | bytes 786440 | tf_op jit(solution)/shard_map/ppermute | solution.py:80
  21.2 6.4 %collective-permute-start.13 = (f32[16,32,128]{2,1,0:T(8,128)S(1)}, f32[16,32,128]{2,1,0:T(8,128)S(1)}, u32[]{:S(2)}, u32[]{:S(2)}) collective-permute-start(f32[16,32,128]{2,1,0:T(8,128)S(1)} %get-tuple-element.97), channel_id=1, source_target_pairs={{0,16},{4,20},{8,24},{12,28},{16,0},{20,4},{24,8},{28,12},{1,17},{... | collective-permute-start | bytes 786440 | tf_op jit(solution)/shard_map/ppermute | solution.py:80
  22.9 4.7 %collective-permute-start.11 = (f32[4,104,128]{2,1,0:T(8,128)}, f32[4,104,128]{2,1,0:T(8,128)}, u32[]{:S(2)}, u32[]{:S(2)}) collective-permute-start(f32[4,104,128]{2,1,0:T(8,128)} %pad_maximum_fusion.rest_0_.own), channel_id=1, source_target_pairs={{0,4},{4,0},{8,12},{12,8},{16,20},{20,16},{24,28},{28,24},{1,5},{5... | collective-permute-start | bytes 638984 | tf_op jit(solution)/shard_map/ppermute | solution.py:80
  31.4 5.4 %collective-permute-start.14 = (f32[6,32,128]{2,1,0:T(8,128)S(1)}, f32[6,32,128]{2,1,0:T(8,128)S(1)}, u32[]{:S(2)}, u32[]{:S(2)}) collective-permute-start(f32[6,32,128]{2,1,0:T(8,128)S(1)} %get-tuple-element.105), channel_id=1, source_target_pairs={{0,8},{4,12},{8,0},{12,4},{16,24},{20,28},{24,16},{28,20},{1,9},{5... | collective-permute-start | bytes 294920 | tf_op jit(solution)/shard_map/ppermute | solution.py:80
  33.0 4.8 %collective-permute-start.15 = (f32[6,32,128]{2,1,0:T(8,128)S(1)}, f32[6,32,128]{2,1,0:T(8,128)S(1)}, u32[]{:S(2)}, u32[]{:S(2)}) collective-permute-start(f32[6,32,128]{2,1,0:T(8,128)S(1)} %get-tuple-element.106), channel_id=1, source_target_pairs={{0,16},{4,20},{8,24},{12,28},{16,0},{20,4},{24,8},{28,12},{1,17},{... | collective-permute-start | bytes 294920 | tf_op jit(solution)/shard_map/ppermute | solution.py:80
  33.4 5.7 %collective-permute-start.16 = (f32[6,32,128]{2,1,0:T(8,128)}, f32[6,32,128]{2,1,0:T(8,128)S(1)}, u32[]{:S(2)}, u32[]{:S(2)}) collective-permute-start(f32[6,32,128]{2,1,0:T(8,128)} %get-tuple-element.107), channel_id=1, source_target_pairs={{0,24},{4,28},{8,16},{12,20},{16,8},{20,12},{24,0},{28,4},{1,25},{... | collective-permute-start | bytes 294920 | tf_op jit(solution)/shard_map/ppermute | solution.py:80
  39.2 19.5 %collective-permute-start.19 = (f32[6,4,32,128]{3,2,1,0:T(8,128)S(1)}, f32[6,4,32,128]{3,2,1,0:T(8,128)S(1)}, u32[]{:S(2)}, u32[]{:S(2)}) collective-permute-start(f32[6,4,32,128]{3,2,1,0:T(8,128)S(1)} %arrange_kernel.1.rest_0_), channel_id=1, source_target_pairs={{0,2},{1,3},{2,0},{3,1},{4,6},{5,7},{6,4},{7,5},{8,10},{9,11},{10,... | collective-permute-start | bytes 1179656 | tf_op jit(solution)/shard_map/ppermute | solution.py:80
  41.5 21.7 %collective-permute-start.17 = (f32[6,4,32,128]{3,2,1,0:T(8,128)S(1)}, f32[6,4,32,128]{3,2,1,0:T(8,128)S(1)}, u32[]{:S(2)}, u32[]{:S(2)}) collective-permute-start(f32[6,4,32,128]{3,2,1,0:T(8,128)S(1)} %arrange_kernel.1.rest_0_), channel_id=1, source_target_pairs={{0,1},{1,2},{2,3},{4,5},{5,6},{6,7},{8,9},{9,10},{10,11},{12,13},{... | collective-permute-start | bytes 1179656 | tf_op jit(solution)/shard_map/ppermute | solution.py:559
  45.5 19.0 %collective-permute-start.18 = (f32[6,4,32,128]{3,2,1,0:T(8,128)S(1)}, f32[6,4,32,128]{3,2,1,0:T(8,128)S(1)}, u32[]{:S(2)}, u32[]{:S(2)}) collective-permute-start(f32[6,4,32,128]{3,2,1,0:T(8,128)S(1)} %arrange_kernel.1.rest_0_), channel_id=1, source_target_pairs={{1,0},{2,1},{3,2},{5,4},{6,5},{7,6},{9,8},{10,9},{11,10},{13,12},{... | collective-permute-start | bytes 1179656 | tf_op jit(solution)/shard_map/ppermute | solution.py:560
  58.7 12.2 %collective-permute-start.20 = (f32[6,4,32,128]{3,2,1,0:T(8,128)S(1)}, f32[6,4,32,128]{3,2,1,0:T(8,128)S(1)}, u32[]{:S(2)}, u32[]{:S(2)}) collective-permute-start(f32[6,4,32,128]{3,2,1,0:T(8,128)S(1)} %collective-permute-done.19.rest_3_), channel_id=1, source_target_pairs={{2,3},{1,0},{6,7},{5,4},{10,11},{9,8},{14,15},{13,12},{18,19},{17,... | collective-permute-start | bytes 1179656 | tf_op jit(solution)/shard_map/ppermute | solution.py:561
  76.1 6.7 %collective-permute-start.23 = (f32[144,256]{1,0:T(8,128)S(1)}, f32[144,256]{1,0:T(8,128)S(1)}, u32[]{:S(2)}, u32[]{:S(2)}) collective-permute-start(f32[144,256]{1,0:T(8,128)S(1)} %get-tuple-element.112), channel_id=1, source_target_pairs={{0,8},{4,12},{8,0},{12,4},{16,24},{20,28},{24,16},{28,20},{1,9},{5... | collective-permute-start | bytes 442376 | tf_op jit(solution)/shard_map/ppermute | solution.py:80
  77.2 7.6 %collective-permute-start.24 = (f32[144,256]{1,0:T(8,128)S(1)}, f32[144,256]{1,0:T(8,128)S(1)}, u32[]{:S(2)}, u32[]{:S(2)}) collective-permute-start(f32[144,256]{1,0:T(8,128)S(1)} %get-tuple-element.113), channel_id=1, source_target_pairs={{0,12},{4,8},{8,4},{12,0},{16,28},{20,24},{24,20},{28,16},{1,13},{... | collective-permute-start | bytes 442376 | tf_op jit(solution)/shard_map/ppermute | solution.py:80
  77.8 7.0 %collective-permute-start.25 = (f32[144,256]{1,0:T(8,128)S(1)}, f32[144,256]{1,0:T(8,128)S(1)}, u32[]{:S(2)}, u32[]{:S(2)}) collective-permute-start(f32[144,256]{1,0:T(8,128)S(1)} %get-tuple-element.114), channel_id=1, source_target_pairs={{0,16},{4,20},{8,24},{12,28},{16,0},{20,4},{24,8},{28,12},{1,17},{... | collective-permute-start | bytes 442376 | tf_op jit(solution)/shard_map/ppermute | solution.py:80
  78.5 14.6 %collective-permute-start.26 = (f32[144,256]{1,0:T(8,128)S(1)}, f32[144,256]{1,0:T(8,128)S(1)}, u32[]{:S(2)}, u32[]{:S(2)}) collective-permute-start(f32[144,256]{1,0:T(8,128)S(1)} %get-tuple-element.115), channel_id=1, source_target_pairs={{0,20},{4,16},{8,28},{12,24},{16,4},{20,0},{24,12},{28,8},{1,21},{... | collective-permute-start | bytes 442376 | tf_op jit(solution)/shard_map/ppermute | solution.py:80
  79.6 13.4 %collective-permute-start.27 = (f32[144,256]{1,0:T(8,128)S(1)}, f32[144,256]{1,0:T(8,128)S(1)}, u32[]{:S(2)}, u32[]{:S(2)}) collective-permute-start(f32[144,256]{1,0:T(8,128)S(1)} %get-tuple-element.116), channel_id=1, source_target_pairs={{0,24},{4,28},{8,16},{12,20},{16,8},{20,12},{24,0},{28,4},{1,25},{... | collective-permute-start | bytes 442376 | tf_op jit(solution)/shard_map/ppermute | solution.py:80
  82.8 10.3 %collective-permute-start.28 = (f32[144,256]{1,0:T(8,128)S(1)}, f32[144,256]{1,0:T(8,128)S(1)}, u32[]{:S(2)}, u32[]{:S(2)}) collective-permute-start(f32[144,256]{1,0:T(8,128)S(1)} %get-tuple-element.117), channel_id=1, source_target_pairs={{0,28},{4,24},{8,20},{12,16},{16,12},{20,8},{24,4},{28,0},{1,29},{... | collective-permute-start | bytes 442376 | tf_op jit(solution)/shard_map/ppermute | solution.py:80
  (17 other events, 193.3 us)

commit v4 on v3

--- a/solution.py
+++ b/solution.py
@@ -15,6 +15,7 @@
 POINTS_BLK = 16
 STEPS = 2
 RIM = 16
+FAR_FIRST = (3, 1, 2)
 
 FULL_PRECISION = lax.Precision.HIGHEST
 VMEM = pl.BlockSpec(memory_space=pltpu.VMEM)
@@ -211,9 +212,10 @@
         pass
 
 
-def arrange_kernel(own, first, second, third, out):
+def arrange_kernel(order, *rest):
+    pieces, out = rest[:-1], rest[-1]
     chip = lax.axis_index("shot") // 2
-    for q, piece in enumerate((own, first, second, third)):
+    for q, piece in zip(order, pieces):
         out[:, chip ^ q] = piece[...]
 
 
@@ -262,8 +264,8 @@
     side = picks[(z + 1) // 4]
     taps[...] = per_trace(jnp.dot(table, side, precision=FULL_PRECISION, preferred_element_type=jnp.float32))
     lane = lax.broadcasted_iota(jnp.int32, (devices * padded, lanes), 1)
-    for slot, step in enumerate((0, 3, 1, 2)):
-        cols = pl.ds(pl.multiple_of((z + step) % 4 * lanes, lanes), lanes)
+    for slot in range(4):
+        cols = pl.ds(pl.multiple_of((z ^ slot) * lanes, lanes), lanes)
         answer = jnp.dot(table, waves[:, cols], precision=FULL_PRECISION, preferred_element_type=jnp.float32)
         turned = pltpu.roll(answer, lanes // 2, 1)
         into = slice(slot * lanes, (slot + 1) * lanes)
@@ -296,6 +298,13 @@
     return full * (2.0 / NT)
 
 
+def transform_band(value, into_high, into_low):
+    left_high, left_low = split_two(value)
+    both = jnp.concatenate([left_high, left_low], axis=1)
+    twice = jnp.concatenate([into_high[...], into_high[...]], axis=1)
+    return (dot_nt(both, twice) + dot_nt(left_high, into_low[...])) * (2.0 / NT)
+
+
 def respond(value, same_side, cross_side):
     lanes = 2 * NF // 4
     bands = [value[:, i : i + lanes] for i in range(0, value.shape[1], lanes)]
@@ -303,13 +312,13 @@
     return value * same_side + turned * cross_side
 
 
-def wrapped_ends(value, end_high, end_low, end_sums, taps):
-    beyond_high, beyond_low = split_two(transform(value, end_high, end_low) * taps[...])
+def wrapped_ends(beyond, end_sums, taps):
+    beyond_high, beyond_low = split_two(beyond * taps[...])
     return dot_nn(beyond_high, end_sums[...]) + dot_nn(beyond_low, end_sums[...])
 
 
 def inverse_kernel(high, low, end_high, end_low, sums, taps, same_side, cross_side, *rest):
-    own, right, left, across, out, gathered, tab_high, tab_low, tab_end_high, tab_end_low, end_sums, sems, tab_sems = rest
+    own, near, across, middle, out, gathered, tab_high, tab_low, tab_end_high, tab_end_low, end_sums, sems, tab_sems = rest
     z = lax.axis_index("freq")
     lanes = own.shape[3]
     quarter = tab_high.shape[0]
@@ -319,8 +328,8 @@
     end_rows = pl.ds(pl.multiple_of((z + 1) // 4 * end_size, 16), end_size)
     loads = []
     end_loads = [pltpu.make_async_copy(sums.at[end_rows], end_sums, tab_sems.at[16])]
-    for slot, step in enumerate((0, 3, 1, 2)):
-        cols = pl.ds(pl.multiple_of((z + step) % 4 * lanes, lanes), lanes)
+    for slot in range(4):
+        cols = pl.ds(pl.multiple_of((z ^ slot) * lanes, lanes), lanes)
         into = pl.ds(slot * lanes, lanes)
         for i, (table, scratch) in enumerate(((high, tab_high), (low, tab_low))):
             loads.append(pltpu.make_async_copy(table.at[rows, cols], scratch.at[:, into], tab_sems.at[4 * slot + i]))
@@ -338,23 +347,21 @@
     def fetch(source, slot):
         return pltpu.make_async_copy(source, gathered.at[:, :, :, pl.ds(slot * lanes, lanes)], sems.at[slot])
 
-    fetch(own, 0).start()
-    fetch(across, 3).start()
-    for slot, source, there in ((1, right, z > 0), (2, left, z < 3)):
-
-        @pl.when(there)
-        def _(slot=slot, source=source):
-            fetch(source, slot).start()
-            fetch(source, slot).wait()
-
-        @pl.when(jnp.logical_not(there))
-        def _(slot=slot):
-            gathered[:, :, :, slot * lanes : (slot + 1) * lanes] = jnp.zeros(own.shape, jnp.float32)
-
-    for load in loads:
-        load.wait()
-    fetch(own, 0).wait()
-    fetch(across, 3).wait()
+    straight = [fetch(band, slot) for slot, band in enumerate((own, near, across))]
+    for copy in straight:
+        copy.start()
+
+    @pl.when(at_end)
+    def _():
+        gathered[:, :, :, 3 * lanes :] = jnp.zeros(own.shape, jnp.float32)
+
+    @pl.when(jnp.logical_not(at_end))
+    def _():
+        fetch(middle, 3).start()
+        fetch(middle, 3).wait()
+
+    for copy in loads + straight:
+        copy.wait()
     total = math.prod(own.shape[:3])
     value = gathered[...].reshape(total, 4 * lanes)
     out[...] = transform(respond(value, same_side[...], cross_side[...]), tab_high, tab_low)
@@ -363,7 +370,8 @@
     def _():
         for load in end_loads:
             load.wait()
-        wrapped = wrapped_ends(gathered[...].reshape(total, 4 * lanes), tab_end_high, tab_end_low, end_sums, taps)
+        beyond = transform(gathered[...].reshape(total, 4 * lanes), tab_end_high, tab_end_low)
+        wrapped = wrapped_ends(beyond, end_sums, taps)
         cols = pl.ds(pl.multiple_of(jnp.where(z == 0, 0, quarter - lanes), lanes), lanes)
         out[:, cols] = out[:, cols] - wrapped
 
@@ -389,12 +397,11 @@
             pltpu.make_async_copy(sums.at[end_rows], end_sums, sems.at[4]),
         ]
         run_all(loads)
-        slot = jnp.where(z == 0, 1, 2)
-        some = pl.ds(pl.multiple_of(slot * lanes, lanes), lanes)
+        some = slice(3 * lanes, 4 * lanes)
         value = forward[...].reshape(total, lanes)
         answer = respond(value, same_side[:, some], cross_side[:, some])
-        result[...] = partial[...] + transform(answer, tab_high, tab_low)
-        wrapped = wrapped_ends(value, tab_end_high, tab_end_low, end_sums, taps)
+        result[...] = partial[...] + transform_band(answer, tab_high, tab_low)
+        wrapped = wrapped_ends(transform_band(value, tab_end_high, tab_end_low), end_sums, taps)
         at = pl.ds(pl.multiple_of(jnp.where(z == 0, 0, quarter - lanes), lanes), lanes)
         result[:, at] = result[:, at] - wrapped
         keep[...] = result[: total // 2].reshape(keep.shape)
@@ -406,8 +413,8 @@
         send[...] = partial[total // 2 :].reshape(send.shape)
 
 
-def unpack_kernel(most, *rest):
-    slots, out = rest[:-1], rest[-1]
+def unpack_kernel(most, order, *rest):
+    slots, out = dict(zip(order, rest[:-1])), rest[-1]
     d = lax.axis_index("shot")
     chip, core = d // 2, d % 2
     for q in range(len(slots) // 2):
@@ -535,7 +542,7 @@
     both = (block_owner[0] ^ block_owner[1]) == 1
     sent, every = lax.optimization_barrier((sent, every))
     *outs, chosen = lax.cond(both, lambda *sent: others(*sent, *scatter(1)), others, *sent)
-    turned = {q: swap(outs[q - 1], "shot", devices, 2 * q) for q in (3, 2, 1)}
+    turned = {q: swap(outs[q - 1], "shot", devices, 2 * q) for q in FAR_FIRST}
     own = kernel_call(
         own_kernel,
         f32(2 * shots, chunk, lanes),
@@ -547,17 +554,17 @@
         vmem=16 << 20,
     )(chosen, *every)
     own = kernel_call(
-        arrange_kernel,
+        functools.partial(arrange_kernel, FAR_FIRST + (0,)),
         f32(2 * shots, 4, chunk, lanes),
         [VMEM] * 4,
         VMEM,
         [],
         moved=1 << 19,
         vmem=8 << 20,
-    )(own, turned[1], turned[2], turned[3])
+    )(*[turned[q] for q in FAR_FIRST], own)
     across = swap(own, "freq", 4, 2)
-    right = lax.ppermute(own, "freq", [(0, 1), (1, 2), (2, 3)])
-    left = lax.ppermute(own, "freq", [(1, 0), (2, 1), (3, 2)])
+    near = swap(own, "freq", 4, 1)
+    middle = lax.ppermute(own, "freq", [(1, 2), (2, 1)])
     forward = lax.ppermute(across, "freq", [(2, 3), (1, 0)])
 
     tables = (high, low, end_high, end_low, sums, taps, same_side, cross_side)
@@ -580,7 +587,7 @@
         flops=6 * rows * 4 * lanes * quarter,
         moved=4 << 20,
         vmem=32 << 20,
-    )(*tables, own, right, left, across)
+    )(*tables, own, near, across, middle)
     keep, send = kernel_call(
         forward_kernel,
         [f32(shots, half, quarter)] * 2,
@@ -612,9 +619,10 @@
         moved=6 << 20,
         vmem=32 << 20,
     )(keep, got, traces, places)
-    slots = [slots[0]] + [swap(slots[k], "shot", devices, k) for k in range(1, devices)]
+    order = [2 * q + c for q in FAR_FIRST for c in range(2)] + [1, 0]
+    slots = [swap(slots[k], "shot", devices, k) if k else slots[k] for k in order]
     return kernel_call(
-        functools.partial(unpack_kernel, most),
+        functools.partial(unpack_kernel, most, order),
         f32(filters.shape[0], devices * most, quarter),
         [VMEM] * devices,
         VMEM,

time: 94.4 us -> 90 us (0.953)
  waiting for transfers between devices: 39.2 us -> 35.3 us
    ppermute x23 -> x24, starting transfers between devices: 24.6 us -> 29.2 us  [swap(): return lax.ppermute(value, axis, [(i, i ^ bit) for i in range(count)])]
    ppermute x2 -> x1, starting transfers between devices: 5.22 us -> 0.67 us  [plane_device(): middle = lax.ppermute(own, 'freq', [(1, 2), (2, 1)])]
    ppermute x23 -> x24, waiting for transfers between devices: 34.9 us -> 32.2 us  [swap(): return lax.ppermute(value, axis, [(i, i ^ bit) for i in range(count)])]
    ppermute x2 -> x1, waiting for transfers between devices: 1.18 us -> 0.01 us  [plane_device(): middle = lax.ppermute(own, 'freq', [(1, 2), (2, 1)])]
  transfers between devices with their start and end apart: 26 -> 26, of which waited for: 14 -> 16; matrix products, arithmetic and copies ran while one was open for 1% -> 1% of each run, Pallas kernels for 12% -> 13%
where the time goes in v4:
time: 90 us; the launch traced here: 89.7 us
  waiting for transfers between devices  35.3 us (39%)
  starting transfers between devices  31.1 us (35%)
  Pallas kernels  20.2 us (22%)
  between operations  1.59 us (2%)
    ppermute x24, waiting for transfers between devices, swap(): return lax.ppermute(value, axis, [(i, i ^ bit) for i in range(count)])  32.2 us
    ppermute x24, starting transfers between devices, swap(): return lax.ppermute(value, axis, [(i, i ^ bit) for i in range(count)])  29.2 us
    pallas_call x1, Pallas kernels, others(): kernel_call(functools.partial(others_kernel, len(sent) > 3), [f32(2 * sho...  3.75 us
    pallas_call x1, Pallas kernels, plane_device(): kernel_call(inverse_kernel, f32(rows, quarter), [ANY] * 5 + [VMEM] * 3 +...  3.36 us
    pallas_call x1, Pallas kernels, plane_device(): kernel_call(functools.partial(response_kernel, filters.shape[0]), [f32(ro...  3.27 us
    ppermute x1, waiting for transfers between devices, plane_device(): forward = lax.ppermute(across, 'freq', [(2, 3), (1, 0)])  3.01 us
    pallas_call x1, Pallas kernels, plane_device(): kernel_call(own_kernel, f32(2 * shots, chunk, lanes), [VMEM] * 3, VMEM, s...  1.88 us
  transfers between devices with their start and end apart: 26, of which 16 were waited for; matrix products, arithmetic and copies ran while one was open for 1% of the time, Pallas kernels for 13%

profile of v4, /device:TPU:0, one launch (start us, length us, event | category | flops | bytes accessed | tf_op | source)
XLA Modules:
  0.0 89.7 jit_solution(13134698328545637467)
XLA Ops:
  0.0 1.4 %sibling_kernel.1 = f32[16,128,128]{2,1,0:T(8,128)S(1)} custom-call(f32[16,256,128]{2,1,0:T(8,128)} %surface.3), custom_call_target="tpu_custom_call" | custom-call | bytes 2097152 | tf_op jit(solution)/shard_map/sibling_kernel/pallas_call | solution.py:460
  3.3 5.1 %collective-permute-start.5 = (f32[104,128]{1,0:T(8,128)S(1)}, f32[104,128]{1,0:T(8,128)S(1)}, u32[]{:S(2)}, u32[]{:S(2)}) collective-permute-start(f32[104,128]{1,0:T(8,128)S(1)} %get-tuple-element.89), channel_id=1, source_target_pairs={{0,3},{1,2},{2,1},{3,0},{4,7},{5,6},{6,5},{7,4},{8,11},{9,10},{10,... | collective-permute-start | bytes 159752 | tf_op jit(solution)/shard_map/ppermute | solution.py:81
  9.7 2.6 %collective-permute-start.4 = (f32[16,32,128]{2,1,0:T(8,128)S(1)}, f32[16,32,128]{2,1,0:T(8,128)S(1)}, u32[]{:S(2)}, u32[]{:S(2)}) collective-permute-start(f32[16,32,128]{2,1,0:T(8,128)S(1)} %get-tuple-element.87), channel_id=1, source_target_pairs={{0,24},{4,28},{8,16},{12,20},{16,8},{20,12},{24,0},{28,4},{1,25},{... | collective-permute-start | bytes 786440 | tf_op jit(solution)/shard_map/ppermute | solution.py:81
  13.5 1.6 %collective-permute-start.8 = (f32[104,128]{1,0:T(8,128)S(1)}, f32[104,128]{1,0:T(8,128)S(1)}, u32[]{:S(2)}, u32[]{:S(2)}) collective-permute-start(f32[104,128]{1,0:T(8,128)S(1)} %add_add_fusion), channel_id=1, source_target_pairs={{0,8},{4,12},{8,0},{12,4},{16,24},{20,28},{24,16},{28,20},{1,9},{5... | collective-permute-start | bytes 159752 | tf_op jit(solution)/shard_map/ppermute | solution.py:81
  15.0 1.5 %collective-permute-start.9 = (f32[104,128]{1,0:T(8,128)S(1)}, f32[104,128]{1,0:T(8,128)S(1)}, u32[]{:S(2)}, u32[]{:S(2)}) collective-permute-start(f32[104,128]{1,0:T(8,128)S(1)} %add_add_fusion), channel_id=1, source_target_pairs={{0,16},{4,20},{8,24},{12,28},{16,0},{20,4},{24,8},{28,12},{1,17},{... | collective-permute-start | bytes 159752 | tf_op jit(solution)/shard_map/ppermute | solution.py:81
  17.0 1.5 %collective-permute-start.12 = (f32[16,32,128]{2,1,0:T(8,128)S(1)}, f32[16,32,128]{2,1,0:T(8,128)S(1)}, u32[]{:S(2)}, u32[]{:S(2)}) collective-permute-start(f32[16,32,128]{2,1,0:T(8,128)S(1)} %get-tuple-element.96), channel_id=1, source_target_pairs={{0,8},{4,12},{8,0},{12,4},{16,24},{20,28},{24,16},{28,20},{1,9},{5... | collective-permute-start | bytes 786440 | tf_op jit(solution)/shard_map/ppermute | solution.py:81
  18.5 2.7 %collective-permute-done.8 = f32[104,128]{1,0:T(8,128)S(1)} collective-permute-done((f32[104,128]{1,0:T(8,128)S(1)}, f32[104,128]{1,0:T(8,128)S(1)}, u32[]{:S(2)}, u32[]{:S(2)}) %collective-permute-start.8) | collective-permute-done | bytes 53280 | tf_op jit(solution)/shard_map/ppermute | solution.py:81
  24.8 1.5 %collective-permute-done.12 = f32[16,32,128]{2,1,0:T(8,128)S(1)} collective-permute-done((f32[16,32,128]{2,1,0:T(8,128)S(1)}, f32[16,32,128]{2,1,0:T(8,128)S(1)}, u32[]{:S(2)}, u32[]{:S(2)}) %collective-permute-start.12) | collective-permute-done | bytes 262176 | tf_op jit(solution)/shard_map/ppermute | solution.py:81
  27.6 3.8 %conditional.1 = ((f32[6,32,128]{2,1,0:T(8,128)S(1)}, f32[6,32,128]{2,1,0:T(8,128)S(1)}, f32[6,32,128]{2,1,0:T(8,128)}, f32[2,16,32,128]{3,2,1,0:T(8,128)})) conditional(s32[]{:T(128)} %bitcast.4, (s32[2]{0:T(128)S(1)}, f32[16,256,128]{2,1,0:T(8,128)S(1)}, f32[16,128,128]{2,1,0:T(8,128)S(1)}, f32[16,32,128]{2,1,0:T(8,128)S(1)}, ...), branch_computations={%region_0.0_spmd, %region_1.0_spmd} | conditional | flops 9437184 | bytes 12583152 | solution.py:544
  27.6 3.8 %others_kernel.2 = (f32[6,32,128]{2,1,0:T(8,128)S(1)}, f32[6,32,128]{2,1,0:T(8,128)S(1)}, f32[6,32,128]{2,1,0:T(8,128)}, f32[2,16,32,128]{3,2,1,0:T(8,128)}) custom-call(s32[2]{0:T(128)S(1)} %get-tuple-element.37.owners, f32[16,256,128]{2,1,0:T(8,128)S(1)} %get-tuple-element.38.surface, f32[16,128,128]{2,1,0:T(8,128)S(1)} %get-tuple-element.39.sibling, ...), custom_call_target="tpu_custom_call" | custom-call | flops 9437184 | bytes 1048576 | tf_op jit(solution)/shard_map/cond/branch_0_fun/others_kernel/pallas_call | solution.py:497
  31.4 1.4 %collective-permute-start.14 = (f32[6,32,128]{2,1,0:T(8,128)}, f32[6,32,128]{2,1,0:T(8,128)S(1)}, u32[]{:S(2)}, u32[]{:S(2)}) collective-permute-start(f32[6,32,128]{2,1,0:T(8,128)} %get-tuple-element.104), channel_id=1, source_target_pairs={{0,24},{4,28},{8,16},{12,20},{16,8},{20,12},{24,0},{28,4},{1,25},{... | collective-permute-start | bytes 294920 | tf_op jit(solution)/shard_map/ppermute | solution.py:81
  33.1 1.9 %collective-permute-start.16 = (f32[6,32,128]{2,1,0:T(8,128)S(1)}, f32[6,32,128]{2,1,0:T(8,128)S(1)}, u32[]{:S(2)}, u32[]{:S(2)}) collective-permute-start(f32[6,32,128]{2,1,0:T(8,128)S(1)} %get-tuple-element.106), channel_id=1, source_target_pairs={{0,16},{4,20},{8,24},{12,28},{16,0},{20,4},{24,8},{28,12},{1,17},{... | collective-permute-start | bytes 294920 | tf_op jit(solution)/shard_map/ppermute | solution.py:81
  35.0 1.9 %own_kernel.1.rest_3_ = f32[6,32,128]{2,1,0:T(8,128)S(1)} custom-call(f32[2,16,32,128]{3,2,1,0:T(8,128)} %get-tuple-element.107.chosen, f32[4,104,128]{2,1,0:T(8,128)} %pad_maximum_fusion.rest_0_.own, f32[4,104,128]{2,1,0:T(8,128)} %collective-permute-done.11.rest_1_.other), custom_call_target="tpu_custom_call" | custom-call | flops 3145728 | bytes 1048576 | tf_op jit(solution)/shard_map/own_kernel/pallas_call | solution.py:546
  38.3 2.2 %collective-permute-start.18 = (f32[6,4,32,128]{3,2,1,0:T(8,128)S(1)}, f32[6,4,32,128]{3,2,1,0:T(8,128)S(1)}, u32[]{:S(2)}, u32[]{:S(2)}) collective-permute-start(f32[6,4,32,128]{3,2,1,0:T(8,128)S(1)} %arrange_kernel.1.rest_0_), channel_id=1, source_target_pairs={{0,2},{1,3},{2,0},{3,1},{4,6},{5,7},{6,4},{7,5},{8,10},{9,11},{10,... | collective-permute-start | bytes 1179656 | tf_op jit(solution)/shard_map/ppermute | solution.py:81
  40.6 2.0 %collective-permute-start.17 = (f32[6,4,32,128]{3,2,1,0:T(8,128)S(1)}, f32[6,4,32,128]{3,2,1,0:T(8,128)S(1)}, u32[]{:S(2)}, u32[]{:S(2)}) collective-permute-start(f32[6,4,32,128]{3,2,1,0:T(8,128)S(1)} %arrange_kernel.1.rest_0_), channel_id=1, source_target_pairs={{0,1},{1,0},{2,3},{3,2},{4,5},{5,4},{6,7},{7,6},{8,9},{9,8},{10,11... | collective-permute-start | bytes 1179656 | tf_op jit(solution)/shard_map/ppermute | solution.py:81
  43.3 13.6 %collective-permute-done.18.rest_2_ = f32[6,4,32,128]{3,2,1,0:T(8,128)S(1)} collective-permute-done((f32[6,4,32,128]{3,2,1,0:T(8,128)S(1)}, f32[6,4,32,128]{3,2,1,0:T(8,128)S(1)}, u32[]{:S(2)}, u32[]{:S(2)}) %collective-permute-start.18) | collective-permute-done | bytes 393248 | tf_op jit(solution)/shard_map/ppermute | solution.py:81
  58.2 3.3 %response_kernel.1 = (f32[768,256]{1,0:T(8,128)S(1)}, f32[768,512]{1,0:T(8,128)S(1)}, f32[768,512]{1,0:T(8,128)S(1)}) custom-call(s32[3,256]{1,0:T(4,128)S(1)} %bitcast.13, f32[128,512]{1,0:T(8,128)S(1)} %copy-done.7, f32[2,128,256]{2,1,0:T(8,128)S(1)} %copy-done.8, f32[4,104,128]{2,1,0:T(8,128)} %pad_maximum_fusion.rest_0_.own, ...), custom_call_target="tpu_custom_call" | custom-call | flops 226492416 | bytes 4194304 | tf_op jit(solution)/shard_map/response_kernel/pallas_call | solution.py:531
  61.5 3.4 %inverse_kernel.1.partial = f32[768,256]{1,0:T(8,128)S(1)} custom-call(bf16[1056,512]{1,0:T(8,128)(2,1)S(1)} %copy-done, bf16[1056,512]{1,0:T(8,128)(2,1)S(1)} %copy-done.1, bf16[512,512]{1,0:T(8,128)(2,1)S(1)} %copy-done.2, bf16[512,512]{1,0:T(8,128)(2,1)S(1)} %copy-done.3, bf16[512,128]{1,0:T(8,128)(2,1)S(1)} %copy-done.6, ...), custom_call_target="tpu_custom_call" | custom-call | flops 603979776 | bytes 4194304 | tf_op jit(solution)/shard_map/inverse_kernel/pallas_call | solution.py:572
  64.9 3.0 %collective-permute-done.20.forward = f32[6,4,32,128]{3,2,1,0:T(8,128)S(1)} collective-permute-done((f32[6,4,32,128]{3,2,1,0:T(8,128)S(1)}, f32[6,4,32,128]{3,2,1,0:T(8,128)S(1)}, u32[]{:S(2)}, u32[]{:S(2)}) %collective-permute-start.20) | collective-permute-done | bytes 393248 | tf_op jit(solution)/shard_map/ppermute | solution.py:568
  72.3 2.6 %collective-permute-start.22 = (f32[144,256]{1,0:T(8,128)S(1)}, f32[144,256]{1,0:T(8,128)S(1)}, u32[]{:S(2)}, u32[]{:S(2)}) collective-permute-start(f32[144,256]{1,0:T(8,128)S(1)} %get-tuple-element.110), channel_id=1, source_target_pairs={{0,24},{4,28},{8,16},{12,20},{16,8},{20,12},{24,0},{28,4},{1,25},{... | collective-permute-start | bytes 442376 | tf_op jit(solution)/shard_map/ppermute | solution.py:81
  76.8 2.1 %collective-permute-start.26 = (f32[144,256]{1,0:T(8,128)S(1)}, f32[144,256]{1,0:T(8,128)S(1)}, u32[]{:S(2)}, u32[]{:S(2)}) collective-permute-start(f32[144,256]{1,0:T(8,128)S(1)} %get-tuple-element.114), channel_id=1, source_target_pairs={{0,16},{4,20},{8,24},{12,28},{16,0},{20,4},{24,8},{28,12},{1,17},{... | collective-permute-start | bytes 442376 | tf_op jit(solution)/shard_map/ppermute | solution.py:81
  80.2 2.2 %collective-permute-done.23.rest_1_ = f32[144,256]{1,0:T(8,128)S(1)} collective-permute-done((f32[144,256]{1,0:T(8,128)S(1)}, f32[144,256]{1,0:T(8,128)S(1)}, u32[]{:S(2)}, u32[]{:S(2)}) %collective-permute-start.23) | collective-permute-done | bytes 147488 | tf_op jit(solution)/shard_map/ppermute | solution.py:81
  82.5 4.5 %collective-permute-done.24.rest_2_ = f32[144,256]{1,0:T(8,128)S(1)} collective-permute-done((f32[144,256]{1,0:T(8,128)S(1)}, f32[144,256]{1,0:T(8,128)S(1)}, u32[]{:S(2)}, u32[]{:S(2)}) %collective-permute-start.24) | collective-permute-done | bytes 147488 | tf_op jit(solution)/shard_map/ppermute | solution.py:81
  86.9 1.6 %collective-permute-done.25.rest_3_ = f32[144,256]{1,0:T(8,128)S(1)} collective-permute-done((f32[144,256]{1,0:T(8,128)S(1)}, f32[144,256]{1,0:T(8,128)S(1)}, u32[]{:S(2)}, u32[]{:S(2)}) %collective-permute-start.25) | collective-permute-done | bytes 147488 | tf_op jit(solution)/shard_map/ppermute | solution.py:81
  (76 shorter events, 20.9 us)
Async XLA Ops:
  1.5 7.6 %collective-permute-start.3 = (f32[16,128,128]{2,1,0:T(8,128)S(1)}, f32[16,128,128]{2,1,0:T(8,128)S(1)}, u32[]{:S(2)}, u32[]{:S(2)}) collective-permute-start(f32[16,128,128]{2,1,0:T(8,128)S(1)} %sibling_kernel.1), channel_id=1, source_target_pairs={{0,4},{4,0},{8,12},{12,8},{16,20},{20,16},{24,28},{28,24},{1,5},{5... | collective-permute-start | bytes 3145736 | tf_op jit(solution)/shard_map/ppermute | solution.py:81
  3.3 9.1 %collective-permute-start.5 = (f32[104,128]{1,0:T(8,128)S(1)}, f32[104,128]{1,0:T(8,128)S(1)}, u32[]{:S(2)}, u32[]{:S(2)}) collective-permute-start(f32[104,128]{1,0:T(8,128)S(1)} %get-tuple-element.89), channel_id=1, source_target_pairs={{0,3},{1,2},{2,1},{3,0},{4,7},{5,6},{6,5},{7,4},{8,11},{9,10},{10,... | collective-permute-start | bytes 159752 | tf_op jit(solution)/shard_map/ppermute | solution.py:81
  8.4 5.0 %collective-permute-start.6 = (f32[104,128]{1,0:T(8,128)S(1)}, f32[104,128]{1,0:T(8,128)S(1)}, u32[]{:S(2)}, u32[]{:S(2)}) collective-permute-start(f32[104,128]{1,0:T(8,128)S(1)} %get-tuple-element.90), channel_id=1, source_target_pairs={{0,2},{1,3},{2,0},{3,1},{4,6},{5,7},{6,4},{7,5},{8,10},{9,11},{10,... | collective-permute-start | bytes 159752 | tf_op jit(solution)/shard_map/ppermute | solution.py:81
  8.4 5.0 %collective-permute-start.7 = (f32[104,128]{1,0:T(8,128)S(1)}, f32[104,128]{1,0:T(8,128)S(1)}, u32[]{:S(2)}, u32[]{:S(2)}) collective-permute-start(f32[104,128]{1,0:T(8,128)S(1)} %get-tuple-element.91), channel_id=1, source_target_pairs={{0,1},{1,0},{2,3},{3,2},{4,5},{5,4},{6,7},{7,6},{8,9},{9,8},{10,11... | collective-permute-start | bytes 159752 | tf_op jit(solution)/shard_map/ppermute | solution.py:81
  9.7 13.2 %collective-permute-start.4 = (f32[16,32,128]{2,1,0:T(8,128)S(1)}, f32[16,32,128]{2,1,0:T(8,128)S(1)}, u32[]{:S(2)}, u32[]{:S(2)}) collective-permute-start(f32[16,32,128]{2,1,0:T(8,128)S(1)} %get-tuple-element.87), channel_id=1, source_target_pairs={{0,24},{4,28},{8,16},{12,20},{16,8},{20,12},{24,0},{28,4},{1,25},{... | collective-permute-start | bytes 786440 | tf_op jit(solution)/shard_map/ppermute | solution.py:81
  13.5 7.8 %collective-permute-start.8 = (f32[104,128]{1,0:T(8,128)S(1)}, f32[104,128]{1,0:T(8,128)S(1)}, u32[]{:S(2)}, u32[]{:S(2)}) collective-permute-start(f32[104,128]{1,0:T(8,128)S(1)} %add_add_fusion), channel_id=1, source_target_pairs={{0,8},{4,12},{8,0},{12,4},{16,24},{20,28},{24,16},{28,20},{1,9},{5... | collective-permute-start | bytes 159752 | tf_op jit(solution)/shard_map/ppermute | solution.py:81
  15.0 6.2 %collective-permute-start.9 = (f32[104,128]{1,0:T(8,128)S(1)}, f32[104,128]{1,0:T(8,128)S(1)}, u32[]{:S(2)}, u32[]{:S(2)}) collective-permute-start(f32[104,128]{1,0:T(8,128)S(1)} %add_add_fusion), channel_id=1, source_target_pairs={{0,16},{4,20},{8,24},{12,28},{16,0},{20,4},{24,8},{28,12},{1,17},{... | collective-permute-start | bytes 159752 | tf_op jit(solution)/shard_map/ppermute | solution.py:81
  16.5 5.7 %collective-permute-start.10 = (f32[104,128]{1,0:T(8,128)S(1)}, f32[104,128]{1,0:T(8,128)S(1)}, u32[]{:S(2)}, u32[]{:S(2)}) collective-permute-start(f32[104,128]{1,0:T(8,128)S(1)} %add_add_fusion), channel_id=1, source_target_pairs={{0,24},{4,28},{8,16},{12,20},{16,8},{20,12},{24,0},{28,4},{1,25},{... | collective-permute-start | bytes 159752 | tf_op jit(solution)/shard_map/ppermute | solution.py:81
  17.0 9.2 %collective-permute-start.12 = (f32[16,32,128]{2,1,0:T(8,128)S(1)}, f32[16,32,128]{2,1,0:T(8,128)S(1)}, u32[]{:S(2)}, u32[]{:S(2)}) collective-permute-start(f32[16,32,128]{2,1,0:T(8,128)S(1)} %get-tuple-element.96), channel_id=1, source_target_pairs={{0,8},{4,12},{8,0},{12,4},{16,24},{20,28},{24,16},{28,20},{1,9},{5... | collective-permute-start | bytes 786440 | tf_op jit(solution)/shard_map/ppermute | solution.py:81
  21.2 6.4 %collective-permute-start.13 = (f32[16,32,128]{2,1,0:T(8,128)S(1)}, f32[16,32,128]{2,1,0:T(8,128)S(1)}, u32[]{:S(2)}, u32[]{:S(2)}) collective-permute-start(f32[16,32,128]{2,1,0:T(8,128)S(1)} %get-tuple-element.97), channel_id=1, source_target_pairs={{0,16},{4,20},{8,24},{12,28},{16,0},{20,4},{24,8},{28,12},{1,17},{... | collective-permute-start | bytes 786440 | tf_op jit(solution)/shard_map/ppermute | solution.py:81
  22.9 4.7 %collective-permute-start.11 = (f32[4,104,128]{2,1,0:T(8,128)}, f32[4,104,128]{2,1,0:T(8,128)}, u32[]{:S(2)}, u32[]{:S(2)}) collective-permute-start(f32[4,104,128]{2,1,0:T(8,128)} %pad_maximum_fusion.rest_0_.own), channel_id=1, source_target_pairs={{0,4},{4,0},{8,12},{12,8},{16,20},{20,16},{24,28},{28,24},{1,5},{5... | collective-permute-start | bytes 638984 | tf_op jit(solution)/shard_map/ppermute | solution.py:81
  31.4 5.9 %collective-permute-start.14 = (f32[6,32,128]{2,1,0:T(8,128)}, f32[6,32,128]{2,1,0:T(8,128)S(1)}, u32[]{:S(2)}, u32[]{:S(2)}) collective-permute-start(f32[6,32,128]{2,1,0:T(8,128)} %get-tuple-element.104), channel_id=1, source_target_pairs={{0,24},{4,28},{8,16},{12,20},{16,8},{20,12},{24,0},{28,4},{1,25},{... | collective-permute-start | bytes 294920 | tf_op jit(solution)/shard_map/ppermute | solution.py:81
  33.1 5.2 %collective-permute-start.16 = (f32[6,32,128]{2,1,0:T(8,128)S(1)}, f32[6,32,128]{2,1,0:T(8,128)S(1)}, u32[]{:S(2)}, u32[]{:S(2)}) collective-permute-start(f32[6,32,128]{2,1,0:T(8,128)S(1)} %get-tuple-element.106), channel_id=1, source_target_pairs={{0,16},{4,20},{8,24},{12,28},{16,0},{20,4},{24,8},{28,12},{1,17},{... | collective-permute-start | bytes 294920 | tf_op jit(solution)/shard_map/ppermute | solution.py:81
  38.3 18.6 %collective-permute-start.18 = (f32[6,4,32,128]{3,2,1,0:T(8,128)S(1)}, f32[6,4,32,128]{3,2,1,0:T(8,128)S(1)}, u32[]{:S(2)}, u32[]{:S(2)}) collective-permute-start(f32[6,4,32,128]{3,2,1,0:T(8,128)S(1)} %arrange_kernel.1.rest_0_), channel_id=1, source_target_pairs={{0,2},{1,3},{2,0},{3,1},{4,6},{5,7},{6,4},{7,5},{8,10},{9,11},{10,... | collective-permute-start | bytes 1179656 | tf_op jit(solution)/shard_map/ppermute | solution.py:81
  40.6 20.9 %collective-permute-start.17 = (f32[6,4,32,128]{3,2,1,0:T(8,128)S(1)}, f32[6,4,32,128]{3,2,1,0:T(8,128)S(1)}, u32[]{:S(2)}, u32[]{:S(2)}) collective-permute-start(f32[6,4,32,128]{3,2,1,0:T(8,128)S(1)} %arrange_kernel.1.rest_0_), channel_id=1, source_target_pairs={{0,1},{1,0},{2,3},{3,2},{4,5},{5,4},{6,7},{7,6},{8,9},{9,8},{10,11... | collective-permute-start | bytes 1179656 | tf_op jit(solution)/shard_map/ppermute | solution.py:81
  42.6 18.9 %collective-permute-start.19 = (f32[6,4,32,128]{3,2,1,0:T(8,128)S(1)}, f32[6,4,32,128]{3,2,1,0:T(8,128)S(1)}, u32[]{:S(2)}, u32[]{:S(2)}) collective-permute-start(f32[6,4,32,128]{3,2,1,0:T(8,128)S(1)} %arrange_kernel.1.rest_0_), channel_id=1, source_target_pairs={{1,2},{2,1},{5,6},{6,5},{9,10},{10,9},{13,14},{14,13},{17,18},{18,... | collective-permute-start | bytes 1179656 | tf_op jit(solution)/shard_map/ppermute | solution.py:567
  56.9 11.0 %collective-permute-start.20 = (f32[6,4,32,128]{3,2,1,0:T(8,128)S(1)}, f32[6,4,32,128]{3,2,1,0:T(8,128)S(1)}, u32[]{:S(2)}, u32[]{:S(2)}) collective-permute-start(f32[6,4,32,128]{3,2,1,0:T(8,128)S(1)} %collective-permute-done.18.rest_2_), channel_id=1, source_target_pairs={{2,3},{1,0},{6,7},{5,4},{10,11},{9,8},{14,15},{13,12},{18,19},{17,... | collective-permute-start | bytes 1179656 | tf_op jit(solution)/shard_map/ppermute | solution.py:568
  72.3 7.1 %collective-permute-start.22 = (f32[144,256]{1,0:T(8,128)S(1)}, f32[144,256]{1,0:T(8,128)S(1)}, u32[]{:S(2)}, u32[]{:S(2)}) collective-permute-start(f32[144,256]{1,0:T(8,128)S(1)} %get-tuple-element.110), channel_id=1, source_target_pairs={{0,24},{4,28},{8,16},{12,20},{16,8},{20,12},{24,0},{28,4},{1,25},{... | collective-permute-start | bytes 442376 | tf_op jit(solution)/shard_map/ppermute | solution.py:81
  75.0 7.4 %collective-permute-start.23 = (f32[144,256]{1,0:T(8,128)S(1)}, f32[144,256]{1,0:T(8,128)S(1)}, u32[]{:S(2)}, u32[]{:S(2)}) collective-permute-start(f32[144,256]{1,0:T(8,128)S(1)} %get-tuple-element.111), channel_id=1, source_target_pairs={{0,28},{4,24},{8,20},{12,16},{16,12},{20,8},{24,4},{28,0},{1,29},{... | collective-permute-start | bytes 442376 | tf_op jit(solution)/shard_map/ppermute | solution.py:81
  75.0 12.0 %collective-permute-start.24 = (f32[144,256]{1,0:T(8,128)S(1)}, f32[144,256]{1,0:T(8,128)S(1)}, u32[]{:S(2)}, u32[]{:S(2)}) collective-permute-start(f32[144,256]{1,0:T(8,128)S(1)} %get-tuple-element.112), channel_id=1, source_target_pairs={{0,8},{4,12},{8,0},{12,4},{16,24},{20,28},{24,16},{28,20},{1,9},{5... | collective-permute-start | bytes 442376 | tf_op jit(solution)/shard_map/ppermute | solution.py:81
  76.0 12.5 %collective-permute-start.25 = (f32[144,256]{1,0:T(8,128)S(1)}, f32[144,256]{1,0:T(8,128)S(1)}, u32[]{:S(2)}, u32[]{:S(2)}) collective-permute-start(f32[144,256]{1,0:T(8,128)S(1)} %get-tuple-element.113), channel_id=1, source_target_pairs={{0,12},{4,8},{8,4},{12,0},{16,28},{20,24},{24,20},{28,16},{1,13},{... | collective-permute-start | bytes 442376 | tf_op jit(solution)/shard_map/ppermute | solution.py:81
  76.8 11.7 %collective-permute-start.26 = (f32[144,256]{1,0:T(8,128)S(1)}, f32[144,256]{1,0:T(8,128)S(1)}, u32[]{:S(2)}, u32[]{:S(2)}) collective-permute-start(f32[144,256]{1,0:T(8,128)S(1)} %get-tuple-element.114), channel_id=1, source_target_pairs={{0,16},{4,20},{8,24},{12,28},{16,0},{20,4},{24,8},{28,12},{1,17},{... | collective-permute-start | bytes 442376 | tf_op jit(solution)/shard_map/ppermute | solution.py:81
  79.5 9.2 %collective-permute-start.27 = (f32[144,256]{1,0:T(8,128)S(1)}, f32[144,256]{1,0:T(8,128)S(1)}, u32[]{:S(2)}, u32[]{:S(2)}) collective-permute-start(f32[144,256]{1,0:T(8,128)S(1)} %get-tuple-element.115), channel_id=1, source_target_pairs={{0,20},{4,16},{8,28},{12,24},{16,4},{20,0},{24,12},{28,8},{1,21},{... | collective-permute-start | bytes 442376 | tf_op jit(solution)/shard_map/ppermute | solution.py:81
  82.4 6.3 %collective-permute-start.28 = (f32[144,256]{1,0:T(8,128)S(1)}, f32[144,256]{1,0:T(8,128)S(1)}, u32[]{:S(2)}, u32[]{:S(2)}) collective-permute-start(f32[144,256]{1,0:T(8,128)S(1)} %get-tuple-element.116), channel_id=1, source_target_pairs={{0,4},{4,0},{8,12},{12,8},{16,20},{20,16},{24,28},{28,24},{1,5},{5... | collective-permute-start | bytes 442376 | tf_op jit(solution)/shard_map/ppermute | solution.py:81
  (17 other events, 181.7 us)
